TPU v7x, 32 devices: a whole 2x2x4 slice. The times are simulated.
32 devices in a mesh: dp: 8 (over z, x), fsdp: 4 (over y, core).
Axes of the slice: x: 2, y: 2, z: 4, core: 2. Of those that a mesh axis runs over, the one named last changes fastest.
Arguments:
- layer_input: bfloat16 [32, 4096, 512], P(('dp', 'fsdp')), may hold values from -6 to 6
- doc_lengths: int32 [32, 8], P(('dp', 'fsdp')), may hold values from 1 to 2048, 4096 in all within a row
- out_cotangent: bfloat16 [32, 4096, 512], P(('dp', 'fsdp')), may hold values from -6 to 6
- proj_master: float32 [512, 2048], P(('dp', 'fsdp')), as said below
- proj_moment1: float32 [512, 2048], P(('dp', 'fsdp')), may hold values from -48 to 48
- proj_moment2: float32 [512, 2048], P(('dp', 'fsdp')), may hold values from 157.2864 to 1572.864
- up_master: float32 [512, 2048], P(('dp', 'fsdp')), may hold values from -0.25 to 0.25
- up_moment1: float32 [512, 2048], P(('dp', 'fsdp')), may hold values from -64 to 64
- up_moment2: float32 [512, 2048], P(('dp', 'fsdp')), may hold values from 353.8944 to 3538.944
- down_master: float32 [2048, 512], P(('dp', 'fsdp')), may hold values from -0.125 to 0.125
- down_moment1: float32 [2048, 512], P(('dp', 'fsdp')), may hold values from -128 to 128
- down_moment2: float32 [2048, 512], P(('dp', 'fsdp')), may hold values from 1441.792 to 14417.92
- sort_master: float32 [512, 128], P(('dp', 'fsdp')), may hold values from -2 to 2
- sort_moment1: float32 [512, 128], P(('dp', 'fsdp')), may hold values from -24 to 24
- sort_moment2: float32 [512, 128], P(('dp', 'fsdp')), may hold values from 39.3216 to 393.216
- norm_master: float32 [4, 512], P(None, ('dp', 'fsdp')), as said below
- norm_moment1: float32 [4, 512], P(None, ('dp', 'fsdp')), may hold values from -256 to 256
- norm_moment2: float32 [4, 512], P(None, ('dp', 'fsdp')), may hold values from 3932.16 to 39321.6
Outputs:
- layer_output: bfloat16 [32, 4096, 512], P(('dp', 'fsdp'))
- input_grad: float32 [32, 4096, 512], P(('dp', 'fsdp'))
- proj_new: float32 [512, 2048], P(('dp', 'fsdp'))
- proj_first: float32 [512, 2048], P(('dp', 'fsdp'))
- proj_second: float32 [512, 2048], P(('dp', 'fsdp'))
- up_new: float32 [512, 2048], P(('dp', 'fsdp'))
- up_first: float32 [512, 2048], P(('dp', 'fsdp'))
- up_second: float32 [512, 2048], P(('dp', 'fsdp'))
- down_new: float32 [2048, 512], P(('dp', 'fsdp'))
- down_first: float32 [2048, 512], P(('dp', 'fsdp'))
- down_second: float32 [2048, 512], P(('dp', 'fsdp'))
- sort_new: float32 [512, 128], P(('dp', 'fsdp'))
- sort_first: float32 [512, 128], P(('dp', 'fsdp'))
- sort_second: float32 [512, 128], P(('dp', 'fsdp'))
- norm_new: float32 [4, 512], P(None, ('dp', 'fsdp'))
- norm_first: float32 [4, 512], P(None, ('dp', 'fsdp'))
- norm_second: float32 [4, 512], P(None, ('dp', 'fsdp'))
Inputs may be any that keep to these rules, and one draw needn't show every extreme that they name: `doc_lengths`: each row's 8 documents fill its 4096 tokens; in every row the longest has exactly 4096 // 2 tokens. `proj_master`: the last 512 columns, the output projection, are about four times as large as the others. `norm_master`: rows 0 and 2 are gains near one, rows 1 and 3 biases.
All inputs are finite; a program needn't handle non-finite values.
Results may differ from a plain program's by a relative error of at most 0.012.
Values may be sent and summed in bfloat16 or wider, within the bound.
A program may use at most 384 MiB of HBM per device.

v0:
```python
import jax
import jax.numpy as jnp
from jax import lax
from jax.sharding import PartitionSpec as P

H = 8
HD = 64
BLOCK = 32
SINK_ITERS = 8
STEP = 10


mask_penalty = 6.0
score_floor = -1000000000.0
norm_eps = 1e-05
beta_first = 0.9
beta_second = 0.95
adam_eps = 1e-08
weight_decay = 0.1
rate_matrix = 0.1
rate_other = 0.5


def matmul(left, right):
    return jnp.einsum("...k,kn->...n", left, right, preferred_element_type=jnp.float32)


def matmul_back(grad, right):
    return jnp.einsum("...n,kn->...k", grad, right, preferred_element_type=jnp.float32)


def outer_total(left, grad):
    left_flat = left.reshape(-1, left.shape[-1])
    grad_flat = grad.reshape(-1, grad.shape[-1])
    return jnp.einsum("tk,tn->kn", left_flat, grad_flat, preferred_element_type=jnp.float32)


def segment_ids(lengths, seq_len):
    ends = jnp.cumsum(lengths, axis=-1)
    places = jnp.arange(seq_len, dtype=jnp.int32)
    return jnp.sum((places[None, :, None] >= ends[:, None, :]).astype(jnp.int32), axis=-1)


def layer_norm(values, gain, shift):
    centre = values - jnp.mean(values, axis=-1, keepdims=True)
    spread = jnp.mean(centre * centre, axis=-1, keepdims=True)
    return centre * lax.rsqrt(spread + norm_eps) * gain + shift


def doubly_stochastic_normalize(unnormalized_logits, split_blocks):
    score_logits = unnormalized_logits - mask_penalty * split_blocks
    for sweep in range(SINK_ITERS):
        score_logits = score_logits - jax.nn.logsumexp(score_logits, axis=2, keepdims=True)
        score_logits = score_logits - jax.nn.logsumexp(score_logits, axis=1, keepdims=True)
    return jnp.exp(score_logits)


def softmax_rows(scores):
    highest = jnp.max(scores, axis=-1, keepdims=True)
    exps = jnp.exp(scores - highest)
    return exps / jnp.sum(exps, axis=-1, keepdims=True)


def gelu_tanh(values):
    return jax.nn.gelu(values, approximate=True)


def forward(inputs, segments, weights):
    proj, up_weight, down_weight, sort_weight, norms = weights
    rows, length, width = inputs.shape
    blocks = length // BLOCK
    normed = layer_norm(inputs, norms[0], norms[1]).astype(jnp.bfloat16)
    projected = matmul(normed, proj[:, : 3 * width]).astype(jnp.bfloat16)
    heads = projected.reshape(rows, blocks, BLOCK, 3, H, HD)
    queries = heads[:, :, :, 0]
    keys_all = heads[:, :, :, 1]
    values_all = heads[:, :, :, 2]
    block_means = jnp.mean(
        normed.astype(jnp.float32).reshape(rows, blocks, BLOCK, width), axis=2
    ).astype(jnp.bfloat16)
    unnormalized_logits = matmul(block_means, sort_weight)
    firsts = segments[:, ::BLOCK]
    split_blocks = (firsts[:, :, None] != firsts[:, None, :]).astype(jnp.float32)
    block_permutation = doubly_stochastic_normalize(unnormalized_logits, split_blocks).astype(
        jnp.bfloat16
    )
    sorted_keys = jnp.einsum(
        "rij,rjthe->rithe", block_permutation, keys_all, preferred_element_type=jnp.float32
    ).astype(jnp.bfloat16)
    sorted_values = jnp.einsum(
        "rij,rjthe->rithe", block_permutation, values_all, preferred_element_type=jnp.float32
    ).astype(jnp.bfloat16)
    scale = HD ** (-0.5)
    local_scores = (
        jnp.einsum("rnthe,rnshe->rnhts", queries, keys_all, preferred_element_type=jnp.float32)
        * scale
    )
    block_segs = segments.reshape(rows, blocks, BLOCK)
    same_doc = (block_segs[:, :, :, None] == block_segs[:, :, None, :])[:, :, None]
    local_scores = jnp.where(same_doc, local_scores, score_floor)
    far_scores = (
        jnp.einsum("rnthe,rnshe->rnhts", queries, sorted_keys, preferred_element_type=jnp.float32)
        * scale
    )
    scores = jnp.concatenate([local_scores, far_scores], axis=-1)
    probs = softmax_rows(scores).astype(jnp.bfloat16)
    context = jnp.einsum(
        "rnhts,rnshe->rnthe", probs[..., :BLOCK], values_all, preferred_element_type=jnp.float32
    )
    context = context + jnp.einsum(
        "rnhts,rnshe->rnthe", probs[..., BLOCK:], sorted_values, preferred_element_type=jnp.float32
    )
    context = context.reshape(rows, length, width).astype(jnp.bfloat16)
    hidden = inputs + matmul(context, proj[:, 3 * width :])
    normed_two = layer_norm(hidden, norms[2], norms[3]).astype(jnp.bfloat16)
    pre_act = matmul(normed_two, up_weight)
    activated = gelu_tanh(pre_act).astype(jnp.bfloat16)
    output = hidden + matmul(activated, down_weight)
    saved = (
        normed,
        projected,
        block_means,
        unnormalized_logits,
        split_blocks,
        block_permutation,
        sorted_keys,
        sorted_values,
        same_doc,
        scores,
        probs,
        context,
        hidden,
        normed_two,
        pre_act,
        activated,
    )
    return (output, saved)


def ffn_backward(cotangent, saved, weights):
    proj, up_weight, down_weight, sort_weight, norms = weights
    hidden, normed_two, pre_act, activated = (saved[12], saved[13], saved[14], saved[15])
    grad_out_low = cotangent.astype(jnp.bfloat16)
    grad_down = outer_total(activated, grad_out_low)
    activation_gradient = matmul_back(grad_out_low, down_weight)
    gelu_pull = jax.vjp(gelu_tanh, pre_act)[1]
    grad_pre_low = gelu_pull(activation_gradient)[0].astype(jnp.bfloat16)
    grad_up = outer_total(normed_two, grad_pre_low)
    grad_normed_two = matmul_back(grad_pre_low, up_weight)
    norm_pull = jax.vjp(layer_norm, hidden, norms[2], norms[3])[1]
    grad_hidden_norm, grad_gain_two, grad_shift_two = norm_pull(grad_normed_two)
    hidden_grad = cotangent + grad_hidden_norm
    return (hidden_grad, grad_up, grad_down, grad_gain_two, grad_shift_two)


def attn_backward(inputs, hidden_grad, saved, weights):
    proj, up_weight, down_weight, sort_weight, norms = weights
    (
        normed,
        projected,
        block_means,
        unnormalized_logits,
        split_blocks,
        block_permutation,
        sorted_keys,
        sorted_values,
        same_doc,
        scores,
        probs,
        context,
    ) = saved[:12]
    rows, length, width = inputs.shape
    blocks = length // BLOCK
    heads = projected.reshape(rows, blocks, BLOCK, 3, H, HD)
    queries = heads[:, :, :, 0]
    keys_all = heads[:, :, :, 1]
    values_all = heads[:, :, :, 2]
    grad_attn_low = hidden_grad.astype(jnp.bfloat16)
    grad_out_proj = outer_total(context, grad_attn_low)
    grad_context_low = (
        matmul_back(grad_attn_low, proj[:, 3 * width :])
        .astype(jnp.bfloat16)
        .reshape(rows, blocks, BLOCK, H, HD)
    )
    grad_probs_local = jnp.einsum(
        "rnthe,rnshe->rnhts", grad_context_low, values_all, preferred_element_type=jnp.float32
    )
    grad_probs_far = jnp.einsum(
        "rnthe,rnshe->rnhts", grad_context_low, sorted_values, preferred_element_type=jnp.float32
    )
    grad_values_local = jnp.einsum(
        "rnhts,rnthe->rnshe",
        probs[..., :BLOCK],
        grad_context_low,
        preferred_element_type=jnp.float32,
    )
    grad_sorted_values = jnp.einsum(
        "rnhts,rnthe->rnshe",
        probs[..., BLOCK:],
        grad_context_low,
        preferred_element_type=jnp.float32,
    )
    grad_probs = jnp.concatenate([grad_probs_local, grad_probs_far], axis=-1)
    soft_pull = jax.vjp(softmax_rows, scores)[1]
    grad_scores_low = soft_pull(grad_probs)[0].astype(jnp.bfloat16)
    scale = HD ** (-0.5)
    zero_low = jnp.zeros((), jnp.bfloat16)
    grad_local = jnp.where(same_doc, grad_scores_low[..., :BLOCK], zero_low) * jnp.bfloat16(scale)
    grad_far = grad_scores_low[..., BLOCK:] * jnp.bfloat16(scale)
    grad_queries = jnp.einsum(
        "rnhts,rnshe->rnthe", grad_local, keys_all, preferred_element_type=jnp.float32
    )
    grad_queries = grad_queries + jnp.einsum(
        "rnhts,rnshe->rnthe", grad_far, sorted_keys, preferred_element_type=jnp.float32
    )
    grad_keys_local = jnp.einsum(
        "rnhts,rnthe->rnshe", grad_local, queries, preferred_element_type=jnp.float32
    )
    sorted_key_gradient_reduced = jnp.einsum(
        "rnhts,rnthe->rnshe", grad_far, queries, preferred_element_type=jnp.float32
    ).astype(jnp.bfloat16)
    grad_sorted_values_low = grad_sorted_values.astype(jnp.bfloat16)
    grad_permute = jnp.einsum(
        "rithe,rjthe->rij",
        sorted_key_gradient_reduced,
        keys_all,
        preferred_element_type=jnp.float32,
    )
    grad_permute = grad_permute + jnp.einsum(
        "rithe,rjthe->rij", grad_sorted_values_low, values_all, preferred_element_type=jnp.float32
    )
    grad_keys = grad_keys_local + jnp.einsum(
        "rij,rithe->rjthe",
        block_permutation,
        sorted_key_gradient_reduced,
        preferred_element_type=jnp.float32,
    )
    grad_values = grad_values_local + jnp.einsum(
        "rij,rithe->rjthe",
        block_permutation,
        grad_sorted_values_low,
        preferred_element_type=jnp.float32,
    )
    grad_projected_low = (
        jnp.stack([grad_queries, grad_keys, grad_values], axis=3)
        .reshape(rows, length, 3 * width)
        .astype(jnp.bfloat16)
    )
    grad_qkv = outer_total(normed, grad_projected_low)
    grad_normed = matmul_back(grad_projected_low, proj[:, : 3 * width])
    balancing_pullback = jax.vjp(
        lambda score_logits: doubly_stochastic_normalize(score_logits, split_blocks),
        unnormalized_logits,
    )[1]
    grad_logits_low = balancing_pullback(grad_permute)[0].astype(jnp.bfloat16)
    grad_sort = outer_total(block_means, grad_logits_low)
    grad_means = matmul_back(grad_logits_low, sort_weight) / BLOCK
    grad_normed = grad_normed + jnp.broadcast_to(
        grad_means[:, :, None, :], (rows, blocks, BLOCK, width)
    ).reshape(rows, length, width)
    norm_pull = jax.vjp(layer_norm, inputs, norms[0], norms[1])[1]
    grad_inputs_norm, grad_gain_one, grad_shift_one = norm_pull(grad_normed)
    input_grad = hidden_grad + grad_inputs_norm
    grad_proj = jnp.concatenate([grad_qkv, grad_out_proj], axis=1)
    return (input_grad, grad_proj, grad_sort, grad_gain_one, grad_shift_one)


def adamw(master, first, second, grad, rate, decay):
    first_new = beta_first * first + (1.0 - beta_first) * grad
    second_new = beta_second * second + (1.0 - beta_second) * grad * grad
    first_hat = first_new / (1.0 - beta_first**STEP)
    second_hat = second_new / (1.0 - beta_second**STEP)
    master_new = master - rate * (first_hat / (jnp.sqrt(second_hat) + adam_eps) + decay * master)
    return (master_new, first_new, second_new)


def arrange(gathered):
    return (gathered[0], gathered[1], gathered[2], gathered[3], gathered[4].astype(jnp.float32))


def body(
    layer_input,
    doc_lengths,
    out_cotangent,
    proj_master,
    proj_moment1,
    proj_moment2,
    up_master,
    up_moment1,
    up_moment2,
    down_master,
    down_moment1,
    down_moment2,
    sort_master,
    sort_moment1,
    sort_moment2,
    norm_master,
    norm_moment1,
    norm_moment2,
):
    shard_low = (
        proj_master.astype(jnp.bfloat16),
        up_master.astype(jnp.bfloat16),
        down_master.astype(jnp.bfloat16),
        sort_master.astype(jnp.bfloat16),
        norm_master.astype(jnp.bfloat16),
    )
    weights_full = arrange(
        (
            lax.all_gather(shard_low[0], ("dp", "fsdp"), axis=0, tiled=True),
            lax.all_gather(shard_low[1], ("dp", "fsdp"), axis=0, tiled=True),
            lax.all_gather(shard_low[2], ("dp", "fsdp"), axis=0, tiled=True),
            lax.all_gather(shard_low[3], ("dp", "fsdp"), axis=0, tiled=True),
            lax.all_gather(shard_low[4], ("dp", "fsdp"), axis=1, tiled=True),
        )
    )
    segments = segment_ids(doc_lengths, layer_input.shape[1])
    inputs = layer_input.astype(jnp.float32)
    cotangent = out_cotangent.astype(jnp.float32)
    output, unused = forward(inputs, segments, weights_full)
    weights_back = arrange(
        (
            lax.all_gather(shard_low[0], ("dp", "fsdp"), axis=0, tiled=True),
            lax.all_gather(shard_low[1], ("dp", "fsdp"), axis=0, tiled=True),
            lax.all_gather(shard_low[2], ("dp", "fsdp"), axis=0, tiled=True),
            lax.all_gather(shard_low[3], ("dp", "fsdp"), axis=0, tiled=True),
            lax.all_gather(shard_low[4], ("dp", "fsdp"), axis=1, tiled=True),
        )
    )
    output_again, saved = forward(inputs, segments, weights_back)
    hidden_grad, grad_up, grad_down, grad_gain_two, grad_shift_two = ffn_backward(
        cotangent, saved, weights_back
    )
    input_grad, grad_proj, grad_sort, grad_gain_one, grad_shift_one = attn_backward(
        inputs, hidden_grad, saved, weights_back
    )
    grad_norm = jnp.stack([grad_gain_one, grad_shift_one, grad_gain_two, grad_shift_two], axis=0)
    sum_proj, sum_up, sum_down, sum_sort, sum_norm = (
        lax.psum_scatter(grad_proj, ("dp", "fsdp"), scatter_dimension=0, tiled=True),
        lax.psum_scatter(grad_up, ("dp", "fsdp"), scatter_dimension=0, tiled=True),
        lax.psum_scatter(grad_down, ("dp", "fsdp"), scatter_dimension=0, tiled=True),
        lax.psum_scatter(grad_sort, ("dp", "fsdp"), scatter_dimension=0, tiled=True),
        lax.psum_scatter(grad_norm, ("dp", "fsdp"), scatter_dimension=1, tiled=True),
    )
    proj_new, proj_first, proj_second = adamw(
        proj_master, proj_moment1, proj_moment2, sum_proj, rate_matrix, weight_decay
    )
    up_new, up_first, up_second = adamw(
        up_master, up_moment1, up_moment2, sum_up, rate_matrix, weight_decay
    )
    down_new, down_first, down_second = adamw(
        down_master, down_moment1, down_moment2, sum_down, rate_matrix, weight_decay
    )
    sort_new, sort_first, sort_second = adamw(
        sort_master, sort_moment1, sort_moment2, sum_sort, rate_other, weight_decay
    )
    norm_new, norm_first, norm_second = adamw(
        norm_master, norm_moment1, norm_moment2, sum_norm, rate_other, 0.0
    )
    return (
        output.astype(jnp.bfloat16),
        input_grad,
        proj_new,
        proj_first,
        proj_second,
        up_new,
        up_first,
        up_second,
        down_new,
        down_first,
        down_second,
        sort_new,
        sort_first,
        sort_second,
        norm_new,
        norm_first,
        norm_second,
    )


def solution(mesh):
    in_specs = (
        P(("dp", "fsdp"), None, None),
        P(("dp", "fsdp"), None),
        P(("dp", "fsdp"), None, None),
        P(("dp", "fsdp"), None),
        P(("dp", "fsdp"), None),
        P(("dp", "fsdp"), None),
        P(("dp", "fsdp"), None),
        P(("dp", "fsdp"), None),
        P(("dp", "fsdp"), None),
        P(("dp", "fsdp"), None),
        P(("dp", "fsdp"), None),
        P(("dp", "fsdp"), None),
        P(("dp", "fsdp"), None),
        P(("dp", "fsdp"), None),
        P(("dp", "fsdp"), None),
        P(None, ("dp", "fsdp")),
        P(None, ("dp", "fsdp")),
        P(None, ("dp", "fsdp")),
    )
    out_specs = (
        P(("dp", "fsdp"), None, None),
        P(("dp", "fsdp"), None, None),
        P(("dp", "fsdp"), None),
        P(("dp", "fsdp"), None),
        P(("dp", "fsdp"), None),
        P(("dp", "fsdp"), None),
        P(("dp", "fsdp"), None),
        P(("dp", "fsdp"), None),
        P(("dp", "fsdp"), None),
        P(("dp", "fsdp"), None),
        P(("dp", "fsdp"), None),
        P(("dp", "fsdp"), None),
        P(("dp", "fsdp"), None),
        P(("dp", "fsdp"), None),
        P(None, ("dp", "fsdp")),
        P(None, ("dp", "fsdp")),
        P(None, ("dp", "fsdp")),
    )
    return jax.shard_map(body, mesh=mesh, in_specs=in_specs, out_specs=out_specs, check_vma=False)
```

profile of v0, /device:TPU:0, one launch (start us, length us, event | category | flops | bytes accessed | tf_op | source)
XLA Modules:
  0.0 1746.0 jit_solution(2471495360586980248)
XLA Ops:
  13.1 43.3 %all-gather = bf16[32,16,4]{1,2,0:T(4,128)(2,1)S(1)} all-gather(bf16[1,16,4]{1,2,0:T(4,128)(2,1)S(1)} %convert_bitcast_fusion.2), channel_id=1, replica_groups=mesh['dp'=8,'fsdp'=4] {'dp','fsdp'}, dimensions={0}, use_global_device_ids=true | all-gather | bytes 4224 | tf_op jit(solution)/shard_map/all_gather | solution.py:314
  57.3 37.0 %all_gather.22 = bf16[512,128]{1,0:T(8,128)(2,1)S(1)} all-gather(bf16[16,128]{1,0:T(8,128)(2,1)S(1)} %convert_element_type.207), channel_id=1, replica_groups=mesh['dp'=8,'fsdp'=4] {'dp','fsdp'}, dimensions={0}, use_global_device_ids=true | all-gather | bytes 135168 | tf_op jit(solution)/shard_map/all_gather | solution.py:313
  138.4 12.4 convolution_convert_fusion
  150.9 31.0 %reshape.1774 = bf16[1,128,32,3,8,64]{5,4,3,2,1,0:T(8,128)(2,1)} reshape(bf16[4096,1536]{1,0:T(8,128)(2,1)} %convolution_convert_fusion) | data formatting | bytes 25165824 | tf_op jit(solution)/shard_map/reshape | solution.py:74
  181.8 24.4 %slice_bitcast_fusion.8 = (bf16[128,32,8,64]{3,2,1,0:T(8,128)(2,1)}, bf16[128,32,8,64]{3,2,1,0:T(8,128)(2,1)}, bf16[1,128,32,1,8,64]{5,4,3,2,1,0:T(8,128)(2,1)},...) fusion(bf16[1,128,32,3,8,64]{5,4,3,2,1,0:T(8,128)(2,1)} %reshape.1774), kind=kLoop, calls=%fused_computation.342 | loop fusion | bytes 33554432 | tf_op jit(solution)/shard_map/reshape.105
  206.3 11.5 copy.196
  224.3 13.0 copy.197
  237.4 11.9 copy.194
  255.9 13.0 copy.195
  268.8 11.5 fusion.37
  280.3 22.7 %multiply_bitcast_fusion = (f32[1,128,8,32,32]{4,3,2,1,0:T(8,128)}, f32[128,8,32]{2,1,0:T(8,128)S(1)}, f32[128,8,32]{2,1,0:T(8,128)S(1)}, f32[1,128,8,32,32]{4,3,2,1,0:T(8,128)}) fusion(f32[128,8,32,32]{3,2,1,0:T(8,128)} %fusion.37, pred[128,32,32]{2,1,0:T(8,128)(4,1)S(1)} %broadcast_compare_fusion.1, bf16[128,32,8,64]{3,1,2,0:T(8,128)(2,1)} %copy.195, ...), kind=kOutput, calls=%fused_computation.22 | convolution fusion | flops 139395072 | bytes 21364736 | tf_op jit(solution)/shard_map/rnthe,rnshe->rnhts/dot_general | solution.py:102
  303.1 37.1 %convert_reduce_fusion = (f32[128,8,32]{2,1,0:T(8,128)}, pred[1,128,8,32,64]{4,3,2,1,0:T(8,128)(4,1)}, f32[1,128,8,32,64]{4,3,2,1,0:T(8,128)S(1)}) fusion(f32[128,8,32]{2,1,0:T(8,128)S(1)} %reduce_max.198, f32[1,128,8,32,32]{4,3,2,1,0:T(8,128)} %get-tuple-element.153, f32[1,128,8,32,32]{4,3,2,1,0:T(8,128)} %get-tuple-element.171), kind=kLoop, calls=%fused_computation.14 | loop fusion | flops 8355840 | bytes 19136512 | tf_op jit(solution)/shard_map/jvp()/reduce_sum | solution.py:59
  361.0 13.8 fusion.38
  374.8 15.9 fusion.21
  390.7 15.1 copy.198
  405.8 12.2 convert_element_type.215
  428.7 18.5 %fusion.172 = f32[4096,2048]{1,0:T(8,128)} fusion(bf16[512,2048]{1,0:T(8,128)(2,1)} %all-gather.7.cloned.1.call-done, f32[1,4096,512]{1,2,0:T(8,128)} %copy-done.3, f32[512]{0:T(512)S(1)} %bitcast.236, f32[512]{0:T(512)S(1)} %bitcast.224, f32[4096]{0:T(1024)S(1)} %fusion.122, f32[4096]{0:T(1024)S(1)} %broadcast_multiply_fusion), kind=kOutput, calls=%fused_computation.345 | convolution fusion | flops 8600420352 | bytes 44077056 | tf_op jit(solution)/shard_map/...k,kn->...n/dot_general | solution.py:25
  447.1 20.5 %fusion.55 = f32[2048,512]{1,0:T(8,128)} fusion(bf16[1,4096,512]{2,1,0:T(8,128)(2,1)} %param.20, f32[4096,2048]{1,0:T(8,128)} %fusion.172), kind=kOutput, calls=%fused_computation.98 | convolution fusion | flops 8665432064 | bytes 41943040 | tf_op jit(solution)/shard_map/tk,tn->kn/dot_general | solution.py:35
  467.7 138.7 %reduce-scatter.12.cloned.1.call-done = f32[64,512]{1,0:T(8,128)} async-done(((f32[2048,512]{1,0:T(8,128)}), f32[64,512]{1,0:T(8,128)}) %reduce-scatter.12.cloned.1.call-update) | async-done | bytes 131088 | tf_op jit(solution)/shard_map/reduce_scatter | solution.py:341
  615.8 46.3 %all-gather.9.cloned.1.call-done = bf16[2048,512]{1,0:T(8,128)(2,1)} async-done(((bf16[64,512]{1,0:T(8,128)(2,1)}), bf16[2048,512]{1,0:T(8,128)(2,1)}) %all-gather.9.cloned.1.call-update) | async-done | bytes 2097168 | tf_op jit(solution)/shard_map/all_gather | solution.py:312
  662.1 32.0 %fusion.6 = bf16[4096,2048]{1,0:T(8,128)(2,1)} fusion(f32[4096,2048]{1,0:T(8,128)} %fusion.172, bf16[2048,512]{1,0:T(8,128)(2,1)} %all-gather.9.cloned.1.call-done, bf16[1,4096,512]{2,1,0:T(8,128)(2,1)} %param.20), kind=kOutput, calls=%fused_computation.8 | convolution fusion | flops 8757706752 | bytes 56623104 | tf_op jit(solution)/shard_map/...n,kn->...k/dot_general | solution.py:29
  694.1 15.1 fusion.197
  753.5 11.5 convolution_bitcast_fusion
  765.0 12.7 convert_bitcast_fusion
  777.7 11.6 convolution_bitcast_fusion.1
  800.1 21.7 %multiply_reduce_fusion = f32[128,8,32]{2,1,0:T(8,128)S(1)} fusion(f32[1,128,8,32,64]{4,3,2,1,0:T(8,128)} %copy-done, f32[128,8,32]{2,1,0:T(8,128)S(1)} %copy-done.26, f32[128,8,32]{2,1,0:T(8,128)S(1)} %copy-done.9, f32[1,128,8,32,32]{4,3,2,1,0:T(8,128)} %convolution_bitcast_fusion, f32[1,128,8,32,32]{4,3,2,1,0:T(8,128)} %convolution_bitcast_fusion.1), kind=kLoop, calls=%fused_computation.16 | loop fusion | flops 10452992 | bytes 17170432 | tf_op jit(solution)/shard_map/transpose(jvp())/reduce_sum | solution.py:61
  821.9 27.8 %fusion.188 = (f32[128,8,32]{2,1,0:T(8,128)S(1)}, f32[1,128,8,32,64]{4,3,2,1,0:T(8,128)S(1)}) fusion(f32[1,128,8,32,64]{4,3,2,1,0:T(8,128)} %copy-done, f32[128,8,32]{2,1,0:T(8,128)S(1)} %copy-done.9, f32[128,8,32]{2,1,0:T(8,128)S(1)} %neg.177, f32[128,8,32]{2,1,0:T(8,128)S(1)} %copy-done.20, f32[1,128,8,32,32]{4,3,2,1,0:T(8,128)} %convolution_bitcast_fusion, ...), kind=kLoop, calls=%fused_computation.353 | loop fusion | flops 12550144 | bytes 25690112 | tf_op jit(solution)/shard_map/transpose(jvp())/reduce_sum | solution.py:60
  856.1 11.5 convert_bitcast_fusion.1
  867.6 19.3 %fusion.70 = f32[128,128]{1,0:T(8,128)S(1)} fusion(bf16[128,32,8,64]{3,2,1,0:T(8,128)(2,1)} %get-tuple-element.147, bf16[128,32,8,64]{3,1,2,0:T(8,128)(2,1)} %convert_bitcast_fusion.1), kind=kOutput, calls=%fused_computation.114 | convolution fusion | flops 536870912 | bytes 8454144 | tf_op jit(solution)/shard_map/rithe,rjthe->rij/dot_general | solution.py:223
  887.0 11.5 copy.211
  909.4 14.5 fusion.36
  923.8 14.5 fusion.42
  938.3 11.4 copy.217
  956.3 14.7 copy.214
  971.5 19.9 %fusion.196 = (f32[128]{0:T(128)S(1)}, f32[128,128]{1,0:T(8,128)S(1)}) fusion(f32[128]{0:T(128)} %copy-done.149, f32[128]{0:T(128)S(1)} %copy-done.77, f32[128]{0:T(128)S(1)} %copy-done.66, f32[128]{0:T(128)S(1)} %copy-done.62, f32[128,128]{1,0:T(8,128)S(1)} %copy-done.11, f32[128]{0:T(128)S(1)} %copy-done.56, f32[128,128]{1,0:T(8,128)S(1)} %fusion.70, ...), kind=kOutput, calls=%fused_computation.361 | convolution fusion | flops 537001856 | bytes 8588288 | tf_op jit(solution)/shard_map/rithe,rjthe->rij/dot_general | solution.py:229
  1018.8 14.6 copy.209
  1033.4 14.6 copy.206
  1047.9 15.0 copy.207
  1100.1 35.0 %copy.218 = bf16[1,128,32,3,8,64]{5,4,3,2,1,0:T(8,128)(2,1)} copy(bf16[1,128,32,3,8,64]{1,5,4,3,2,0:T(8,128)(2,1)} %maximum_convert_fusion) | data formatting | bytes 25165824 | tf_op jit(solution)/shard_map/convert_element_type | solution.py:247
  1135.1 32.7 %convert_element_type.234 = bf16[4096,1536]{1,0:T(8,128)(2,1)} reshape(bf16[1,128,32,3,8,64]{5,4,3,2,1,0:T(8,128)(2,1)} %copy.218) | data formatting | bytes 25165824 | tf_op jit(solution)/shard_map/convert_element_type | solution.py:247
  1167.8 15.7 fusion.20
  1196.3 16.3 fusion.170
  1231.0 21.1 %fusion.33 = bf16[1,4096,512]{1,2,0:T(8,128)(2,1)} fusion(f32[1,4096,512]{1,2,0:T(8,128)} %copy-done.3, bf16[2048,512]{1,0:T(8,128)(2,1)S(1)} %copy-done.150, f32[4096,2048]{1,0:T(8,128)} %fusion.172), kind=kOutput, calls=%fused_computation.69 | convolution fusion | flops 8669626368 | bytes 48234496 | tf_op jit(solution)/shard_map/...k,kn->...n/dot_general | solution.py:25
  1258.6 13.6 add_add_fusion.2
  1281.4 46.1 %reduce-scatter.16.cloned.1.call-done = f32[16,4]{1,0:T(8,128)} async-done(((f32[512,4]{1,0:T(8,128)}), f32[16,4]{1,0:T(8,128)}) %reduce-scatter.16.cloned.1.call-update) | async-done | bytes 272
  1328.9 130.1 %reduce-scatter.14.cloned.1.call-done = f32[16,128]{1,0:T(8,128)} async-done(((f32[512,128]{1,0:T(8,128)}), f32[16,128]{1,0:T(8,128)}) %reduce-scatter.14.cloned.1.call-update) | async-done | bytes 8208 | tf_op jit(solution)/shard_map/reduce_scatter | solution.py:342
  1460.4 137.8 %reduce-scatter.10.cloned.1.call-done = f32[16,2048]{1,0:T(8,128)} async-done(((f32[512,2048]{1,0:T(8,128)}), f32[16,2048]{1,0:T(8,128)}) %reduce-scatter.10.cloned.1.call-update) | async-done | bytes 131088 | tf_op jit(solution)/shard_map/reduce_scatter | solution.py:340
  1599.9 137.4 %reduce-scatter.8.cloned.1.call-done = f32[16,2048]{1,0:T(8,128)} async-done(((f32[512,2048]{1,0:T(8,128)}), f32[16,2048]{1,0:T(8,128)}) %reduce-scatter.8.cloned.1.call-update) | async-done | bytes 131088 | tf_op jit(solution)/shard_map/reduce_scatter | solution.py:339
  (492 shorter events, 300.2 us)
Async XLA Ops:
  7.2 131.2 %all-gather.5.cloned.1.call-start = ((), (), s32[]{:S(2)}) async-start(), calls=%async_computation.5 | async-start | bytes 2162688 | tf_op jit(solution)/shard_map/all_gather | solution.py:310
  8.8 419.8 %all-gather.7.cloned.1.call-start = ((), (), s32[]{:S(2)}) async-start(), calls=%async_computation.6 | async-start | bytes 2162688 | tf_op jit(solution)/shard_map/all_gather | solution.py:311
  10.4 596.0 %reduce-scatter.12.cloned.1.call-start = ((), (), s32[]{:S(2)}) async-start(), calls=%async_computation.10 | async-start | bytes 4325376 | tf_op jit(solution)/shard_map/reduce_scatter | solution.py:341
  57.2 81.1 %copy-start.67 = (f32[1,512]{1,0:T(1,128)}, f32[1,512]{1,0:T(1,128)S(1)}, u32[]{:S(2)}) copy-start(f32[1,512]{1,0:T(1,128)S(1)} %get-tuple-element.159) | copy-start | bytes 6148
  57.2 81.1 %copy-start.88 = (f32[1,512]{1,0:T(1,128)}, f32[1,512]{1,0:T(1,128)S(1)}, u32[]{:S(2)}) copy-start(f32[1,512]{1,0:T(1,128)S(1)} %get-tuple-element.158) | copy-start | bytes 6148
  94.3 33.9 %copy-start.27 = (bf16[512,128]{1,0:T(8,128)(2,1)}, bf16[512,128]{1,0:T(8,128)(2,1)S(1)}, u32[]{:S(2)}) copy-start(bf16[512,128]{1,0:T(8,128)(2,1)S(1)} %all_gather.22) | copy-start | bytes 393220
  95.3 185.1 %copy-start.13 = (pred[128,32,32]{2,1,0:T(8,128)(4,1)}, pred[128,32,32]{2,1,0:T(8,128)(4,1)S(1)}, u32[]{:S(2)}) copy-start(pred[128,32,32]{2,1,0:T(8,128)(4,1)S(1)} %broadcast_compare_fusion.1) | copy-start | bytes 393220
  105.2 33.2 %copy-start.33 = (f32[4096]{0:T(1024)}, f32[4096]{0:T(1024)S(1)}, u32[]{:S(2)}) copy-start(f32[4096]{0:T(1024)S(1)} %broadcast_multiply_fusion.1) | copy-start | bytes 49156
  108.6 29.8 %copy-start.35 = (f32[4096]{0:T(1024)}, f32[4096]{0:T(1024)S(1)}, u32[]{:S(2)}) copy-start(f32[4096]{0:T(1024)S(1)} %fusion.121) | copy-start | bytes 49156
  138.3 110.9 %copy-start.29 = (bf16[128,128]{1,0:T(8,128)(2,1)}, bf16[128,128]{1,0:T(8,128)(2,1)S(1)}, u32[]{:S(2)}) copy-start(bf16[128,128]{1,0:T(8,128)(2,1)S(1)} %fusion.111) | copy-start | bytes 98308
  303.1 46.7 %copy-start.8 = (f32[128,8,32]{2,1,0:T(8,128)}, f32[128,8,32]{2,1,0:T(8,128)S(1)}, u32[]{:S(2)}) copy-start(f32[128,8,32]{2,1,0:T(8,128)S(1)} %reduce_max.198) | copy-start | bytes 393220
  349.8 265.1 %copy-start.19 = (f32[128,8,32]{2,1,0:T(8,128)}, f32[128,8,32]{2,1,0:T(8,128)S(1)}, u32[]{:S(2)}) copy-start(f32[128,8,32]{2,1,0:T(8,128)S(1)} %fusion.13) | copy-start | bytes 393220
  424.4 301.8 %copy-start.37 = (f32[4096]{0:T(1024)}, f32[4096]{0:T(1024)S(1)}, u32[]{:S(2)}) copy-start(f32[4096]{0:T(1024)S(1)} %broadcast_multiply_fusion) | copy-start | bytes 49156
  428.6 297.7 %copy-start.45 = (f32[4096]{0:T(1024)}, f32[4096]{0:T(1024)S(1)}, u32[]{:S(2)}) copy-start(f32[4096]{0:T(1024)S(1)} %fusion.122) | copy-start | bytes 49156
  447.1 159.3 %copy-start.48 = (f32[64,512]{1,0:T(8,128)S(1)}, f32[64,512]{1,0:T(8,128)}, u32[]{:S(2)}) copy-start(f32[64,512]{1,0:T(8,128)} %param.27) | copy-start | bytes 393220
  447.1 159.3 %copy-start.49 = (f32[64,512]{1,0:T(8,128)S(1)}, f32[64,512]{1,0:T(8,128)}, u32[]{:S(2)}) copy-start(f32[64,512]{1,0:T(8,128)} %param.28) | copy-start | bytes 393220
  447.1 159.3 %copy-start.50 = (f32[64,512]{1,0:T(8,128)S(1)}, f32[64,512]{1,0:T(8,128)}, u32[]{:S(2)}) copy-start(f32[64,512]{1,0:T(8,128)} %param.29) | copy-start | bytes 393220
  467.7 194.4 %all-gather.9.cloned.1.call-start = ((), (), s32[]{:S(2)}) async-start(), calls=%async_computation.7 | async-start | bytes 2162688 | tf_op jit(solution)/shard_map/all_gather | solution.py:312
  608.2 719.4 %reduce-scatter.16.cloned.1.call-start = ((), (), s32[]{:S(2)}) async-start(), calls=%async_computation.12 | async-start | bytes 270336
  662.1 32.0 %copy-start.151 = (bf16[512,2048]{1,0:T(8,128)(2,1)S(1)}, bf16[512,2048]{1,0:T(8,128)(2,1)}, u32[]{:S(2)}) copy-start(bf16[512,2048]{1,0:T(8,128)(2,1)} %all-gather.7.cloned.1.call-done) | copy-start | bytes 6291460
  971.4 28.8 %copy-start.22 = (f32[128,128]{1,0:T(8,128)S(1)}, f32[128,128]{1,0:T(8,128)}, u32[]{:S(2)}) copy-start(f32[128,128]{1,0:T(8,128)} %copy-done.21) | copy-start | bytes 196612
  971.4 28.8 %copy-start.64 = (f32[128]{0:T(128)S(1)}, f32[128]{0:T(128)}, u32[]{:S(2)}) copy-start(f32[128]{0:T(128)} %copy-done.63) | copy-start | bytes 1540
  971.4 28.8 %copy-start.75 = (f32[128]{0:T(128)S(1)}, f32[128]{0:T(128)}, u32[]{:S(2)}) copy-start(f32[128]{0:T(128)} %copy-done.74) | copy-start | bytes 1540
  971.4 28.8 %copy-start.85 = (f32[128]{0:T(128)S(1)}, f32[128]{0:T(128)}, u32[]{:S(2)}) copy-start(f32[128]{0:T(128)} %copy-done.84) | copy-start | bytes 1540
  971.4 28.9 %copy-start.130 = (f32[128]{0:T(128)S(1)}, f32[128]{0:T(128)}, u32[]{:S(2)}) copy-start(f32[128]{0:T(128)} %copy-done.129) | copy-start | bytes 1540
  971.4 28.9 %copy-start.94 = (f32[128]{0:T(128)S(1)}, f32[128]{0:T(128)}, u32[]{:S(2)}) copy-start(f32[128]{0:T(128)} %copy-done.93) | copy-start | bytes 1540
  971.5 29.1 %copy-start.128 = (f32[128]{0:T(128)S(1)}, f32[128]{0:T(128)}, u32[]{:S(2)}) copy-start(f32[128]{0:T(128)} %copy-done.127) | copy-start | bytes 1540
  971.5 29.1 %copy-start.28 = (bf16[512,128]{1,0:T(8,128)(2,1)S(1)}, bf16[512,128]{1,0:T(8,128)(2,1)}, u32[]{:S(2)}) copy-start(bf16[512,128]{1,0:T(8,128)(2,1)} %copy-done.27) | copy-start | bytes 393220
  971.5 29.1 %copy-start.109 = (f32[128]{0:T(128)S(1)}, f32[128]{0:T(128)}, u32[]{:S(2)}) copy-start(f32[128]{0:T(128)} %copy-done.108) | copy-start | bytes 1540
  971.5 29.4 %copy-start.7 = (bf16[128,32,8,64]{0,3,2,1:T(8,128)(2,1)S(1)}, bf16[128,32,8,64]{0,3,2,1:T(8,128)(2,1)}, u32[]{:S(2)}) copy-start(bf16[128,32,8,64]{0,3,2,1:T(8,128)(2,1)} %copy.211) | copy-start | bytes 12582916
  1135.1 32.7 %copy-start.34 = (f32[4096]{0:T(1024)S(1)}, f32[4096]{0:T(1024)}, u32[]{:S(2)}) copy-start(f32[4096]{0:T(1024)} %copy-done.33) | copy-start | bytes 49156
  1135.1 32.7 %copy-start.47 = (bf16[512,2048]{1,0:T(8,128)(2,1)S(1)}, bf16[512,2048]{1,0:T(8,128)(2,1)}, u32[]{:S(2)}) copy-start(bf16[512,2048]{1,0:T(8,128)(2,1)} %all-gather.5.cloned.1.call-done) | copy-start | bytes 6291460
  1135.1 32.7 %copy-start.68 = (f32[1,512]{1,0:T(1,128)S(1)}, f32[1,512]{1,0:T(1,128)}, u32[]{:S(2)}) copy-start(f32[1,512]{1,0:T(1,128)} %copy-done.67) | copy-start | bytes 6148
  1195.1 264.0 %reduce-scatter.14.cloned.1.call-start = ((), (), s32[]{:S(2)}) async-start(), calls=%async_computation.11 | async-start | bytes 270336 | tf_op jit(solution)/shard_map/reduce_scatter | solution.py:342
  1196.2 402.0 %reduce-scatter.10.cloned.1.call-start = ((), (), s32[]{:S(2)}) async-start(), calls=%async_computation.9 | async-start | bytes 4325376 | tf_op jit(solution)/shard_map/reduce_scatter | solution.py:340
  1212.7 524.6 %reduce-scatter.8.cloned.1.call-start = ((), (), s32[]{:S(2)}) async-start(), calls=%async_computation.8 | async-start | bytes 4325376 | tf_op jit(solution)/shard_map/reduce_scatter | solution.py:339
  1272.2 56.1 %copy-start.92 = (f32[4,16]{1,0:T(4,128)S(1)}, f32[4,16]{1,0:T(4,128)}, u32[]{:S(2)}) copy-start(f32[4,16]{1,0:T(4,128)} %param.33) | copy-start | bytes 772
  1272.2 56.1 %copy-start.122 = (f32[4,16]{1,0:T(4,128)S(1)}, f32[4,16]{1,0:T(4,128)}, u32[]{:S(2)}) copy-start(f32[4,16]{1,0:T(4,128)} %param.34) | copy-start | bytes 772
  1272.2 56.1 %copy-start.123 = (f32[4,16]{1,0:T(4,128)S(1)}, f32[4,16]{1,0:T(4,128)}, u32[]{:S(2)}) copy-start(f32[4,16]{1,0:T(4,128)} %param.35) | copy-start | bytes 772
  1272.2 186.9 %copy-start.69 = (f32[16,128]{1,0:T(8,128)S(1)}, f32[16,128]{1,0:T(8,128)}, u32[]{:S(2)}) copy-start(f32[16,128]{1,0:T(8,128)} %param.30) | copy-start | bytes 24580
  1272.2 186.9 %copy-start.90 = (f32[16,128]{1,0:T(8,128)S(1)}, f32[16,128]{1,0:T(8,128)}, u32[]{:S(2)}) copy-start(f32[16,128]{1,0:T(8,128)} %param.31) | copy-start | bytes 24580
  1272.2 186.9 %copy-start.91 = (f32[16,128]{1,0:T(8,128)S(1)}, f32[16,128]{1,0:T(8,128)}, u32[]{:S(2)}) copy-start(f32[16,128]{1,0:T(8,128)} %param.32) | copy-start | bytes 24580
  1272.2 325.9 %copy-start.31 = (f32[16,2048]{1,0:T(8,128)S(1)}, f32[16,2048]{1,0:T(8,128)}, u32[]{:S(2)}) copy-start(f32[16,2048]{1,0:T(8,128)} %param.24) | copy-start | bytes 393220
  1272.2 325.9 %copy-start.51 = (f32[16,2048]{1,0:T(8,128)S(1)}, f32[16,2048]{1,0:T(8,128)}, u32[]{:S(2)}) copy-start(f32[16,2048]{1,0:T(8,128)} %param.25) | copy-start | bytes 393220
  1272.3 325.9 %copy-start.52 = (f32[16,2048]{1,0:T(8,128)S(1)}, f32[16,2048]{1,0:T(8,128)}, u32[]{:S(2)}) copy-start(f32[16,2048]{1,0:T(8,128)} %param.26) | copy-start | bytes 393220
  1272.3 465.0 %copy-start.32 = (f32[16,2048]{1,0:T(8,128)S(1)}, f32[16,2048]{1,0:T(8,128)}, u32[]{:S(2)}) copy-start(f32[16,2048]{1,0:T(8,128)} %param.21) | copy-start | bytes 393220
  1272.3 465.0 %copy-start.53 = (f32[16,2048]{1,0:T(8,128)S(1)}, f32[16,2048]{1,0:T(8,128)}, u32[]{:S(2)}) copy-start(f32[16,2048]{1,0:T(8,128)} %param.22) | copy-start | bytes 393220
  1272.3 465.0 %copy-start.54 = (f32[16,2048]{1,0:T(8,128)S(1)}, f32[16,2048]{1,0:T(8,128)}, u32[]{:S(2)}) copy-start(f32[16,2048]{1,0:T(8,128)} %param.23) | copy-start | bytes 393220
  (112 other events, 1257.5 us)
Sparse Core Ops, SparseCore 0:
  11.5 59.2 all-gather.4
  74.2 55.3 all-gather.6
  467.8 138.5 reduce-scatter.11
  609.7 52.2 all-gather.8
  1195.2 132.2 reduce-scatter.15
  1329.7 129.3 reduce-scatter.13
  1461.4 136.7 reduce-scatter.9
  1600.4 136.7 reduce-scatter.7
where the time goes:
time: 1760 us; the launch traced here: 1750 us
  waiting for transfers between devices  637 us (36%)
  matrix products  401 us (23%)
  local copies, waits for them, and re-layouts  365 us (21%)
  other arithmetic  246 us (14%)
  blocking collectives  80.3 us (5%)
    reduce_scatter x1, waiting for transfers between devices, body(): lax.psum_scatter(grad_down, ('dp', 'fsdp'), scatter_dimension=0, tiled=True)  139 us
    reduce_scatter x1, waiting for transfers between devices, body(): lax.psum_scatter(grad_up, ('dp', 'fsdp'), scatter_dimension=0, tiled=True)  138 us
    reduce_scatter x1, waiting for transfers between devices, body(): lax.psum_scatter(grad_proj, ('dp', 'fsdp'), scatter_dimension=0, tiled=True)  137 us
    reduce_scatter x1, waiting for transfers between devices, body(): lax.psum_scatter(grad_sort, ('dp', 'fsdp'), scatter_dimension=0, tiled=True)  130 us
    another operation x6, local copies, waits for them, and re-layouts  81.9 us
    dot_general x5, matrix products, matmul_back(): jnp.einsum('...n,kn->...k', grad, right, preferred_element_type=jnp.float32)  69.7 us
    convert_element_type x2, local copies, waits for them, and re-layouts, attn_backward(): grad_projected_low = jnp.stack([grad_queries, grad_keys, grad_values], ax...  67.7 us
    dot_general x5, matrix products, matmul(): jnp.einsum('...k,kn->...n', left, right, preferred_element_type=jnp.float32)  58.6 us
  transfers between devices with their start and end apart: 8, of which 6 were waited for; matrix products, arithmetic and copies ran while one was open for 25% of the time, Pallas kernels for 0%

commit v1 on v0

v1 whole, which is shorter than its diff:
```python
import functools
import jax
import jax.numpy as jnp
from jax import lax
from jax.experimental import pallas as pl
from jax.experimental.pallas import tpu as pltpu
from jax.sharding import PartitionSpec as P

HD = 64
BLOCK = 32
SINK_ITERS = 8
STEP = 10
TILE = 512
LANES = 128

mask_penalty = 6.0
score_floor = -1000000000.0
norm_eps = 1e-05
beta_first = 0.9
beta_second = 0.95
adam_eps = 1e-08
weight_decay = 0.1
rate_matrix = 0.1
rate_other = 0.5

bf16 = jnp.bfloat16
f32 = jnp.float32
VMEM_LIMIT = 62 * 2**20


def dot(left, right):
    return lax.dot_general(left, right, (((1,), (0,)), ((), ())), preferred_element_type=f32)


def dot_nt(left, right):
    return lax.dot_general(left, right, (((1,), (1,)), ((), ())), preferred_element_type=f32)


def dot_tn(left, right):
    return lax.dot_general(left, right, (((0,), (0,)), ((), ())), preferred_element_type=f32)


def doc_ends(lengths_ref):
    total = lengths_ref[0, 0]
    ends = [total]
    for k in range(1, lengths_ref.shape[1]):
        total = total + lengths_ref[0, k]
        ends.append(total)
    return ends


def segments_of(places, ends):
    count = jnp.zeros(places.shape, jnp.int32)
    for end in ends:
        count = count + (places >= end).astype(jnp.int32)
    return count


def center_scale(values):
    centre = values - jnp.mean(values, axis=-1, keepdims=True)
    spread = jnp.mean(centre * centre, axis=-1, keepdims=True)
    inverse = lax.rsqrt(spread + norm_eps)
    return centre * inverse, inverse


def log_sum_exp(logits, axis):
    top = jnp.max(logits, axis=axis, keepdims=True)
    return top + jnp.log(jnp.sum(jnp.exp(logits - top), axis=axis, keepdims=True))


def front_kernel(
    lengths_ref, norms_ref, x_ref, proj_ref, sort_ref,
    normed_hbm, qkv_hbm, skv_hbm, tkv_hbm, means_ref, states_ref,
    normed_s, stage, qkv_buf, low_buf, flip_buf, copy_sem, qkv_sem, low_sem, flip_sem,
):
    seq, width = x_ref.shape
    tiles = seq // TILE
    blocks = seq // BLOCK
    per_tile = TILE // BLOCK
    chunks = 2 * width // LANES
    ends = doc_ends(lengths_ref)
    gain = norms_ref[0:1, :].astype(f32)
    shift = norms_ref[1:2, :].astype(f32)

    def norm_step(k, carry):
        rows = pl.ds(pl.multiple_of(k * TILE, TILE), TILE)
        xhat, unused = center_scale(x_ref[rows, :].astype(f32))
        normed = (xhat * gain + shift).astype(bf16)
        normed_s[rows, :] = normed
        sums = jnp.sum(normed.astype(f32).reshape(per_tile, BLOCK, width), axis=1)
        means_ref[pl.ds(pl.multiple_of(k * per_tile, per_tile), per_tile), :] = (
            sums * (1.0 / BLOCK)
        ).astype(bf16)
        return carry

    lax.fori_loop(0, tiles, norm_step, 0)
    normed_copy = pltpu.make_async_copy(normed_s, normed_hbm, copy_sem)
    normed_copy.start()

    logits = dot(means_ref[...], sort_ref[...])
    first_i = segments_of(lax.broadcasted_iota(jnp.int32, (blocks, blocks), 0) * BLOCK, ends)
    first_j = segments_of(lax.broadcasted_iota(jnp.int32, (blocks, blocks), 1) * BLOCK, ends)
    logits = jnp.where(first_i != first_j, logits - mask_penalty, logits)

    def qkv_copy(k, slot):
        rows = pl.ds(pl.multiple_of(k * TILE, TILE), TILE)
        return pltpu.make_async_copy(qkv_buf.at[slot], qkv_hbm.at[rows, :], qkv_sem.at[slot])

    def project_step(k, logits):
        rows = pl.ds(pl.multiple_of(k * TILE, TILE), TILE)
        slot = lax.rem(k, 2)

        @pl.when(k >= 2)
        def _():
            qkv_copy(k - 2, slot).wait()

        logits = logits - log_sum_exp(logits, 1)
        states_ref[2 * k] = jnp.exp(logits)
        logits = logits - log_sum_exp(logits, 0)
        states_ref[2 * k + 1] = jnp.exp(logits)
        normed = normed_s[rows, :]
        qkv_buf[slot, :, :width] = dot(normed, proj_ref[:, :width]).astype(bf16)
        for half in range(2):
            columns = slice((1 + half) * width, (2 + half) * width)
            product = dot(normed, proj_ref[:, columns]).astype(bf16)
            qkv_buf[slot, :, columns] = product
            wide = product.astype(f32)
            for c in range(width // LANES):
                stage[half * (width // LANES) + c, rows, :] = wide[:, c * LANES : (c + 1) * LANES]
        qkv_copy(k, slot).start()
        return logits

    assert tiles == SINK_ITERS
    lax.fori_loop(0, tiles, project_step, logits)
    permute = states_ref[2 * SINK_ITERS - 1].astype(bf16)

    def flip_copy(t, slot):
        return pltpu.make_async_copy(flip_buf.at[slot], tkv_hbm.at[t], flip_sem.at[slot])

    def sort_step(i, carry):
        group = flip_buf.shape[0]

        @pl.when(i >= 1)
        def _():
            for u in range(group):
                flip_copy((i - 1) * group + u, u).wait()

        loaded = []
        for u in range(group):
            t = i * group + u
            loaded.append(
                jnp.concatenate(
                    [stage[c, pl.ds(t, blocks, stride=BLOCK), :] for c in range(chunks)], axis=1
                ).astype(bf16)
            )
        for u in range(group):
            t = i * group + u
            flip_buf[u] = loaded[u].T
            flip_copy(t, u).start()
            moved = dot(permute, loaded[u])
            for c in range(chunks):
                stage[c, pl.ds(t, blocks, stride=BLOCK), :] = moved[:, c * LANES : (c + 1) * LANES]
        return carry

    group = flip_buf.shape[0]
    lax.fori_loop(0, BLOCK // group, sort_step, 0)

    def low_copy(k, slot):
        rows = pl.ds(pl.multiple_of(k * TILE, TILE), TILE)
        return pltpu.make_async_copy(low_buf.at[slot], skv_hbm.at[rows, :], low_sem.at[slot])

    def low_step(k, carry):
        rows = pl.ds(pl.multiple_of(k * TILE, TILE), TILE)
        slot = lax.rem(k, 2)

        @pl.when(k >= 2)
        def _():
            low_copy(k - 2, slot).wait()

        for c in range(chunks):
            low_buf[slot, :, c * LANES : (c + 1) * LANES] = stage[c, rows, :].astype(bf16)
        low_copy(k, slot).start()
        return carry

    lax.fori_loop(0, tiles, low_step, 0)
    for u in range(group):
        flip_copy(BLOCK - group + u, u).wait()
    for k in (tiles - 2, tiles - 1):
        qkv_copy(k, k % 2).wait()
        low_copy(k, k % 2).wait()
    normed_copy.wait()


def front(lengths, norms, x, proj, sort):
    seq, width = x.shape
    blocks = seq // BLOCK
    hbm = pl.BlockSpec(memory_space=pl.ANY)
    vmem = pl.BlockSpec(memory_space=pltpu.VMEM)
    return pl.pallas_call(
        front_kernel,
        out_shape=(
            jax.ShapeDtypeStruct((seq, width), bf16),
            jax.ShapeDtypeStruct((seq, 3 * width), bf16),
            jax.ShapeDtypeStruct((seq, 2 * width), bf16),
            jax.ShapeDtypeStruct((BLOCK, 2 * width, blocks), bf16),
            jax.ShapeDtypeStruct((blocks, width), bf16),
            jax.ShapeDtypeStruct((2 * SINK_ITERS, blocks, blocks), f32),
        ),
        in_specs=[pl.BlockSpec(memory_space=pltpu.SMEM), vmem, vmem, vmem, vmem],
        out_specs=[hbm, hbm, hbm, hbm, vmem, vmem],
        scratch_shapes=[
            pltpu.VMEM((seq, width), bf16),
            pltpu.VMEM((2 * width // LANES, seq, LANES), f32),
            pltpu.VMEM((2, TILE, 3 * width), bf16),
            pltpu.VMEM((2, TILE, 2 * width), bf16),
            pltpu.VMEM((2, 2 * width, blocks), bf16),
            pltpu.SemaphoreType.DMA,
            pltpu.SemaphoreType.DMA((2,)),
            pltpu.SemaphoreType.DMA((2,)),
            pltpu.SemaphoreType.DMA((2,)),
        ],
        compiler_params=pltpu.CompilerParams(vmem_limit_bytes=VMEM_LIMIT),
        name="front",
    )(lengths, norms, x, proj, sort)


def layer_norm_back(grad, gain, xhat, inverse):
    scaled = grad * gain
    mean_one = jnp.mean(scaled, axis=-1, keepdims=True)
    mean_two = jnp.mean(scaled * xhat, axis=-1, keepdims=True)
    return (scaled - mean_one - xhat * mean_two) * inverse


def middle_kernel(
    lengths_ref, norms_ref, x_ref, cot_ref, qkv_ref, skv_ref, out_proj_ref, up_ref, down_ref,
    y_ref, hidden_grad_ref, gq_ref, gkv_ref, gskv_ref, gup_ref, gdown_ref, gout_ref, gnorm_ref,
    gup, gdown, gout, probs_s, context_s, gcontext_s,
):
    step = pl.program_id(0)
    tile, width = x_ref.shape
    hidden_units = up_ref.shape[1]
    pairs = tile // (2 * BLOCK)
    head_pairs = width // LANES
    scale = HD ** (-0.5)
    ends = doc_ends(lengths_ref)

    @pl.when(step == 0)
    def _():
        gup[...] = jnp.zeros_like(gup)
        gdown[...] = jnp.zeros_like(gdown)
        gout[...] = jnp.zeros_like(gout)
        gnorm_ref[...] = jnp.zeros_like(gnorm_ref)

    lane = lax.broadcasted_iota(jnp.int32, (1, LANES), 1)
    low_head = lane < HD
    low_block = lax.rem(lane, 2 * BLOCK) < BLOCK
    zero = jnp.zeros((), bf16)

    def two_heads(part):
        return jnp.concatenate(
            [jnp.where(low_head, part, zero), jnp.where(low_head, zero, part)], axis=0
        )

    def two_blocks(part):
        return jnp.concatenate(
            [jnp.where(low_block, part, zero), jnp.where(low_block, zero, part)], axis=0
        )

    def stack_keys(own, far):
        return jnp.concatenate(
            [own[:BLOCK], far[:BLOCK], own[BLOCK:], far[BLOCK:]], axis=0
        )

    def pick_block(full):
        return jnp.where(low_block, full[: 2 * BLOCK], full[2 * BLOCK :])

    def pick_head(full):
        return jnp.where(low_head, full[: 2 * BLOCK], full[2 * BLOCK :])

    def attend(p, carry):
        rows = pl.ds(pl.multiple_of(p * 2 * BLOCK, 2 * BLOCK), 2 * BLOCK)
        base = step * tile + p * 2 * BLOCK
        query_seg = segments_of(base + lax.rem(lane, 2 * BLOCK), ends)
        key_place = (
            base
            + jnp.where(low_block, 0, BLOCK)
            + lax.broadcasted_iota(jnp.int32, (BLOCK, LANES), 0)
        )
        same = segments_of(key_place, ends) == query_seg
        for hp in range(head_pairs):
            cols = slice(hp * LANES, (hp + 1) * LANES)
            key_cols = slice(width + hp * LANES, width + (hp + 1) * LANES)
            value_cols = slice(2 * width + hp * LANES, 2 * width + (hp + 1) * LANES)
            queries = two_heads(qkv_ref[rows, cols])
            keys = stack_keys(qkv_ref[rows, key_cols], skv_ref[rows, cols])
            values = stack_keys(qkv_ref[rows, value_cols], skv_ref[rows, key_cols])
            scores = pick_block(dot(keys, queries.T)) * scale
            scores = jnp.concatenate(
                [jnp.where(same, scores[:BLOCK], score_floor), scores[BLOCK:]], axis=0
            )
            exps = jnp.exp(scores - jnp.max(scores, axis=0, keepdims=True))
            probs = (exps / jnp.sum(exps, axis=0, keepdims=True)).astype(bf16)
            probs_s[p * head_pairs + hp] = probs
            context_s[rows, cols] = pick_head(dot_tn(two_blocks(probs), values)).astype(bf16)
        return carry

    lax.fori_loop(0, pairs, attend, 0)

    inputs = x_ref[...].astype(f32)
    context = context_s[...]
    hidden = inputs + dot(context, out_proj_ref[...])
    xhat_two, inverse_two = center_scale(hidden)
    gain_two = norms_ref[2:3, :].astype(f32)
    normed_two = (xhat_two * gain_two + norms_ref[3:4, :].astype(f32)).astype(bf16)
    normed_two_t = normed_two.T
    cot = cot_ref[...]
    total_out = hidden
    grad_normed_two = None
    root = 0.7978845608028654
    for c in range(hidden_units // TILE):
        cols = slice(c * TILE, (c + 1) * TILE)
        pre = dot(normed_two, up_ref[:, cols])
        grad_act = dot_nt(cot, down_ref[cols, :])
        square = pre * pre
        half_tanh = 0.5 + 0.5 * jnp.tanh(pre * (root + (root * 0.044715) * square))
        act = pre * half_tanh
        slope = half_tanh + act * (1.0 - half_tanh) * (
            2.0 * root + (6.0 * root * 0.044715) * square
        )
        act = act.astype(bf16)
        grad_pre = (grad_act * slope).astype(bf16)
        total_out = total_out + dot(act, down_ref[cols, :])
        back = dot_nt(grad_pre, up_ref[:, cols])
        grad_normed_two = back if grad_normed_two is None else grad_normed_two + back
        gup[:, cols] += dot(normed_two_t, grad_pre)
        gdown[cols, :] += dot_tn(act, cot)
    y_ref[...] = total_out.astype(bf16)
    gnorm_ref[0:1, :] += jnp.sum(grad_normed_two * xhat_two, axis=0, keepdims=True)
    gnorm_ref[1:2, :] += jnp.sum(grad_normed_two, axis=0, keepdims=True)
    hidden_grad = cot.astype(f32) + layer_norm_back(
        grad_normed_two, gain_two, xhat_two, inverse_two
    )
    hidden_grad_ref[...] = hidden_grad
    grad_attn = hidden_grad.astype(bf16)
    gout[...] += dot_tn(context, grad_attn)
    gcontext_s[...] = dot_nt(grad_attn, out_proj_ref[...]).astype(bf16)

    def attend_back(p, carry):
        rows = pl.ds(pl.multiple_of(p * 2 * BLOCK, 2 * BLOCK), 2 * BLOCK)
        for hp in range(head_pairs):
            cols = slice(hp * LANES, (hp + 1) * LANES)
            key_cols = slice(width + hp * LANES, width + (hp + 1) * LANES)
            value_cols = slice(2 * width + hp * LANES, 2 * width + (hp + 1) * LANES)
            queries = two_heads(qkv_ref[rows, cols])
            keys = stack_keys(qkv_ref[rows, key_cols], skv_ref[rows, cols])
            values = stack_keys(qkv_ref[rows, value_cols], skv_ref[rows, key_cols])
            gcontext = two_heads(gcontext_s[rows, cols])
            probs = probs_s[p * head_pairs + hp]
            wide = probs.astype(f32)
            grad_probs = pick_block(dot(values, gcontext.T))
            weighted = wide * grad_probs
            grad_scores = weighted - wide * jnp.sum(weighted, axis=0, keepdims=True)
            grad_scores = two_blocks((grad_scores * scale).astype(bf16))
            gq_ref[rows, cols] = pick_head(dot_tn(grad_scores, keys)).astype(bf16)
            gkeys = dot(grad_scores, queries).astype(bf16)
            gvalues = dot(two_blocks(probs), gcontext).astype(bf16)
            for grads, where in ((gkeys, cols), (gvalues, key_cols)):
                gkv_ref[rows, where] = jnp.concatenate(
                    [grads[:BLOCK], grads[2 * BLOCK : 3 * BLOCK]], axis=0
                )
                gskv_ref[rows, where] = jnp.concatenate(
                    [grads[BLOCK : 2 * BLOCK], grads[3 * BLOCK :]], axis=0
                )
        return carry

    lax.fori_loop(0, pairs, attend_back, 0)

    @pl.when(step == pl.num_programs(0) - 1)
    def _():
        gup_ref[...] = gup[...].astype(bf16)
        gdown_ref[...] = gdown[...].astype(bf16)
        gout_ref[...] = gout[...].astype(bf16)


def middle(lengths, norms, x, cot, qkv, skv, proj, up, down):
    seq, width = x.shape
    hidden_units = up.shape[1]
    tiles = seq // TILE

    def rows(columns):
        return pl.BlockSpec((TILE, columns), lambda i: (i, 0))

    def fixed(shape, index=(0, 0)):
        return pl.BlockSpec(shape, lambda i: index, pipeline_mode=pl.Buffered(1))

    return pl.pallas_call(
        middle_kernel,
        grid=(tiles,),
        out_shape=(
            jax.ShapeDtypeStruct((seq, width), bf16),
            jax.ShapeDtypeStruct((seq, width), f32),
            jax.ShapeDtypeStruct((seq, width), bf16),
            jax.ShapeDtypeStruct((seq, 2 * width), bf16),
            jax.ShapeDtypeStruct((seq, 2 * width), bf16),
            jax.ShapeDtypeStruct((width, hidden_units), bf16),
            jax.ShapeDtypeStruct((hidden_units, width), bf16),
            jax.ShapeDtypeStruct((width, width), bf16),
            jax.ShapeDtypeStruct((2, width), f32),
        ),
        in_specs=[
            pl.BlockSpec(memory_space=pltpu.SMEM),
            fixed(norms.shape),
            rows(width),
            rows(width),
            rows(3 * width),
            rows(2 * width),
            fixed((width, width), (0, 3)),
            fixed(up.shape),
            fixed(down.shape),
        ],
        out_specs=[
            rows(width),
            rows(width),
            rows(width),
            rows(2 * width),
            rows(2 * width),
            fixed((width, hidden_units)),
            fixed((hidden_units, width)),
            fixed((width, width)),
            fixed((2, width)),
        ],
        scratch_shapes=[
            pltpu.VMEM((width, hidden_units), f32),
            pltpu.VMEM((hidden_units, width), f32),
            pltpu.VMEM((width, width), f32),
            pltpu.VMEM((TILE // (2 * BLOCK) * (width // LANES), 2 * BLOCK, LANES), bf16),
            pltpu.VMEM((TILE, width), bf16),
            pltpu.VMEM((TILE, width), bf16),
        ],
        compiler_params=pltpu.CompilerParams(vmem_limit_bytes=VMEM_LIMIT),
        name="middle",
    )(lengths, norms, x, cot, qkv, skv, proj, up, down)


def back_kernel(
    norms_ref, gskv_hbm, tkv_hbm, states_ref, means_ref, proj_ref, sort_ref,
    x_hbm, normed_hbm, hidden_grad_hbm, gq_hbm, gkv_hbm,
    gx_hbm, gproj_ref, gsort_ref, gnorm_ref,
    stage, low_buf, flip_buf, gproj, gperm, gmeans, low_sem, flip_sem,
):
    seq, width = x_hbm.shape
    tiles = seq // TILE
    blocks = seq // BLOCK
    chunks = 2 * width // LANES
    per_tile = TILE // BLOCK

    def low_copy(k, slot):
        rows = pl.ds(pl.multiple_of(k * TILE, TILE), TILE)
        return pltpu.make_async_copy(gskv_hbm.at[rows, :], low_buf.at[slot], low_sem.at[slot])

    group = flip_buf.shape[0] // 2

    def flip_copy(t, slot):
        return pltpu.make_async_copy(tkv_hbm.at[t], flip_buf.at[slot], flip_sem.at[slot])

    low_copy(0, 0).start()
    low_copy(1, 1).start()
    for u in range(group):
        flip_copy(u, u).start()

    def load_step(k, carry):
        rows = pl.ds(pl.multiple_of(k * TILE, TILE), TILE)
        slot = lax.rem(k, 2)
        low_copy(k, slot).wait()
        for c in range(chunks):
            stage[c, rows, :] = low_buf[slot, :, c * LANES : (c + 1) * LANES].astype(f32)

        @pl.when(k + 2 < tiles)
        def _():
            low_copy(k + 2, slot).start()

        return carry

    lax.fori_loop(0, tiles, load_step, 0)

    final = states_ref[2 * SINK_ITERS - 1]
    permute_t = final.astype(bf16).T
    gperm[...] = jnp.zeros_like(gperm)

    def sort_step(i, carry):
        side = lax.rem(i, 2) * group

        @pl.when(i + 1 < BLOCK // group)
        def _():
            for u in range(group):
                flip_copy((i + 1) * group + u, group - side + u).start()

        for u in range(group):
            flip_copy(i * group + u, side + u).wait()
        loaded = []
        for u in range(group):
            t = i * group + u
            loaded.append(
                jnp.concatenate(
                    [stage[c, pl.ds(t, blocks, stride=BLOCK), :] for c in range(chunks)], axis=1
                ).astype(bf16)
            )
        total = gperm[...]
        for u in range(group):
            t = i * group + u
            total = total + dot(loaded[u], flip_buf[side + u])
            moved = dot(permute_t, loaded[u])
            for c in range(chunks):
                stage[c, pl.ds(t, blocks, stride=BLOCK), :] = moved[:, c * LANES : (c + 1) * LANES]
        gperm[...] = total
        return carry

    lax.fori_loop(0, BLOCK // group, sort_step, 0)

    grad = gperm[...] * final
    for sweep in reversed(range(SINK_ITERS)):
        grad = grad - states_ref[2 * sweep + 1] * jnp.sum(grad, axis=0, keepdims=True)
        grad = grad - states_ref[2 * sweep] * jnp.sum(grad, axis=1, keepdims=True)
    grad = grad.astype(bf16)
    gsort_ref[...] = dot_tn(means_ref[...], grad).astype(gsort_ref.dtype)
    gmeans[...] = dot_nt(grad, sort_ref[...]) * (1.0 / BLOCK)
    gproj[...] = jnp.zeros_like(gproj)
    gnorm_ref[...] = jnp.zeros_like(gnorm_ref)
    gain = norms_ref[0:1, :].astype(f32)

    def tile_step(x_ref, normed_ref, hidden_grad_ref, gq_ref, gkv_ref, gx_ref):
        k = pl.program_id(0)
        rows = pl.ds(pl.multiple_of(k * TILE, TILE), TILE)
        far = jnp.concatenate([stage[c, rows, :] for c in range(chunks)], axis=1)
        gkv = (gkv_ref[...].astype(f32) + far).astype(bf16)
        gq = gq_ref[...]
        normed = normed_ref[...]
        gproj[:, :width] += dot_tn(normed, gq)
        gproj[:, width:] += dot_tn(normed, gkv)
        grad_normed = dot_nt(gq, proj_ref[:, :width]) + dot_nt(gkv, proj_ref[:, width : 3 * width])
        means = gmeans[pl.ds(pl.multiple_of(k * per_tile, per_tile), per_tile), :]
        grad_normed = grad_normed + jnp.broadcast_to(
            means[:, None, :], (per_tile, BLOCK, width)
        ).reshape(TILE, width)
        xhat, inverse = center_scale(x_ref[...].astype(f32))
        gnorm_ref[0:1, :] += jnp.sum(grad_normed * xhat, axis=0, keepdims=True)
        gnorm_ref[1:2, :] += jnp.sum(grad_normed, axis=0, keepdims=True)
        gx_ref[...] = hidden_grad_ref[...] + layer_norm_back(grad_normed, gain, xhat, inverse)

    def rows_of(columns):
        return pl.BlockSpec((TILE, columns), lambda i: (i, 0))

    pltpu.emit_pipeline(
        tile_step,
        grid=(tiles,),
        in_specs=[rows_of(width)] * 4 + [rows_of(2 * width)],
        out_specs=[rows_of(width)],
    )(x_hbm, normed_hbm, hidden_grad_hbm, gq_hbm, gkv_hbm, gx_hbm)
    gproj_ref[...] = gproj[...].astype(gproj_ref.dtype)


def back(norms, gskv, tkv, states, means, proj, sort, x, normed, hidden_grad, gq, gkv):
    seq, width = x.shape
    blocks = seq // BLOCK
    hbm = pl.BlockSpec(memory_space=pl.ANY)
    vmem = pl.BlockSpec(memory_space=pltpu.VMEM)
    return pl.pallas_call(
        back_kernel,
        out_shape=(
            jax.ShapeDtypeStruct((seq, width), f32),
            jax.ShapeDtypeStruct((width, 3 * width), bf16),
            jax.ShapeDtypeStruct((width, blocks), bf16),
            jax.ShapeDtypeStruct((2, width), f32),
        ),
        in_specs=[vmem, hbm, hbm, vmem, vmem, vmem, vmem, hbm, hbm, hbm, hbm, hbm],
        out_specs=[hbm, vmem, vmem, vmem],
        scratch_shapes=[
            pltpu.VMEM((2 * width // LANES, seq, LANES), f32),
            pltpu.VMEM((2, TILE, 2 * width), bf16),
            pltpu.VMEM((4, 2 * width, blocks), bf16),
            pltpu.VMEM((width, 3 * width), f32),
            pltpu.VMEM((blocks, blocks), f32),
            pltpu.VMEM((blocks, width), f32),
            pltpu.SemaphoreType.DMA((2,)),
            pltpu.SemaphoreType.DMA((4,)),
        ],
        compiler_params=pltpu.CompilerParams(vmem_limit_bytes=VMEM_LIMIT),
        name="back",
    )(norms, gskv, tkv, states, means, proj, sort, x, normed, hidden_grad, gq, gkv)


MESH_ID = pl.DeviceIdType.MESH
AXES = ("dp", "fsdp")
SPLIT = (4, 2, 2, 2)
COPIES = 8


def coordinates():
    dp, fsdp = lax.axis_index("dp"), lax.axis_index("fsdp")
    return dp // 2, dp % 2, fsdp // 2, fsdp % 2


def device_of(z, x, y, c):
    return (z * 2 + x, y * 2 + c)


def z_others(z):
    return (z + 1 - 2 * (z % 2), (z + 2) % 4, 3 - z)


def neighbours():
    z, x, y, c = coordinates()
    others = [device_of(one, x, y, c) for one in z_others(z)]
    return others + [
        device_of(z, 1 - x, y, c), device_of(z, x, 1 - y, c), device_of(z, x, y, 1 - c)
    ]


def meet_neighbours():
    barrier = pltpu.get_barrier_semaphore()
    peers = neighbours()
    for peer in peers:
        pl.semaphore_signal(barrier, inc=1, device_id=peer, device_id_type=MESH_ID)
    pl.semaphore_wait(barrier, len(peers))


def halves(shape):
    if shape[-1] > LANES:
        middle_column = shape[-1] // 2
        return (
            (slice(None), pl.ds(0, middle_column)),
            (slice(None), pl.ds(middle_column, middle_column)),
        )
    middle_row = shape[-2] // 2
    return (
        (pl.ds(0, middle_row), slice(None)),
        (pl.ds(middle_row, middle_row), slice(None)),
    )


def remote(source, target, sems, index, device):
    send, recv = sems
    return pltpu.make_async_remote_copy(
        src_ref=source, dst_ref=target, send_sem=send.at[index], recv_sem=recv.at[index],
        device_id=device, device_id_type=MESH_ID,
    )


def gather_stages(full, sems, base):
    z, x, y, c = coordinates()
    first, second = halves(full.shape)
    every = slice(None)

    def same(index, place, device):
        part = full.at[place]
        return remote(part, part, sems, base + index, device)

    def stage_z():
        return [
            same(k, (z, x, y, c), device_of(one, x, y, c)) for k, one in enumerate(z_others(z))
        ]

    def stage_one():
        return [
            same(3, (every, x, y, c) + first, device_of(z, 1 - x, y, c)),
            same(4, (every, x, y, c) + second, device_of(z, x, 1 - y, c)),
        ]

    def stage_two():
        return [
            same(5, (every, every, y, c) + first, device_of(z, x, 1 - y, c)),
            same(6, (every, x, every, c) + second, device_of(z, 1 - x, y, c)),
        ]

    def stage_core():
        return [same(7, (every, every, every, c), device_of(z, x, y, 1 - c))]

    return [stage_z, stage_one, stage_two, stage_core]


def start_all(copies):
    for copy in copies:
        copy.start()


def wait_all(copies):
    for copy in copies:
        copy.wait()


def one_hot(shape, row_of, column_of):
    rows = lax.broadcasted_iota(jnp.int32, shape, 0)
    columns = lax.broadcasted_iota(jnp.int32, shape, 1)
    return row_of(rows, columns) == column_of(rows, columns)


def norm_place():
    z, x, y, c = coordinates()
    device = (z * 2 + x) * 4 + y * 2 + c
    return device // 8, device % 8


def gather_kernel(proj_ref, up_ref, down_ref, sort_ref, norm_ref, proj, up, down, small, send, recv):
    z, x, y, c = coordinates()
    mine = (z, x, y, c)
    proj[mine] = proj_ref[...].astype(bf16)
    up[mine] = up_ref[...].astype(bf16)
    down[mine] = down_ref[...].astype(bf16)
    quarter, eighth = norm_place()
    own = norm_ref.shape[1]
    spread = one_hot((own, LANES), lambda r, l: r + eighth * own, lambda r, l: l)
    lanes = dot(norm_ref[...].astype(bf16), spread.astype(bf16)).astype(bf16)
    lift = one_hot((16, 4), lambda r, l: r, lambda r, l: l * 4 + quarter)
    tile = dot(lift.astype(bf16), lanes).astype(bf16)
    small[mine] = jnp.concatenate([sort_ref[...].astype(bf16), tile], axis=0)
    meet_neighbours()
    fulls = (proj, up, down, small)
    plans = [gather_stages(full, (send, recv), COPIES * b) for b, full in enumerate(fulls)]
    for step in range(4):
        copies = [copy for plan in plans for copy in plan[step]()]
        start_all(copies)
        wait_all(copies)


def gather(proj, up, down, sort, norm):
    shapes = (proj.shape, up.shape, down.shape, (32, LANES))
    vmem = pl.BlockSpec(memory_space=pltpu.VMEM)
    proj, up, down, small = pl.pallas_call(
        gather_kernel,
        out_shape=tuple(jax.ShapeDtypeStruct(SPLIT + shape, bf16) for shape in shapes),
        in_specs=[vmem] * 5,
        out_specs=[vmem] * 4,
        scratch_shapes=[pltpu.SemaphoreType.DMA((4 * COPIES,))] * 2,
        compiler_params=pltpu.CompilerParams(
            collective_id=0, has_side_effects=True, vmem_limit_bytes=VMEM_LIMIT
        ),
        name="gather",
    )(proj, up, down, sort, norm)
    small = small.reshape(32, 32, LANES)
    sort = small[:, :16].reshape(-1, LANES)
    norms = jnp.sum(small[:, 16:].astype(f32), axis=0).astype(bf16).reshape(4, -1)

    def flat(array):
        return array.reshape(-1, array.shape[-1])

    return flat(proj), flat(up), flat(down), sort, norms


def add_low(*parts):
    total = parts[0].astype(f32)
    for part in parts[1:]:
        total = total + part.astype(f32)
    return total


class Reduce:
    def __init__(self, part, total, got_c, sum_c, got_a, got_b, sum_a, sum_b, got_z, sems, base):
        self.part, self.total, self.got_c, self.sum_c = part, total, got_c, sum_c
        self.got_a, self.got_b, self.sum_a, self.sum_b = got_a, got_b, sum_a, sum_b
        self.got_z, self.sems, self.base = got_z, sems, base
        self.first, self.second = halves(part.shape)

    def copies(self, step):
        z, x, y, c = coordinates()
        every = slice(None)
        to_x, to_y = device_of(z, 1 - x, y, c), device_of(z, x, 1 - y, c)

        def one(source, target, index, device):
            return remote(source, target, self.sems, self.base + index, device)

        if step == 0:
            away = self.part.at[every, every, every, 1 - c]
            return [one(away, self.got_c, 0, device_of(z, x, y, 1 - c))]
        if step == 1:
            away_a = self.sum_c.at[(every, every, 1 - y) + self.first]
            away_b = self.sum_c.at[(every, 1 - x, every) + self.second]
            return [one(away_a, self.got_a, 1, to_y), one(away_b, self.got_b, 2, to_x)]
        if step == 2:
            away_a, away_b = self.sum_a.at[every, 1 - x], self.sum_b.at[every, 1 - y]
            return [
                one(away_a, self.got_c.at[(every, 0, 0) + self.first], 3, to_x),
                one(away_b, self.got_c.at[(every, 0, 0) + self.second], 4, to_y),
            ]
        return [
            one(self.sum_c.at[other, 0, 0], self.got_z.at[k], 5 + k, device_of(other, x, y, c))
            for k, other in enumerate(z_others(z))
        ]

    def add(self, step):
        z, x, y, c = coordinates()
        if step == 3:
            self.total[...] = add_low(self.sum_c[z, 0, 0], *[self.got_z[k] for k in range(3)])
            return

        def line(i, carry):
            if step == 0:
                for j in range(2):
                    for k in range(2):
                        self.sum_c[i, j, k] = add_low(
                            self.part[i, j, k, c], self.got_c[i, j, k]
                        ).astype(bf16)
            elif step == 1:
                for j in range(2):
                    self.sum_a[i, j] = add_low(
                        self.sum_c[(i, j, y) + self.first], self.got_a[i, j]
                    ).astype(bf16)
                    self.sum_b[i, j] = add_low(
                        self.sum_c[(i, x, j) + self.second], self.got_b[i, j]
                    ).astype(bf16)
            else:
                self.sum_c[(i, 0, 0) + self.first] = add_low(
                    self.sum_a[i, x], self.got_c[(i, 0, 0) + self.first]
                ).astype(bf16)
                self.sum_c[(i, 0, 0) + self.second] = add_low(
                    self.sum_b[i, y], self.got_c[(i, 0, 0) + self.second]
                ).astype(bf16)
            return carry

        lax.fori_loop(0, 4, line, 0)


def reduce_scratch(rows, columns):
    half = (rows, columns // 2) if columns > LANES else (rows // 2, columns)
    shapes = (
        (4, 2, 2, rows, columns), (4, 2, 2, rows, columns), (4, 2) + half, (4, 2) + half,
        (4, 2) + half, (4, 2) + half, (3, rows, columns),
    )
    return [pltpu.VMEM(shape, bf16) for shape in shapes]


def norm_rows(grads):
    rows = []
    for grad in grads:
        for i in range(grad.shape[0]):
            for q in range(grad.shape[1] // LANES):
                rows.append(grad[i : i + 1, q * LANES : (q + 1) * LANES])
    return jnp.concatenate(rows, axis=0)


def reduce_kernel(
    gqkv_ref, gout_ref, gup_ref, gdown_ref, gsort_ref, gone_ref, gtwo_ref,
    qkv_sum, out_sum, up_sum, down_sum, sort_sum, norm_sum,
    small, small_sum, send, recv, *scratch,
):
    tile = norm_rows((gone_ref[...], gtwo_ref[...])).astype(bf16)
    for i in range(4):
        for j in range(2):
            for k in range(2):
                for m in range(2):
                    small[i, j, k, m, :16] = gsort_ref[i, j, k, m]
                    small[i, j, k, m, 16:] = tile
    meet_neighbours()
    parts = (gqkv_ref, gout_ref, gup_ref, gdown_ref, small)
    totals = (qkv_sum, out_sum, up_sum, down_sum, small_sum)
    plans = [
        Reduce(part, total, *scratch[7 * b : 7 * b + 7], (send, recv), COPIES * b)
        for b, (part, total) in enumerate(zip(parts, totals))
    ]
    for step in range(4):
        copies = [plan.copies(step) for plan in plans]
        for one in copies:
            start_all(one)
        for one, plan in zip(copies, plans):
            wait_all(one)
            plan.add(step)
    sort_sum[...] = small_sum[:16, :]
    quarter, eighth = norm_place()
    own = norm_sum.shape[1]
    drop = one_hot((4, 16), lambda r, l: r * 4 + quarter, lambda r, l: l).astype(f32)
    pick = one_hot((LANES, own), lambda r, l: r, lambda r, l: l + eighth * own).astype(f32)

    def exact(left, right):
        return lax.dot_general(
            left, right, (((1,), (0,)), ((), ())),
            precision=lax.Precision.HIGHEST, preferred_element_type=f32,
        )

    norm_sum[...] = exact(exact(drop, small_sum[16:, :]), pick)


def reduce(gqkv, gout, gup, gdown, gsort, gone, gtwo):
    devices = 32

    def split(grad):
        return grad.reshape(SPLIT + (grad.shape[0] // devices, grad.shape[1]))

    parts = tuple(split(grad) for grad in (gqkv, gout, gup, gdown, gsort))
    shapes = [part.shape[-2:] for part in parts]
    vmem = pl.BlockSpec(memory_space=pltpu.VMEM)
    small = (32, LANES)
    scratch = [pltpu.VMEM(SPLIT + small, bf16), pltpu.VMEM(small, f32)]
    scratch += [pltpu.SemaphoreType.DMA((5 * COPIES,))] * 2
    for shape in shapes[:4] + [small]:
        scratch += reduce_scratch(*shape)
    qkv, out, up, down, sort, norm = pl.pallas_call(
        reduce_kernel,
        out_shape=tuple(
            jax.ShapeDtypeStruct(shape, f32) for shape in shapes + [(4, gone.shape[1] // devices)]
        ),
        in_specs=[vmem] * 7,
        out_specs=[vmem] * 6,
        scratch_shapes=scratch,
        compiler_params=pltpu.CompilerParams(
            collective_id=1, has_side_effects=True, vmem_limit_bytes=VMEM_LIMIT
        ),
        name="reduce",
    )(*parts, gone, gtwo)
    return jnp.concatenate([qkv, out], axis=1), up, down, sort, norm


def adamw(master, first, second, grad, rate, decay):
    first_new = beta_first * first + (1.0 - beta_first) * grad
    second_new = beta_second * second + (1.0 - beta_second) * grad * grad
    first_hat = first_new / (1.0 - beta_first**STEP)
    second_hat = second_new / (1.0 - beta_second**STEP)
    master_new = master - rate * (first_hat / (jnp.sqrt(second_hat) + adam_eps) + decay * master)
    return (master_new, first_new, second_new)


RATES = (
    (rate_matrix, weight_decay), (rate_matrix, weight_decay), (rate_matrix, weight_decay),
    (rate_other, weight_decay), (rate_other, 0.0),
)


def update_kernel(*refs):
    sums, states, results = refs[:5], refs[5:20], refs[20:]
    for b, (rate, decay) in enumerate(RATES):
        state = [ref[...] for ref in states[3 * b : 3 * b + 3]]
        for ref, value in zip(
            results[3 * b : 3 * b + 3], adamw(*state, sums[b][...], rate, decay)
        ):
            ref[...] = value


def update(sums, states):
    vmem = pl.BlockSpec(memory_space=pltpu.VMEM)
    return pl.pallas_call(
        update_kernel,
        out_shape=tuple(jax.ShapeDtypeStruct(state.shape, f32) for state in states),
        in_specs=[vmem] * 20,
        out_specs=[vmem] * 15,
        compiler_params=pltpu.CompilerParams(vmem_limit_bytes=VMEM_LIMIT),
        name="update",
    )(*sums, *states)


def gather_plain(proj, up, down, sort, norm):
    def gathered(shard, axis):
        return lax.all_gather(shard.astype(bf16), AXES, axis=axis, tiled=True)

    return (*(gathered(shard, 0) for shard in (proj, up, down, sort)), gathered(norm, 1))


def reduce_plain(gqkv, gout, gup, gdown, gsort, gone, gtwo):
    def summed(grad, axis):
        return lax.psum_scatter(
            grad.astype(f32), AXES, scatter_dimension=axis, tiled=True
        )

    gproj = jnp.concatenate([gqkv, gout], axis=1)
    gnorm = jnp.concatenate([gone, gtwo], axis=0)
    return (*(summed(grad, 0) for grad in (gproj, gup, gdown, gsort)), summed(gnorm, 1))


def body(
    near, layer_input, doc_lengths, out_cotangent, *states,
):
    x = layer_input[0]
    cot = out_cotangent[0]
    proj, up, down, sort, norms = (gather if near else gather_plain)(*states[::3])
    normed, qkv, skv, tkv, means, kept = front(doc_lengths, norms, x, proj, sort)
    y, hidden_grad, gq, gkv, gskv, gup, gdown, gout, gnorm_two = middle(
        doc_lengths, norms, x, cot, qkv, skv, proj, up, down
    )
    gx, gqkv, gsort, gnorm_one = back(
        norms, gskv, tkv, kept, means, proj, sort, x, normed, hidden_grad, gq, gkv
    )
    sums = (reduce if near else reduce_plain)(gqkv, gout, gup, gdown, gsort, gnorm_one, gnorm_two)
    return (y[None], gx[None], *update(sums, states))


def solution(mesh):
    rows3, rows2, columns = P(AXES, None, None), P(AXES, None), P(None, AXES)
    near = (mesh.shape["dp"], mesh.shape["fsdp"]) == (8, 4)
    return jax.shard_map(
        functools.partial(body, near),
        mesh=mesh,
        in_specs=(rows3, rows2, rows3) + (rows2,) * 12 + (columns,) * 3,
        out_specs=(rows3, rows3) + (rows2,) * 12 + (columns,) * 3,
        check_vma=False,
    )
```

time: 1760 us -> 494 us (0.28)
  waiting for transfers between devices: 637 us -> 0 us
  Pallas kernels: 0 us -> 489 us
  matrix products: 401 us -> 0 us
  local copies, waits for them, and re-layouts: 365 us -> 0.6 us
  other arithmetic: 246 us -> 3.22 us
  blocking collectives: 80.3 us -> 0 us
    reduce_scatter x4 -> x0, waiting for transfers between devices: 544 us -> none  [the longest x1 139 us: body(): lax.psum_scatter(grad_down, ('dp', 'fsdp'), scatter_dimension=0, tiled=True)]
    pallas_call x0 -> x6, Pallas kernels: none -> 489 us  [the longest x1 230 us: middle(): pl.pallas_call(middle_kernel, grid=(tiles,), out_shape=(jax.ShapeDtypeStr...]
    dot_general x29 -> x0, matrix products: 383 us -> none  [the longest x5 69.7 us: matmul_back(): jnp.einsum('...n,kn->...k', grad, right, preferred_element_type=jnp.float32)]
    reduce_sum x44 -> x0, other arithmetic: 137 us -> none  [the longest x1 37.1 us: softmax_rows(): highest = jnp.max(scores, axis=-1, keepdims=True)]
    convert_element_type x8 -> x0, local copies, waits for them, and re-layouts: 121 us -> none  [the longest x2 67.7 us: attn_backward(): grad_projected_low = jnp.stack([grad_queries, grad_keys, grad_values], ax...]
    another operation x6 -> x0, local copies, waits for them, and re-layouts: 81.9 us -> none
    all_gather x2 -> x0, blocking collectives: 80.3 us -> none  [the longest x1 43.3 us: body(): lax.all_gather(shard_low[4], ('dp', 'fsdp'), axis=1, tiled=True)]
    dot_general x5 -> x0, local copies, waits for them, and re-layouts: 67.8 us -> none  [the longest x1 15 us: attn_backward(): jnp.einsum('rnhts,rnshe->rnthe', grad_far, sorted_keys, preferred_element...]
  transfers between devices with their start and end apart: 8 -> 0, of which waited for: 6 -> 0; matrix products, arithmetic and copies ran while one was open for 25% -> 0% of each run, Pallas kernels for 0% -> 0%
where the time goes in v1:
time: 494 us
  Pallas kernels  489 us (99%)
    pallas_call x1, Pallas kernels, middle(): pl.pallas_call(middle_kernel, grid=(tiles,), out_shape=(jax.ShapeDtypeStr...  230 us
    pallas_call x1, Pallas kernels, back(): pl.pallas_call(back_kernel, out_shape=(jax.ShapeDtypeStruct((seq, width),...  68.4 us
    pallas_call x1, Pallas kernels, front(): pl.pallas_call(front_kernel, out_shape=(jax.ShapeDtypeStruct((seq, width)...  65.4 us
    pallas_call x1, Pallas kernels, gather(): pl.pallas_call(gather_kernel, out_shape=tuple((jax.ShapeDtypeStruct(SPLIT...  61.7 us
    pallas_call x1, Pallas kernels, reduce(): pl.pallas_call(reduce_kernel, out_shape=tuple((jax.ShapeDtypeStruct(shape...  60.9 us

profile of v1, /device:TPU:0, one launch (start us, length us, event | category | flops | bytes accessed | tf_op | source)
XLA Modules:
  0.0 494.1 jit_solution(13380749395599102188)
XLA Ops:
  0.7 61.7 %gather.1 = (bf16[4,2,2,2,16,2048]{5,4,3,2,1,0:T(8,128)(2,1)}, bf16[4,2,2,2,16,2048]{5,4,3,2,1,0:T(8,128)(2,1)}, bf16[4,2,2,2,64,512]{5,4,3,2,1,0:T(8,128)(2,1)}, bf16[4,2,2,2,32,128]{5,4,3,2,1,0:T(8,128)(2,1)}) custom-call(f32[16,2048]{1,0:T(8,128)} %refs_5_.1, f32[16,2048]{1,0:T(8,128)} %refs_8_.1, f32[64,512]{1,0:T(8,128)} %refs_11_.1, ...), custom_call_target="tpu_custom_call" | custom-call | tf_op jit(solution)/shard_map/gather/pallas_call | solution.py:728
  62.4 1.6 fusion
  64.0 0.6 reshape.68.norms_ref
  64.6 65.4 %front.1 = (bf16[4096,512]{1,0:T(8,128)(2,1)}, bf16[4096,1536]{1,0:T(8,128)(2,1)}, bf16[4096,1024]{1,0:T(8,128)(2,1)}, bf16[32,1024,128]{2,1,0:T(8,128)(2,1)}, b...) custom-call(s32[1,8]{1,0:T(1,128)} %lengths_ref.3, bf16[4,512]{1,0:T(4,128)(2,1)} %reshape.68.norms_ref, ...), custom_call_target="tpu_custom_call" | custom-call | tf_op jit(solution)/shard_map/front/pallas_call | solution.py:199
  130.1 230.3 %middle.1 = (bf16[4096,512]{1,0:T(8,128)(2,1)}, f32[4096,512]{1,0:T(8,128)}, bf16[4096,512]{1,0:T(8,128)(2,1)}, bf16[4096,1024]{1,0:T(8,128)(2,1)}, bf16[4096,10...) custom-call(s32[1,8]{1,0:T(1,128)} %lengths_ref.3, ...), custom_call_target="tpu_custom_call" | custom-call | tf_op jit(solution)/shard_map/middle/pallas_call | solution.py:396
  360.4 68.4 %back.1 = (f32[4096,512]{1,0:T(8,128)}, bf16[512,1536]{1,0:T(8,128)(2,1)}, bf16[512,128]{1,0:T(8,128)(2,1)}, f32[2,512]{1,0:T(2,128)}) custom-call(bf16[4,512]{1,0:T(4,128)(2,1)} %reshape.68.norms_ref, bf16[4096,1024]{1,0:T(8,128)(2,1)} %get-tuple-element.68.gskv_hbm, bf16[32,1024,128]{2,1,0:T(8,128)(2,1)} %get-tuple-element.69.tkv_hbm, ...), custom_call_target="tpu_custom_call" | custom-call | tf_op jit(solution)/shard_map/back/pallas_call | solution.py:567
  428.8 60.9 %reduce.2 = (f32[16,1536]{1,0:T(8,128)}, f32[16,512]{1,0:T(8,128)}, f32[16,2048]{1,0:T(8,128)}, f32[64,512]{1,0:T(8,128)}, f32[16,128]{1,0:T(8,128)}, /*index=5*/f32[4,16]{1,0:T(4,128)}) custom-call(bf16[4,2,2,2,16,1536]{5,4,3,2,1,0:T(8,128)(2,1)} %bitcast.25, bf16[4,2,2,2,16,512]{5,4,3,2,1,0:T(8,128)(2,1)} %bitcast.28, ...), custom_call_target="tpu_custom_call" | custom-call | tf_op jit(solution)/shard_map/reduce/pallas_call | solution.py:895
  489.7 1.6 pad_maximum_fusion.refs_0_
  491.3 2.6 update.1

commit v2 on v1

--- a/solution.py
+++ b/solution.py
@@ -68,10 +68,37 @@
     return top + jnp.log(jnp.sum(jnp.exp(logits - top), axis=axis, keepdims=True))
 
 
+GROUP = 8 * BLOCK
+
+
+def regroup_matrix(inverse):
+    rows = lax.broadcasted_iota(jnp.int32, (GROUP, GROUP), 1 if inverse else 0)
+    columns = lax.broadcasted_iota(jnp.int32, (GROUP, GROUP), 0 if inverse else 1)
+    hit = (rows // 8 == columns % BLOCK) & (rows % 8 == columns // BLOCK)
+    return hit.astype(f32).astype(bf16)
+
+
+def spread_tokens(stage, matrix, k, part):
+    columns = part.shape[1]
+    for g in range(part.shape[0] // GROUP):
+        place = pl.multiple_of((k * (part.shape[0] // GROUP) + g) * 8, 8)
+        moved = dot(matrix, part[g * GROUP : (g + 1) * GROUP])
+        stage[:, pl.ds(place, 8), :] = moved.reshape(BLOCK, 8, columns)
+
+
+def collect_tokens(stage, matrix, k, rows):
+    parts = []
+    for g in range(rows // GROUP):
+        place = pl.multiple_of((k * (rows // GROUP) + g) * 8, 8)
+        part = stage[:, pl.ds(place, 8), :].reshape(GROUP, stage.shape[2]).astype(bf16)
+        parts.append(dot(matrix, part))
+    return jnp.concatenate(parts, axis=0)
+
+
 def front_kernel(
     lengths_ref, norms_ref, x_ref, proj_ref, sort_ref,
     normed_hbm, qkv_hbm, skv_hbm, tkv_hbm, means_ref, states_ref,
-    normed_s, stage, qkv_buf, low_buf, flip_buf, copy_sem, qkv_sem, low_sem, flip_sem,
+    normed_s, stage, matrix, qkv_buf, low_buf, flip_buf, copy_sem, qkv_sem, low_sem, flip_sem,
 ):
     seq, width = x_ref.shape
     tiles = seq // TILE
@@ -120,17 +147,14 @@
         states_ref[2 * k + 1] = jnp.exp(logits)
         normed = normed_s[rows, :]
         qkv_buf[slot, :, :width] = dot(normed, proj_ref[:, :width]).astype(bf16)
-        for half in range(2):
-            columns = slice((1 + half) * width, (2 + half) * width)
-            product = dot(normed, proj_ref[:, columns]).astype(bf16)
-            qkv_buf[slot, :, columns] = product
-            wide = product.astype(f32)
-            for c in range(width // LANES):
-                stage[half * (width // LANES) + c, rows, :] = wide[:, c * LANES : (c + 1) * LANES]
+        product = dot(normed, proj_ref[:, width : 3 * width]).astype(bf16)
+        qkv_buf[slot, :, width:] = product
+        spread_tokens(stage, matrix[...], k, product)
         qkv_copy(k, slot).start()
         return logits
 
     assert tiles == SINK_ITERS
+    matrix[...] = regroup_matrix(False)
     lax.fori_loop(0, tiles, project_step, logits)
     permute = states_ref[2 * SINK_ITERS - 1].astype(bf16)
 
@@ -148,18 +172,12 @@
         loaded = []
         for u in range(group):
             t = i * group + u
-            loaded.append(
-                jnp.concatenate(
-                    [stage[c, pl.ds(t, blocks, stride=BLOCK), :] for c in range(chunks)], axis=1
-                ).astype(bf16)
-            )
+            loaded.append(stage[t].astype(bf16))
         for u in range(group):
             t = i * group + u
-            flip_buf[u] = loaded[u].T
+            flip_buf[u] = loaded[u].astype(f32).T.astype(bf16)
             flip_copy(t, u).start()
-            moved = dot(permute, loaded[u])
-            for c in range(chunks):
-                stage[c, pl.ds(t, blocks, stride=BLOCK), :] = moved[:, c * LANES : (c + 1) * LANES]
+            stage[t] = dot(permute, loaded[u])
         return carry
 
     group = flip_buf.shape[0]
@@ -177,11 +195,11 @@
         def _():
             low_copy(k - 2, slot).wait()
 
-        for c in range(chunks):
-            low_buf[slot, :, c * LANES : (c + 1) * LANES] = stage[c, rows, :].astype(bf16)
+        low_buf[slot] = collect_tokens(stage, matrix[...], k, TILE).astype(bf16)
         low_copy(k, slot).start()
         return carry
 
+    matrix[...] = regroup_matrix(True)
     lax.fori_loop(0, tiles, low_step, 0)
     for u in range(group):
         flip_copy(BLOCK - group + u, u).wait()
@@ -210,14 +228,15 @@
         out_specs=[hbm, hbm, hbm, hbm, vmem, vmem],
         scratch_shapes=[
             pltpu.VMEM((seq, width), bf16),
-            pltpu.VMEM((2 * width // LANES, seq, LANES), f32),
+            pltpu.VMEM((BLOCK, blocks, 2 * width), f32),
+            pltpu.VMEM((GROUP, GROUP), bf16),
             pltpu.VMEM((2, TILE, 3 * width), bf16),
             pltpu.VMEM((2, TILE, 2 * width), bf16),
-            pltpu.VMEM((2, 2 * width, blocks), bf16),
+            pltpu.VMEM((4, 2 * width, blocks), bf16),
             pltpu.SemaphoreType.DMA,
             pltpu.SemaphoreType.DMA((2,)),
             pltpu.SemaphoreType.DMA((2,)),
-            pltpu.SemaphoreType.DMA((2,)),
+            pltpu.SemaphoreType.DMA((8,)),
         ],
         compiler_params=pltpu.CompilerParams(vmem_limit_bytes=VMEM_LIMIT),
         name="front",
@@ -234,7 +253,7 @@
 def middle_kernel(
     lengths_ref, norms_ref, x_ref, cot_ref, qkv_ref, skv_ref, out_proj_ref, up_ref, down_ref,
     y_ref, hidden_grad_ref, gq_ref, gkv_ref, gskv_ref, gup_ref, gdown_ref, gout_ref, gnorm_ref,
-    gup, gdown, gout, probs_s, context_s, gcontext_s,
+    gup, gdown, gout, probs_s, context_s, gcontext_s, gq_s, gkv_s, gskv_s, grads_s,
 ):
     step = pl.program_id(0)
     tile, width = x_ref.shape
@@ -254,16 +273,19 @@
     lane = lax.broadcasted_iota(jnp.int32, (1, LANES), 1)
     low_head = lane < HD
     low_block = lax.rem(lane, 2 * BLOCK) < BLOCK
-    zero = jnp.zeros((), bf16)
+    head_one = low_head.astype(f32).astype(bf16)
+    head_two = (1.0 - low_head.astype(f32)).astype(bf16)
+    block_one = low_block.astype(f32).astype(bf16)
+    block_two = (1.0 - low_block.astype(f32)).astype(bf16)
 
     def two_heads(part):
         return jnp.concatenate(
-            [jnp.where(low_head, part, zero), jnp.where(low_head, zero, part)], axis=0
+            [part * head_one, part * head_two], axis=0
         )
 
     def two_blocks(part):
         return jnp.concatenate(
-            [jnp.where(low_block, part, zero), jnp.where(low_block, zero, part)], axis=0
+            [part * block_one, part * block_two], axis=0
         )
 
     def stack_keys(own, far):
@@ -294,7 +316,7 @@
             queries = two_heads(qkv_ref[rows, cols])
             keys = stack_keys(qkv_ref[rows, key_cols], skv_ref[rows, cols])
             values = stack_keys(qkv_ref[rows, value_cols], skv_ref[rows, key_cols])
-            scores = pick_block(dot(keys, queries.T)) * scale
+            scores = pick_block(dot(keys, queries.astype(f32).T.astype(bf16))) * scale
             scores = jnp.concatenate(
                 [jnp.where(same, scores[:BLOCK], score_floor), scores[BLOCK:]], axis=0
             )
@@ -304,7 +326,7 @@
             context_s[rows, cols] = pick_head(dot_tn(two_blocks(probs), values)).astype(bf16)
         return carry
 
-    lax.fori_loop(0, pairs, attend, 0)
+    lax.fori_loop(0, pairs, attend, 0, unroll=8)
 
     inputs = x_ref[...].astype(f32)
     context = context_s[...]
@@ -351,29 +373,41 @@
             cols = slice(hp * LANES, (hp + 1) * LANES)
             key_cols = slice(width + hp * LANES, width + (hp + 1) * LANES)
             value_cols = slice(2 * width + hp * LANES, 2 * width + (hp + 1) * LANES)
-            queries = two_heads(qkv_ref[rows, cols])
-            keys = stack_keys(qkv_ref[rows, key_cols], skv_ref[rows, cols])
             values = stack_keys(qkv_ref[rows, value_cols], skv_ref[rows, key_cols])
             gcontext = two_heads(gcontext_s[rows, cols])
-            probs = probs_s[p * head_pairs + hp]
-            wide = probs.astype(f32)
-            grad_probs = pick_block(dot(values, gcontext.T))
+            wide = probs_s[p * head_pairs + hp].astype(f32)
+            grad_probs = pick_block(dot(values, gcontext.astype(f32).T.astype(bf16)))
             weighted = wide * grad_probs
             grad_scores = weighted - wide * jnp.sum(weighted, axis=0, keepdims=True)
-            grad_scores = two_blocks((grad_scores * scale).astype(bf16))
-            gq_ref[rows, cols] = pick_head(dot_tn(grad_scores, keys)).astype(bf16)
-            gkeys = dot(grad_scores, queries).astype(bf16)
-            gvalues = dot(two_blocks(probs), gcontext).astype(bf16)
+            grad_scores = (grad_scores * scale).astype(bf16)
+            grads_s[p * head_pairs + hp] = grad_scores
+        return carry
+
+    lax.fori_loop(0, pairs, attend_back, 0, unroll=8)
+
+    def attend_last(p, carry):
+        rows = pl.ds(pl.multiple_of(p * 2 * BLOCK, 2 * BLOCK), 2 * BLOCK)
+        for hp in range(head_pairs):
+            cols = slice(hp * LANES, (hp + 1) * LANES)
+            key_cols = slice(width + hp * LANES, width + (hp + 1) * LANES)
+            value_cols = slice(2 * width + hp * LANES, 2 * width + (hp + 1) * LANES)
+            keys = stack_keys(qkv_ref[rows, key_cols], skv_ref[rows, cols])
+            gq_s[rows, cols] = pick_head(dot_tn(two_blocks(grads_s[p * head_pairs + hp]), keys)).astype(bf16)
+            gkeys = dot(two_blocks(grads_s[p * head_pairs + hp]), two_heads(qkv_ref[rows, cols])).astype(bf16)
+            gvalues = dot(two_blocks(probs_s[p * head_pairs + hp]), two_heads(gcontext_s[rows, cols])).astype(bf16)
             for grads, where in ((gkeys, cols), (gvalues, key_cols)):
-                gkv_ref[rows, where] = jnp.concatenate(
+                gkv_s[rows, where] = jnp.concatenate(
                     [grads[:BLOCK], grads[2 * BLOCK : 3 * BLOCK]], axis=0
                 )
-                gskv_ref[rows, where] = jnp.concatenate(
+                gskv_s[rows, where] = jnp.concatenate(
                     [grads[BLOCK : 2 * BLOCK], grads[3 * BLOCK :]], axis=0
                 )
         return carry
 
-    lax.fori_loop(0, pairs, attend_back, 0)
+    lax.fori_loop(0, pairs, attend_last, 0, unroll=8)
+    gq_ref[...] = gq_s[...]
+    gkv_ref[...] = gkv_s[...]
+    gskv_ref[...] = gskv_s[...]
 
     @pl.when(step == pl.num_programs(0) - 1)
     def _():
@@ -435,7 +469,8 @@
             pltpu.VMEM((width, width), f32),
             pltpu.VMEM((TILE // (2 * BLOCK) * (width // LANES), 2 * BLOCK, LANES), bf16),
             pltpu.VMEM((TILE, width), bf16),
-            pltpu.VMEM((TILE, width), bf16),
+            pltpu.VMEM((TILE, width), bf16),pltpu.VMEM((TILE, width), bf16),pltpu.VMEM((TILE, 2*width), bf16),pltpu.VMEM((TILE, 2*width), bf16),
+            pltpu.VMEM((TILE // (2 * BLOCK) * (width // LANES), 2 * BLOCK, LANES), bf16),
         ],
         compiler_params=pltpu.CompilerParams(vmem_limit_bytes=VMEM_LIMIT),
         name="middle",
@@ -446,7 +481,7 @@
     norms_ref, gskv_hbm, tkv_hbm, states_ref, means_ref, proj_ref, sort_ref,
     x_hbm, normed_hbm, hidden_grad_hbm, gq_hbm, gkv_hbm,
     gx_hbm, gproj_ref, gsort_ref, gnorm_ref,
-    stage, low_buf, flip_buf, gproj, gperm, gmeans, low_sem, flip_sem,
+    stage, matrix, low_buf, flip_buf, gproj, gperm, gmeans, low_sem, flip_sem,
 ):
     seq, width = x_hbm.shape
     tiles = seq // TILE
@@ -472,8 +507,7 @@
         rows = pl.ds(pl.multiple_of(k * TILE, TILE), TILE)
         slot = lax.rem(k, 2)
         low_copy(k, slot).wait()
-        for c in range(chunks):
-            stage[c, rows, :] = low_buf[slot, :, c * LANES : (c + 1) * LANES].astype(f32)
+        spread_tokens(stage, matrix[...], k, low_buf[slot])
 
         @pl.when(k + 2 < tiles)
         def _():
@@ -481,10 +515,12 @@
 
         return carry
 
+    matrix[...] = regroup_matrix(False)
     lax.fori_loop(0, tiles, load_step, 0)
+    matrix[...] = regroup_matrix(True)
 
     final = states_ref[2 * SINK_ITERS - 1]
-    permute_t = final.astype(bf16).T
+    permute_t = final.T.astype(bf16)
     gperm[...] = jnp.zeros_like(gperm)
 
     def sort_step(i, carry):
@@ -500,18 +536,12 @@
         loaded = []
         for u in range(group):
             t = i * group + u
-            loaded.append(
-                jnp.concatenate(
-                    [stage[c, pl.ds(t, blocks, stride=BLOCK), :] for c in range(chunks)], axis=1
-                ).astype(bf16)
-            )
+            loaded.append(stage[t].astype(bf16))
         total = gperm[...]
         for u in range(group):
             t = i * group + u
             total = total + dot(loaded[u], flip_buf[side + u])
-            moved = dot(permute_t, loaded[u])
-            for c in range(chunks):
-                stage[c, pl.ds(t, blocks, stride=BLOCK), :] = moved[:, c * LANES : (c + 1) * LANES]
+            stage[t] = dot(permute_t, loaded[u])
         gperm[...] = total
         return carry
 
@@ -531,7 +561,7 @@
     def tile_step(x_ref, normed_ref, hidden_grad_ref, gq_ref, gkv_ref, gx_ref):
         k = pl.program_id(0)
         rows = pl.ds(pl.multiple_of(k * TILE, TILE), TILE)
-        far = jnp.concatenate([stage[c, rows, :] for c in range(chunks)], axis=1)
+        far = collect_tokens(stage, matrix[...], k, TILE)
         gkv = (gkv_ref[...].astype(f32) + far).astype(bf16)
         gq = gq_ref[...]
         normed = normed_ref[...]
@@ -575,14 +605,15 @@
         in_specs=[vmem, hbm, hbm, vmem, vmem, vmem, vmem, hbm, hbm, hbm, hbm, hbm],
         out_specs=[hbm, vmem, vmem, vmem],
         scratch_shapes=[
-            pltpu.VMEM((2 * width // LANES, seq, LANES), f32),
+            pltpu.VMEM((BLOCK, blocks, 2 * width), f32),
+            pltpu.VMEM((GROUP, GROUP), bf16),
             pltpu.VMEM((2, TILE, 2 * width), bf16),
-            pltpu.VMEM((4, 2 * width, blocks), bf16),
+            pltpu.VMEM((8, 2 * width, blocks), bf16),
             pltpu.VMEM((width, 3 * width), f32),
             pltpu.VMEM((blocks, blocks), f32),
             pltpu.VMEM((blocks, width), f32),
             pltpu.SemaphoreType.DMA((2,)),
-            pltpu.SemaphoreType.DMA((4,)),
+            pltpu.SemaphoreType.DMA((8,)),
         ],
         compiler_params=pltpu.CompilerParams(vmem_limit_bytes=VMEM_LIMIT),
         name="back",

time: 494 us -> 314 us (0.64)
  Pallas kernels: 489 us -> 309 us
    pallas_call x1, Pallas kernels: 230 us -> 107 us  [middle(): pl.pallas_call(middle_kernel, grid=(tiles,), out_shape=(jax.ShapeDtypeStr...]
    pallas_call x1, Pallas kernels: 65.4 us -> 33.9 us  [front(): pl.pallas_call(front_kernel, out_shape=(jax.ShapeDtypeStruct((seq, width)...]
    pallas_call x1, Pallas kernels: 68.4 us -> 42.6 us  [back(): pl.pallas_call(back_kernel, out_shape=(jax.ShapeDtypeStruct((seq, width),...]
where the time goes in v2:
time: 314 us; the launch traced here: 313 us
  Pallas kernels  309 us (98%)
  other arithmetic  3.22 us (1%)
    pallas_call x1, Pallas kernels, middle(): pl.pallas_call(middle_kernel, grid=(tiles,), out_shape=(jax.ShapeDtypeStr...  107 us
    pallas_call x1, Pallas kernels, gather(): pl.pallas_call(gather_kernel, out_shape=tuple((jax.ShapeDtypeStruct(SPLIT...  61.7 us
    pallas_call x1, Pallas kernels, reduce(): pl.pallas_call(reduce_kernel, out_shape=tuple((jax.ShapeDtypeStruct(shape...  60.9 us
    pallas_call x1, Pallas kernels, back(): pl.pallas_call(back_kernel, out_shape=(jax.ShapeDtypeStruct((seq, width),...  42.6 us
    pallas_call x1, Pallas kernels, front(): pl.pallas_call(front_kernel, out_shape=(jax.ShapeDtypeStruct((seq, width)...  33.9 us

profile of v2, /device:TPU:0, one launch (start us, length us, event | category | flops | bytes accessed | tf_op | source)
XLA Modules:
  0.0 313.3 jit_solution(962719403647135572)
XLA Ops:
  0.7 61.7 %gather.1 = (bf16[4,2,2,2,16,2048]{5,4,3,2,1,0:T(8,128)(2,1)}, bf16[4,2,2,2,16,2048]{5,4,3,2,1,0:T(8,128)(2,1)}, bf16[4,2,2,2,64,512]{5,4,3,2,1,0:T(8,128)(2,1)}, bf16[4,2,2,2,32,128]{5,4,3,2,1,0:T(8,128)(2,1)}) custom-call(f32[16,2048]{1,0:T(8,128)} %refs_5_.1, f32[16,2048]{1,0:T(8,128)} %refs_8_.1, f32[64,512]{1,0:T(8,128)} %refs_11_.1, ...), custom_call_target="tpu_custom_call" | custom-call | tf_op jit(solution)/shard_map/gather/pallas_call | solution.py:759
  62.4 1.6 fusion
  64.0 0.6 reshape.68.norms_ref
  64.6 33.9 %front.1 = (bf16[4096,512]{1,0:T(8,128)(2,1)}, bf16[4096,1536]{1,0:T(8,128)(2,1)}, bf16[4096,1024]{1,0:T(8,128)(2,1)}, bf16[32,1024,128]{2,1,0:T(8,128)(2,1)}, b...) custom-call(s32[1,8]{1,0:T(1,128)} %lengths_ref.3, bf16[4,512]{1,0:T(4,128)(2,1)} %reshape.68.norms_ref, ...), custom_call_target="tpu_custom_call" | custom-call | tf_op jit(solution)/shard_map/front/pallas_call | solution.py:217
  98.5 106.9 %middle.1 = (bf16[4096,512]{1,0:T(8,128)(2,1)}, f32[4096,512]{1,0:T(8,128)}, bf16[4096,512]{1,0:T(8,128)(2,1)}, bf16[4096,1024]{1,0:T(8,128)(2,1)}, bf16[4096,10...) custom-call(s32[1,8]{1,0:T(1,128)} %lengths_ref.3, ...), custom_call_target="tpu_custom_call" | custom-call | tf_op jit(solution)/shard_map/middle/pallas_call | solution.py:430
  205.4 42.6 %back.1 = (f32[4096,512]{1,0:T(8,128)}, bf16[512,1536]{1,0:T(8,128)(2,1)}, bf16[512,128]{1,0:T(8,128)(2,1)}, f32[2,512]{1,0:T(2,128)}) custom-call(bf16[4,512]{1,0:T(4,128)(2,1)} %reshape.68.norms_ref, bf16[4096,1024]{1,0:T(8,128)(2,1)} %get-tuple-element.68.gskv_hbm, bf16[32,1024,128]{2,1,0:T(8,128)(2,1)} %get-tuple-element.69.tkv_hbm, ...), custom_call_target="tpu_custom_call" | custom-call | tf_op jit(solution)/shard_map/back/pallas_call | solution.py:597
  248.0 60.9 %reduce.2 = (f32[16,1536]{1,0:T(8,128)}, f32[16,512]{1,0:T(8,128)}, f32[16,2048]{1,0:T(8,128)}, f32[64,512]{1,0:T(8,128)}, f32[16,128]{1,0:T(8,128)}, /*index=5*/f32[4,16]{1,0:T(4,128)}) custom-call(bf16[4,2,2,2,16,1536]{5,4,3,2,1,0:T(8,128)(2,1)} %bitcast.25, bf16[4,2,2,2,16,512]{5,4,3,2,1,0:T(8,128)(2,1)} %bitcast.28, ...), custom_call_target="tpu_custom_call" | custom-call | tf_op jit(solution)/shard_map/reduce/pallas_call | solution.py:926
  308.9 1.6 pad_maximum_fusion.refs_0_
  310.5 2.6 update.1

commit v3 on v2

--- a/solution.py
+++ b/solution.py
@@ -68,6 +68,117 @@
     return top + jnp.log(jnp.sum(jnp.exp(logits - top), axis=axis, keepdims=True))
 
 
+MESH_ID = pl.DeviceIdType.MESH
+AXES = ("dp", "fsdp")
+SPLIT = (4, 2, 2, 2)
+COPIES = 8
+
+
+def coordinates():
+    dp, fsdp = lax.axis_index("dp"), lax.axis_index("fsdp")
+    return dp // 2, dp % 2, fsdp // 2, fsdp % 2
+
+
+def device_of(z, x, y, c):
+    return (z * 2 + x, y * 2 + c)
+
+
+def z_others(z):
+    return (z + 1 - 2 * (z % 2), (z + 2) % 4, 3 - z)
+
+
+def neighbours():
+    z, x, y, c = coordinates()
+    others = [device_of(one, x, y, c) for one in z_others(z)]
+    return others + [
+        device_of(z, 1 - x, y, c), device_of(z, x, 1 - y, c), device_of(z, x, y, 1 - c)
+    ]
+
+
+def meet_neighbours():
+    barrier = pltpu.get_barrier_semaphore()
+    peers = neighbours()
+    for peer in peers:
+        pl.semaphore_signal(barrier, inc=1, device_id=peer, device_id_type=MESH_ID)
+    pl.semaphore_wait(barrier, len(peers))
+
+
+def halves(shape):
+    if shape[-1] > LANES:
+        middle_column = shape[-1] // 2
+        return (
+            (slice(None), pl.ds(0, middle_column)),
+            (slice(None), pl.ds(middle_column, middle_column)),
+        )
+    middle_row = shape[-2] // 2
+    return (
+        (pl.ds(0, middle_row), slice(None)),
+        (pl.ds(middle_row, middle_row), slice(None)),
+    )
+
+
+def remote(source, target, sems, index, device):
+    send, recv = sems
+    return pltpu.make_async_remote_copy(
+        src_ref=source, dst_ref=target, send_sem=send.at[index], recv_sem=recv.at[index],
+        device_id=device, device_id_type=MESH_ID,
+    )
+
+
+def gather_stages(full, sems, base):
+    z, x, y, c = coordinates()
+    first, second = halves(full.shape)
+    every = slice(None)
+
+    def same(index, place, device):
+        part = full.at[place]
+        return remote(part, part, sems, base + index, device)
+
+    def stage_z():
+        return [
+            same(k, (z, x, y, c), device_of(one, x, y, c)) for k, one in enumerate(z_others(z))
+        ]
+
+    def stage_one():
+        return [
+            same(3, (every, x, y, c) + first, device_of(z, 1 - x, y, c)),
+            same(4, (every, x, y, c) + second, device_of(z, x, 1 - y, c)),
+        ]
+
+    def stage_two():
+        return [
+            same(5, (every, every, y, c) + first, device_of(z, x, 1 - y, c)),
+            same(6, (every, x, every, c) + second, device_of(z, 1 - x, y, c)),
+        ]
+
+    def stage_core():
+        return [same(7, (every, every, every, c), device_of(z, x, y, 1 - c))]
+
+    return [stage_z, stage_one, stage_two, stage_core]
+
+
+def start_all(copies):
+    for copy in copies:
+        copy.start()
+
+
+def wait_all(copies):
+    for copy in copies:
+        copy.wait()
+
+
+def one_hot(shape, row_of, column_of):
+    rows = lax.broadcasted_iota(jnp.int32, shape, 0)
+    columns = lax.broadcasted_iota(jnp.int32, shape, 1)
+    return row_of(rows, columns) == column_of(rows, columns)
+
+
+def norm_place():
+    z, x, y, c = coordinates()
+    device = (z * 2 + x) * 4 + y * 2 + c
+    return device // 8, device % 8
+
+
 GROUP = 8 * BLOCK
 
 
@@ -95,8 +206,108 @@
     return jnp.concatenate(parts, axis=0)
 
 
-def front_kernel(
-    lengths_ref, norms_ref, x_ref, proj_ref, sort_ref,
+class Quiet:
+    def __getattr__(self, name):
+        return lambda *unused: None
+
+
+class GatherSteps:
+    def __init__(self, proj, up, down, small, sems):
+        fulls = (proj, up, down, small)
+        self.proj, self.up, self.down, self.small = [
+            gather_stages(full, sems, COPIES * b) for b, full in enumerate(fulls)
+        ]
+
+    def start(self, plan, step):
+        start_all(plan[step]())
+
+    def turn(self, plan, step):
+        wait_all(plan[step]())
+        if step < 3:
+            start_all(plan[step + 1]())
+
+    def begin(self):
+        self.start(self.small, 0)
+        self.start(self.proj, 0)
+        for step in range(4):
+            self.turn(self.small, step)
+        self.turn(self.proj, 0)
+
+    def half_normed(self):
+        self.turn(self.proj, 1)
+        self.start(self.up, 0)
+
+    def all_normed(self):
+        self.turn(self.proj, 2)
+
+    def before_project(self):
+        self.turn(self.proj, 3)
+        self.turn(self.up, 0)
+        self.start(self.down, 0)
+
+    def project(self, k):
+        self.when(k, 2, self.up, 1)
+        self.when(k, 5, self.up, 2)
+        self.when(k, 6, self.down, 0)
+
+    def sort(self, i):
+        self.when(i, 2, self.down, 1)
+
+    def low(self, k):
+        self.when(k, 0, self.up, 3)
+        self.when(k, 2, self.down, 2)
+
+    def end(self):
+        self.turn(self.down, 3)
+
+    def when(self, k, place, plan, step):
+        pl.when(k == place)(functools.partial(self.turn, plan, step))
+
+
+def front_near_kernel(
+    lengths_ref, x_ref, proj_own, up_own, down_own, sort_own, norm_own,
+    proj, up, down, sort_ref, norms_ref, *rest,
+):
+    rest, (small, send, recv) = rest[:-3], rest[-3:]
+    mine = coordinates()
+    proj[mine] = proj_own[...].astype(bf16)
+    up[mine] = up_own[...].astype(bf16)
+    down[mine] = down_own[...].astype(bf16)
+    quarter, eighth = norm_place()
+    own = norm_own.shape[1]
+    spread = one_hot((own, LANES), lambda r, l: r + eighth * own, lambda r, l: l)
+    lanes = dot(norm_own[...].astype(bf16), spread.astype(f32).astype(bf16)).astype(bf16)
+    lift = one_hot((16, 4), lambda r, l: r, lambda r, l: l * 4 + quarter)
+    tile = dot(lift.astype(f32).astype(bf16), lanes).astype(bf16)
+    small[mine] = jnp.concatenate([sort_own[...].astype(bf16), tile], axis=0)
+    meet_neighbours()
+    steps = GatherSteps(proj, up, down, small, (send, recv))
+    steps.begin()
+    pieces = small[...].reshape(-1, 32, LANES)
+    sort_ref[...] = pieces[:, :16].reshape(sort_ref.shape)
+    tile = jnp.sum(pieces[:, 16:].astype(f32), axis=0)
+    norms_ref[...] = jnp.concatenate(
+        [
+            jnp.concatenate([tile[4 * i + q : 4 * i + q + 1] for q in range(4)], axis=1)
+            for i in range(4)
+        ],
+        axis=0,
+    )
+
+    def columns_of(columns):
+        return proj[:, :, :, :, :, columns].reshape(x_ref.shape[1], -1)
+
+    front_steps(steps, columns_of, lengths_ref, norms_ref, x_ref, sort_ref, *rest)
+
+
+def front_plain_kernel(lengths_ref, norms_ref, x_ref, proj_ref, sort_ref, *rest):
+    front_steps(
+        Quiet(), lambda columns: proj_ref[:, columns], lengths_ref, norms_ref, x_ref, sort_ref, *rest
+    )
+
+
+def front_steps(
+    steps, proj_columns, lengths_ref, norms_ref, x_ref, sort_ref,
     normed_hbm, qkv_hbm, skv_hbm, tkv_hbm, means_ref, states_ref,
     normed_s, stage, matrix, qkv_buf, low_buf, flip_buf, copy_sem, qkv_sem, low_sem, flip_sem,
 ):
@@ -120,7 +331,10 @@
         ).astype(bf16)
         return carry
 
-    lax.fori_loop(0, tiles, norm_step, 0)
+    lax.fori_loop(0, tiles // 2, norm_step, 0)
+    steps.half_normed()
+    lax.fori_loop(tiles // 2, tiles, norm_step, 0)
+    steps.all_normed()
     normed_copy = pltpu.make_async_copy(normed_s, normed_hbm, copy_sem)
     normed_copy.start()
 
@@ -141,19 +355,21 @@
         def _():
             qkv_copy(k - 2, slot).wait()
 
+        steps.project(k)
         logits = logits - log_sum_exp(logits, 1)
         states_ref[2 * k] = jnp.exp(logits)
         logits = logits - log_sum_exp(logits, 0)
         states_ref[2 * k + 1] = jnp.exp(logits)
         normed = normed_s[rows, :]
-        qkv_buf[slot, :, :width] = dot(normed, proj_ref[:, :width]).astype(bf16)
-        product = dot(normed, proj_ref[:, width : 3 * width]).astype(bf16)
+        qkv_buf[slot, :, :width] = dot(normed, proj_columns(slice(0, width))).astype(bf16)
+        product = dot(normed, proj_columns(slice(width, 3 * width))).astype(bf16)
         qkv_buf[slot, :, width:] = product
         spread_tokens(stage, matrix[...], k, product)
         qkv_copy(k, slot).start()
         return logits
 
     assert tiles == SINK_ITERS
+    steps.before_project()
     matrix[...] = regroup_matrix(False)
     lax.fori_loop(0, tiles, project_step, logits)
     permute = states_ref[2 * SINK_ITERS - 1].astype(bf16)
@@ -163,6 +379,7 @@
 
     def sort_step(i, carry):
         group = flip_buf.shape[0]
+        steps.sort(i)
 
         @pl.when(i >= 1)
         def _():
@@ -195,6 +412,7 @@
         def _():
             low_copy(k - 2, slot).wait()
 
+        steps.low(k)
         low_buf[slot] = collect_tokens(stage, matrix[...], k, TILE).astype(bf16)
         low_copy(k, slot).start()
         return carry
@@ -207,26 +425,22 @@
         qkv_copy(k, k % 2).wait()
         low_copy(k, k % 2).wait()
     normed_copy.wait()
-
-
-def front(lengths, norms, x, proj, sort):
-    seq, width = x.shape
+    steps.end()
+
+
+def front_shapes(seq, width):
     blocks = seq // BLOCK
     hbm = pl.BlockSpec(memory_space=pl.ANY)
     vmem = pl.BlockSpec(memory_space=pltpu.VMEM)
-    return pl.pallas_call(
-        front_kernel,
-        out_shape=(
-            jax.ShapeDtypeStruct((seq, width), bf16),
-            jax.ShapeDtypeStruct((seq, 3 * width), bf16),
-            jax.ShapeDtypeStruct((seq, 2 * width), bf16),
-            jax.ShapeDtypeStruct((BLOCK, 2 * width, blocks), bf16),
-            jax.ShapeDtypeStruct((blocks, width), bf16),
-            jax.ShapeDtypeStruct((2 * SINK_ITERS, blocks, blocks), f32),
-        ),
-        in_specs=[pl.BlockSpec(memory_space=pltpu.SMEM), vmem, vmem, vmem, vmem],
-        out_specs=[hbm, hbm, hbm, hbm, vmem, vmem],
-        scratch_shapes=[
+    shapes = (
+        jax.ShapeDtypeStruct((seq, width), bf16),
+        jax.ShapeDtypeStruct((seq, 3 * width), bf16),
+        jax.ShapeDtypeStruct((seq, 2 * width), bf16),
+        jax.ShapeDtypeStruct((BLOCK, 2 * width, blocks), bf16),
+        jax.ShapeDtypeStruct((blocks, width), bf16),
+        jax.ShapeDtypeStruct((2 * SINK_ITERS, blocks, blocks), f32),
+    )
+    scratch = [
             pltpu.VMEM((seq, width), bf16),
             pltpu.VMEM((BLOCK, blocks, 2 * width), f32),
             pltpu.VMEM((GROUP, GROUP), bf16),
@@ -237,10 +451,47 @@
             pltpu.SemaphoreType.DMA((2,)),
             pltpu.SemaphoreType.DMA((2,)),
             pltpu.SemaphoreType.DMA((8,)),
-        ],
+    ]
+    return shapes, [hbm, hbm, hbm, hbm, vmem, vmem], scratch
+
+
+def front_plain(lengths, x, *shards):
+    proj, up, down, sort, norms = gather_plain(*shards)
+    shapes, specs, scratch = front_shapes(*x.shape)
+    vmem = pl.BlockSpec(memory_space=pltpu.VMEM)
+    results = pl.pallas_call(
+        front_plain_kernel,
+        out_shape=shapes,
+        in_specs=[pl.BlockSpec(memory_space=pltpu.SMEM), vmem, vmem, vmem, vmem],
+        out_specs=specs,
+        scratch_shapes=scratch,
         compiler_params=pltpu.CompilerParams(vmem_limit_bytes=VMEM_LIMIT),
         name="front",
     )(lengths, norms, x, proj, sort)
+    return (proj, up, down, sort, norms, *results)
+
+
+def front_near(lengths, x, proj, up, down, sort, norm):
+    seq, width = x.shape
+    shapes, specs, scratch = front_shapes(seq, width)
+    vmem = pl.BlockSpec(memory_space=pltpu.VMEM)
+    fulls = [jax.ShapeDtypeStruct(SPLIT + own.shape, bf16) for own in (proj, up, down)]
+    fulls += [jax.ShapeDtypeStruct((32 * sort.shape[0], LANES), bf16)]
+    fulls += [jax.ShapeDtypeStruct((4, width), f32)]
+    scratch = scratch + [pltpu.VMEM(SPLIT + (32, LANES), bf16)]
+    scratch += [pltpu.SemaphoreType.DMA((4 * COPIES,))] * 2
+    results = pl.pallas_call(
+        front_near_kernel,
+        out_shape=tuple(fulls) + shapes,
+        in_specs=[pl.BlockSpec(memory_space=pltpu.SMEM)] + [vmem] * 6,
+        out_specs=[vmem] * 5 + specs,
+        scratch_shapes=scratch,
+        compiler_params=pltpu.CompilerParams(
+            collective_id=0, has_side_effects=True, vmem_limit_bytes=VMEM_LIMIT
+        ),
+        name="front",
+    )(lengths, x, proj, up, down, sort, norm)
+    return tuple(full.reshape(-1, full.shape[-1]) for full in results[:3]) + tuple(results[3:])
 
 
 def layer_norm_back(grad, gain, xhat, inverse):
@@ -477,12 +728,209 @@
     )(lengths, norms, x, cot, qkv, skv, proj, up, down)
 
 
-def back_kernel(
-    norms_ref, gskv_hbm, tkv_hbm, states_ref, means_ref, proj_ref, sort_ref,
+def add_low(*parts):
+    total = parts[0].astype(f32)
+    for part in parts[1:]:
+        total = total + part.astype(f32)
+    return total
+
+
+class Reduce:
+    def __init__(self, part, total, columns, got_c, got_a, got_b, got_two, got_z, sems, base):
+        self.part, self.total, self.columns = part, total, columns
+        self.got_c, self.got_a, self.got_b = got_c, got_a, got_b
+        self.got_two, self.got_z, self.sems, self.base = got_two, got_z, sems, base
+        self.first, self.second = halves(part.shape)
+
+    def copies(self, step):
+        z, x, y, c = coordinates()
+        every = slice(None)
+        to_x, to_y = device_of(z, 1 - x, y, c), device_of(z, x, 1 - y, c)
+
+        def one(source, target, index, device):
+            return remote(source, target, self.sems, self.base + index, device)
+
+        if step == 0:
+            away = self.part.at[every, every, every, 1 - c]
+            return [one(away, self.got_c, 0, device_of(z, x, y, 1 - c))]
+        if step == 1:
+            away_a = self.got_c.at[(every, every, 1 - y) + self.first]
+            away_b = self.got_c.at[(every, 1 - x, every) + self.second]
+            return [one(away_a, self.got_a, 1, to_y), one(away_b, self.got_b, 2, to_x)]
+        if step == 2:
+            away_a, away_b = self.got_a.at[every, 1 - x], self.got_b.at[every, 1 - y]
+            return [
+                one(away_a, self.got_two.at[(every,) + self.first], 3, to_x),
+                one(away_b, self.got_two.at[(every,) + self.second], 4, to_y),
+            ]
+        return [
+            one(self.got_two.at[other], self.got_z.at[k], 5 + k, device_of(other, x, y, c))
+            for k, other in enumerate(z_others(z))
+        ]
+
+    def start(self, step):
+        start_all(self.copies(step))
+
+    def turn(self, step):
+        wait_all(self.copies(step))
+        self.add(step)
+        if step < 3:
+            self.start(step + 1)
+
+    def add(self, step):
+        z, x, y, c = coordinates()
+        if step == 3:
+            self.total[:, self.columns] = add_low(
+                self.got_two[z], *[self.got_z[k] for k in range(3)]
+            )
+            return
+
+        def line(i, carry):
+            if step == 0:
+                for j in range(2):
+                    for k in range(2):
+                        self.got_c[i, j, k] = add_low(
+                            self.part[i, j, k, c], self.got_c[i, j, k]
+                        ).astype(bf16)
+            elif step == 1:
+                for j in range(2):
+                    self.got_a[i, j] = add_low(
+                        self.got_c[(i, j, y) + self.first], self.got_a[i, j]
+                    ).astype(bf16)
+                    self.got_b[i, j] = add_low(
+                        self.got_c[(i, x, j) + self.second], self.got_b[i, j]
+                    ).astype(bf16)
+            else:
+                self.got_two[(i,) + self.first] = add_low(
+                    self.got_a[i, x], self.got_two[(i,) + self.first]
+                ).astype(bf16)
+                self.got_two[(i,) + self.second] = add_low(
+                    self.got_b[i, y], self.got_two[(i,) + self.second]
+                ).astype(bf16)
+            return carry
+
+        lax.fori_loop(0, 4, line, 0)
+
+
+def reduce_scratch(rows, columns):
+    half = (rows, columns // 2) if columns > LANES else (rows // 2, columns)
+    shapes = (
+        (4, 2, 2, rows, columns), (4, 2) + half, (4, 2) + half, (4, rows, columns),
+        (3, rows, columns),
+    )
+    return [pltpu.VMEM(shape, bf16) for shape in shapes]
+
+
+class ReduceSteps:
+    def __init__(self, qkv, out, up, down, small):
+        self.qkv, self.out, self.up, self.down, self.small = qkv, out, up, down, small
+
+    def begin(self):
+        self.up.start(0)
+        self.down.start(0)
+        self.out.start(0)
+
+    def loaded(self):
+        self.up.turn(0)
+
+    def sort(self, i):
+        self.when(i, 5, self.up, 1)
+        self.when(i, 6, self.down, 0)
+
+    def swept(self):
+        self.up.turn(2)
+
+    def first(self, k):
+        self.when(k, 1, self.down, 1)
+        self.when(k, 2, self.out, 0)
+        self.when(k, 4, self.down, 2)
+        self.when(k, 6, self.up, 3)
+        self.when(k, 7, self.out, 1)
+
+    def between(self):
+        self.qkv.start(0)
+        self.out.turn(2)
+
+    def second(self, k):
+        self.when(k, 1, self.down, 3)
+        self.when(k, 2, self.qkv, 0)
+        self.when(k, 3, self.out, 3)
+        self.when(k, 6, self.qkv, 1)
+
+    def when(self, k, place, plan, step):
+        pl.when(k == place)(functools.partial(plan.turn, step))
+
+
+def norm_rows(grads):
+    rows = []
+    for grad in grads:
+        for i in range(grad.shape[0]):
+            for q in range(grad.shape[1] // LANES):
+                rows.append(grad[i : i + 1, q * LANES : (q + 1) * LANES])
+    return jnp.concatenate(rows, axis=0)
+
+
+def back_plain_kernel(*refs):
+    back_steps(Quiet(), *refs)
+
+
+def back_near_kernel(*refs):
+    ins, refs = refs[:12], refs[12:]
+    (gout, gup, gdown, gnorm_two), refs = refs[:4], refs[4:]
+    (gx_hbm, gsum_hbm, proj_sum, up_sum, down_sum, sort_sum, norm_sum), refs = refs[:7], refs[7:]
+    work, refs = refs[:9], refs[9:]
+    (gqkv, gsort, gnorm, small, small_sum, send, recv), scratch = refs[:7], refs[7:]
+    width = gsort.shape[0]
+    sems = (send, recv)
+    every = slice(None)
+    places = (
+        (gqkv, proj_sum, pl.ds(0, 3 * width)), (gout, proj_sum, pl.ds(3 * width, width)),
+        (gup, up_sum, every), (gdown, down_sum, every), (small, small_sum, every),
+    )
+    steps = ReduceSteps(
+        *[
+            Reduce(part, total, columns, *scratch[5 * b : 5 * b + 5], sems, COPIES * b)
+            for b, (part, total, columns) in enumerate(places)
+        ]
+    )
+    meet_neighbours()
+    back_steps(steps, *ins, gx_hbm, gsum_hbm, gqkv, gsort, gnorm, *work)
+    tile = norm_rows((gnorm[...], gnorm_two[...])).astype(bf16)
+    shards = gsort[...].astype(bf16).reshape(SPLIT + (width // 32, LANES))
+    small[:, :, :, :, :16] = shards
+    for i in range(4):
+        for j in range(2):
+            for k in range(2):
+                for m in range(2):
+                    small[i, j, k, m, 16:] = tile
+    steps.small.start(0)
+    steps.small.turn(0)
+    steps.qkv.turn(2)
+    for step in range(1, 4):
+        steps.small.turn(step)
+    steps.qkv.turn(3)
+    sort_sum[...] = small_sum[:16, :]
+    quarter, eighth = norm_place()
+    own = norm_sum.shape[1]
+    drop = one_hot((4, 16), lambda r, l: r * 4 + quarter, lambda r, l: l).astype(f32)
+    pick = one_hot((LANES, own), lambda r, l: r, lambda r, l: l + eighth * own).astype(f32)
+
+    def exact(left, right):
+        return lax.dot_general(
+            left, right, (((1,), (0,)), ((), ())),
+            precision=lax.Precision.HIGHEST, preferred_element_type=f32,
+        )
+
+    norm_sum[...] = exact(exact(drop, small_sum[16:, :]), pick)
+
+
+def back_steps(
+    steps, norms_ref, gskv_hbm, tkv_hbm, states_ref, means_ref, proj_ref, sort_ref,
     x_hbm, normed_hbm, hidden_grad_hbm, gq_hbm, gkv_hbm,
-    gx_hbm, gproj_ref, gsort_ref, gnorm_ref,
+    gx_hbm, gsum_hbm, gproj_ref, gsort_ref, gnorm_ref,
     stage, matrix, low_buf, flip_buf, gproj, gperm, gmeans, low_sem, flip_sem,
 ):
+    steps.begin()
     seq, width = x_hbm.shape
     tiles = seq // TILE
     blocks = seq // BLOCK
@@ -518,6 +966,7 @@
     matrix[...] = regroup_matrix(False)
     lax.fori_loop(0, tiles, load_step, 0)
     matrix[...] = regroup_matrix(True)
+    steps.loaded()
 
     final = states_ref[2 * SINK_ITERS - 1]
     permute_t = final.T.astype(bf16)
@@ -525,6 +974,7 @@
 
     def sort_step(i, carry):
         side = lax.rem(i, 2) * group
+        steps.sort(i)
 
         @pl.when(i + 1 < BLOCK // group)
         def _():
@@ -554,19 +1004,25 @@
     grad = grad.astype(bf16)
     gsort_ref[...] = dot_tn(means_ref[...], grad).astype(gsort_ref.dtype)
     gmeans[...] = dot_nt(grad, sort_ref[...]) * (1.0 / BLOCK)
+    steps.swept()
     gproj[...] = jnp.zeros_like(gproj)
     gnorm_ref[...] = jnp.zeros_like(gnorm_ref)
     gain = norms_ref[0:1, :].astype(f32)
 
-    def tile_step(x_ref, normed_ref, hidden_grad_ref, gq_ref, gkv_ref, gx_ref):
+    def weight_step(normed_ref, gq_ref, gkv_ref, gsum_ref):
         k = pl.program_id(0)
-        rows = pl.ds(pl.multiple_of(k * TILE, TILE), TILE)
+        steps.first(k)
         far = collect_tokens(stage, matrix[...], k, TILE)
         gkv = (gkv_ref[...].astype(f32) + far).astype(bf16)
-        gq = gq_ref[...]
+        gsum_ref[...] = gkv
         normed = normed_ref[...]
-        gproj[:, :width] += dot_tn(normed, gq)
+        gproj[:, :width] += dot_tn(normed, gq_ref[...])
         gproj[:, width:] += dot_tn(normed, gkv)
+
+    def input_step(x_ref, hidden_grad_ref, gq_ref, gsum_ref, gx_ref):
+        k = pl.program_id(0)
+        steps.second(k)
+        gq, gkv = gq_ref[...], gsum_ref[...]
         grad_normed = dot_nt(gq, proj_ref[:, :width]) + dot_nt(gkv, proj_ref[:, width : 3 * width])
         means = gmeans[pl.ds(pl.multiple_of(k * per_tile, per_tile), per_tile), :]
         grad_normed = grad_normed + jnp.broadcast_to(
@@ -581,30 +1037,24 @@
         return pl.BlockSpec((TILE, columns), lambda i: (i, 0))
 
     pltpu.emit_pipeline(
-        tile_step,
+        weight_step,
         grid=(tiles,),
-        in_specs=[rows_of(width)] * 4 + [rows_of(2 * width)],
+        in_specs=[rows_of(width)] * 2 + [rows_of(2 * width)],
+        out_specs=[rows_of(2 * width)],
+    )(normed_hbm, gq_hbm, gkv_hbm, gsum_hbm)
+    gproj_ref[...] = gproj[...].astype(bf16).reshape(gproj_ref.shape)
+    steps.between()
+    pltpu.emit_pipeline(
+        input_step,
+        grid=(tiles,),
+        in_specs=[rows_of(width)] * 3 + [rows_of(2 * width)],
         out_specs=[rows_of(width)],
-    )(x_hbm, normed_hbm, hidden_grad_hbm, gq_hbm, gkv_hbm, gx_hbm)
-    gproj_ref[...] = gproj[...].astype(gproj_ref.dtype)
-
-
-def back(norms, gskv, tkv, states, means, proj, sort, x, normed, hidden_grad, gq, gkv):
-    seq, width = x.shape
+    )(x_hbm, hidden_grad_hbm, gq_hbm, gsum_hbm, gx_hbm)
+
+
+def back_scratch(seq, width):
     blocks = seq // BLOCK
-    hbm = pl.BlockSpec(memory_space=pl.ANY)
-    vmem = pl.BlockSpec(memory_space=pltpu.VMEM)
-    return pl.pallas_call(
-        back_kernel,
-        out_shape=(
-            jax.ShapeDtypeStruct((seq, width), f32),
-            jax.ShapeDtypeStruct((width, 3 * width), bf16),
-            jax.ShapeDtypeStruct((width, blocks), bf16),
-            jax.ShapeDtypeStruct((2, width), f32),
-        ),
-        in_specs=[vmem, hbm, hbm, vmem, vmem, vmem, vmem, hbm, hbm, hbm, hbm, hbm],
-        out_specs=[hbm, vmem, vmem, vmem],
-        scratch_shapes=[
+    return [
             pltpu.VMEM((BLOCK, blocks, 2 * width), f32),
             pltpu.VMEM((GROUP, GROUP), bf16),
             pltpu.VMEM((2, TILE, 2 * width), bf16),
@@ -614,329 +1064,72 @@
             pltpu.VMEM((blocks, width), f32),
             pltpu.SemaphoreType.DMA((2,)),
             pltpu.SemaphoreType.DMA((8,)),
-        ],
+    ]
+
+
+def back_plain(ins, gout, gup, gdown, gnorm_two):
+    seq, width = ins[7].shape
+    blocks = seq // BLOCK
+    hbm = pl.BlockSpec(memory_space=pl.ANY)
+    vmem = pl.BlockSpec(memory_space=pltpu.VMEM)
+    gx, unused, gqkv, gsort, gnorm_one = pl.pallas_call(
+        back_plain_kernel,
+        out_shape=(
+            jax.ShapeDtypeStruct((seq, width), f32),
+            jax.ShapeDtypeStruct((seq, 2 * width), bf16),
+            jax.ShapeDtypeStruct((width, 3 * width), bf16),
+            jax.ShapeDtypeStruct((width, blocks), f32),
+            jax.ShapeDtypeStruct((2, width), f32),
+        ),
+        in_specs=[vmem, hbm, hbm, vmem, vmem, vmem, vmem, hbm, hbm, hbm, hbm, hbm],
+        out_specs=[hbm, hbm, vmem, vmem, vmem],
+        scratch_shapes=back_scratch(seq, width),
         compiler_params=pltpu.CompilerParams(vmem_limit_bytes=VMEM_LIMIT),
         name="back",
-    )(norms, gskv, tkv, states, means, proj, sort, x, normed, hidden_grad, gq, gkv)
-
-
-MESH_ID = pl.DeviceIdType.MESH
-AXES = ("dp", "fsdp")
-SPLIT = (4, 2, 2, 2)
-COPIES = 8
-
-
-def coordinates():
-    dp, fsdp = lax.axis_index("dp"), lax.axis_index("fsdp")
-    return dp // 2, dp % 2, fsdp // 2, fsdp % 2
-
-
-def device_of(z, x, y, c):
-    return (z * 2 + x, y * 2 + c)
-
-
-def z_others(z):
-    return (z + 1 - 2 * (z % 2), (z + 2) % 4, 3 - z)
-
-
-def neighbours():
-    z, x, y, c = coordinates()
-    others = [device_of(one, x, y, c) for one in z_others(z)]
-    return others + [
-        device_of(z, 1 - x, y, c), device_of(z, x, 1 - y, c), device_of(z, x, y, 1 - c)
+    )(*ins)
+    return gx, *reduce_plain(gqkv, gout, gup, gdown, gsort, gnorm_one, gnorm_two)
+
+
+def back_near(ins, gout, gup, gdown, gnorm_two):
+    seq, width = ins[7].shape
+    blocks = seq // BLOCK
+    hbm = pl.BlockSpec(memory_space=pl.ANY)
+    vmem = pl.BlockSpec(memory_space=pltpu.VMEM)
+
+    def split(grad):
+        return grad.reshape(SPLIT + (grad.shape[0] // 32, grad.shape[1]))
+
+    gout, gup, gdown = split(gout), split(gup), split(gdown)
+    rows = width // 32
+    small = (32, LANES)
+    qkv = (rows, 3 * width)
+    scratch = back_scratch(seq, width) + [
+        pltpu.VMEM(SPLIT + qkv, bf16),
+        pltpu.VMEM((width, blocks), f32),
+        pltpu.VMEM((2, width), f32),
+        pltpu.VMEM(SPLIT + small, bf16),
+        pltpu.VMEM(small, f32),
     ]
-
-
-def meet_neighbours():
-    barrier = pltpu.get_barrier_semaphore()
-    peers = neighbours()
-    for peer in peers:
-        pl.semaphore_signal(barrier, inc=1, device_id=peer, device_id_type=MESH_ID)
-    pl.semaphore_wait(barrier, len(peers))
-
-
-def halves(shape):
-    if shape[-1] > LANES:
-        middle_column = shape[-1] // 2
-        return (
-            (slice(None), pl.ds(0, middle_column)),
-            (slice(None), pl.ds(middle_column, middle_column)),
-        )
-    middle_row = shape[-2] // 2
-    return (
-        (pl.ds(0, middle_row), slice(None)),
-        (pl.ds(middle_row, middle_row), slice(None)),
-    )
-
-
-def remote(source, target, sems, index, device):
-    send, recv = sems
-    return pltpu.make_async_remote_copy(
-        src_ref=source, dst_ref=target, send_sem=send.at[index], recv_sem=recv.at[index],
-        device_id=device, device_id_type=MESH_ID,
-    )
-
-
-def gather_stages(full, sems, base):
-    z, x, y, c = coordinates()
-    first, second = halves(full.shape)
-    every = slice(None)
-
-    def same(index, place, device):
-        part = full.at[place]
-        return remote(part, part, sems, base + index, device)
-
-    def stage_z():
-        return [
-            same(k, (z, x, y, c), device_of(one, x, y, c)) for k, one in enumerate(z_others(z))
-        ]
-
-    def stage_one():
-        return [
-            same(3, (every, x, y, c) + first, device_of(z, 1 - x, y, c)),
-            same(4, (every, x, y, c) + second, device_of(z, x, 1 - y, c)),
-        ]
-
-    def stage_two():
-        return [
-            same(5, (every, every, y, c) + first, device_of(z, x, 1 - y, c)),
-            same(6, (every, x, every, c) + second, device_of(z, 1 - x, y, c)),
-        ]
-
-    def stage_core():
-        return [same(7, (every, every, every, c), device_of(z, x, y, 1 - c))]
-
-    return [stage_z, stage_one, stage_two, stage_core]
-
-
-def start_all(copies):
-    for copy in copies:
-        copy.start()
-
-
-def wait_all(copies):
-    for copy in copies:
-        copy.wait()
-
-
-def one_hot(shape, row_of, column_of):
-    rows = lax.broadcasted_iota(jnp.int32, shape, 0)
-    columns = lax.broadcasted_iota(jnp.int32, shape, 1)
-    return row_of(rows, columns) == column_of(rows, columns)
-
-
-def norm_place():
-    z, x, y, c = coordinates()
-    device = (z * 2 + x) * 4 + y * 2 + c
-    return device // 8, device % 8
-
-
-def gather_kernel(proj_ref, up_ref, down_ref, sort_ref, norm_ref, proj, up, down, small, send, recv):
-    z, x, y, c = coordinates()
-    mine = (z, x, y, c)
-    proj[mine] = proj_ref[...].astype(bf16)
-    up[mine] = up_ref[...].astype(bf16)
-    down[mine] = down_ref[...].astype(bf16)
-    quarter, eighth = norm_place()
-    own = norm_ref.shape[1]
-    spread = one_hot((own, LANES), lambda r, l: r + eighth * own, lambda r, l: l)
-    lanes = dot(norm_ref[...].astype(bf16), spread.astype(bf16)).astype(bf16)
-    lift = one_hot((16, 4), lambda r, l: r, lambda r, l: l * 4 + quarter)
-    tile = dot(lift.astype(bf16), lanes).astype(bf16)
-    small[mine] = jnp.concatenate([sort_ref[...].astype(bf16), tile], axis=0)
-    meet_neighbours()
-    fulls = (proj, up, down, small)
-    plans = [gather_stages(full, (send, recv), COPIES * b) for b, full in enumerate(fulls)]
-    for step in range(4):
-        copies = [copy for plan in plans for copy in plan[step]()]
-        start_all(copies)
-        wait_all(copies)
-
-
-def gather(proj, up, down, sort, norm):
-    shapes = (proj.shape, up.shape, down.shape, (32, LANES))
-    vmem = pl.BlockSpec(memory_space=pltpu.VMEM)
-    proj, up, down, small = pl.pallas_call(
-        gather_kernel,
-        out_shape=tuple(jax.ShapeDtypeStruct(SPLIT + shape, bf16) for shape in shapes),
-        in_specs=[vmem] * 5,
-        out_specs=[vmem] * 4,
-        scratch_shapes=[pltpu.SemaphoreType.DMA((4 * COPIES,))] * 2,
-        compiler_params=pltpu.CompilerParams(
-            collective_id=0, has_side_effects=True, vmem_limit_bytes=VMEM_LIMIT
+    scratch += [pltpu.SemaphoreType.DMA((5 * COPIES,))] * 2
+    for shape in (qkv, gout.shape[-2:], gup.shape[-2:], gdown.shape[-2:], small):
+        scratch += reduce_scratch(*shape)
+    sums = [(rows, 4 * width), gup.shape[-2:], gdown.shape[-2:], (rows, blocks), (4, rows)]
+    gx, unused, *totals = pl.pallas_call(
+        back_near_kernel,
+        out_shape=(
+            jax.ShapeDtypeStruct((seq, width), f32),
+            jax.ShapeDtypeStruct((seq, 2 * width), bf16),
+            *[jax.ShapeDtypeStruct(shape, f32) for shape in sums],
         ),
-        name="gather",
-    )(proj, up, down, sort, norm)
-    small = small.reshape(32, 32, LANES)
-    sort = small[:, :16].reshape(-1, LANES)
-    norms = jnp.sum(small[:, 16:].astype(f32), axis=0).astype(bf16).reshape(4, -1)
-
-    def flat(array):
-        return array.reshape(-1, array.shape[-1])
-
-    return flat(proj), flat(up), flat(down), sort, norms
-
-
-def add_low(*parts):
-    total = parts[0].astype(f32)
-    for part in parts[1:]:
-        total = total + part.astype(f32)
-    return total
-
-
-class Reduce:
-    def __init__(self, part, total, got_c, sum_c, got_a, got_b, sum_a, sum_b, got_z, sems, base):
-        self.part, self.total, self.got_c, self.sum_c = part, total, got_c, sum_c
-        self.got_a, self.got_b, self.sum_a, self.sum_b = got_a, got_b, sum_a, sum_b
-        self.got_z, self.sems, self.base = got_z, sems, base
-        self.first, self.second = halves(part.shape)
-
-    def copies(self, step):
-        z, x, y, c = coordinates()
-        every = slice(None)
-        to_x, to_y = device_of(z, 1 - x, y, c), device_of(z, x, 1 - y, c)
-
-        def one(source, target, index, device):
-            return remote(source, target, self.sems, self.base + index, device)
-
-        if step == 0:
-            away = self.part.at[every, every, every, 1 - c]
-            return [one(away, self.got_c, 0, device_of(z, x, y, 1 - c))]
-        if step == 1:
-            away_a = self.sum_c.at[(every, every, 1 - y) + self.first]
-            away_b = self.sum_c.at[(every, 1 - x, every) + self.second]
-            return [one(away_a, self.got_a, 1, to_y), one(away_b, self.got_b, 2, to_x)]
-        if step == 2:
-            away_a, away_b = self.sum_a.at[every, 1 - x], self.sum_b.at[every, 1 - y]
-            return [
-                one(away_a, self.got_c.at[(every, 0, 0) + self.first], 3, to_x),
-                one(away_b, self.got_c.at[(every, 0, 0) + self.second], 4, to_y),
-            ]
-        return [
-            one(self.sum_c.at[other, 0, 0], self.got_z.at[k], 5 + k, device_of(other, x, y, c))
-            for k, other in enumerate(z_others(z))
-        ]
-
-    def add(self, step):
-        z, x, y, c = coordinates()
-        if step == 3:
-            self.total[...] = add_low(self.sum_c[z, 0, 0], *[self.got_z[k] for k in range(3)])
-            return
-
-        def line(i, carry):
-            if step == 0:
-                for j in range(2):
-                    for k in range(2):
-                        self.sum_c[i, j, k] = add_low(
-                            self.part[i, j, k, c], self.got_c[i, j, k]
-                        ).astype(bf16)
-            elif step == 1:
-                for j in range(2):
-                    self.sum_a[i, j] = add_low(
-                        self.sum_c[(i, j, y) + self.first], self.got_a[i, j]
-                    ).astype(bf16)
-                    self.sum_b[i, j] = add_low(
-                        self.sum_c[(i, x, j) + self.second], self.got_b[i, j]
-                    ).astype(bf16)
-            else:
-                self.sum_c[(i, 0, 0) + self.first] = add_low(
-                    self.sum_a[i, x], self.got_c[(i, 0, 0) + self.first]
-                ).astype(bf16)
-                self.sum_c[(i, 0, 0) + self.second] = add_low(
-                    self.sum_b[i, y], self.got_c[(i, 0, 0) + self.second]
-                ).astype(bf16)
-            return carry
-
-        lax.fori_loop(0, 4, line, 0)
-
-
-def reduce_scratch(rows, columns):
-    half = (rows, columns // 2) if columns > LANES else (rows // 2, columns)
-    shapes = (
-        (4, 2, 2, rows, columns), (4, 2, 2, rows, columns), (4, 2) + half, (4, 2) + half,
-        (4, 2) + half, (4, 2) + half, (3, rows, columns),
-    )
-    return [pltpu.VMEM(shape, bf16) for shape in shapes]
-
-
-def norm_rows(grads):
-    rows = []
-    for grad in grads:
-        for i in range(grad.shape[0]):
-            for q in range(grad.shape[1] // LANES):
-                rows.append(grad[i : i + 1, q * LANES : (q + 1) * LANES])
-    return jnp.concatenate(rows, axis=0)
-
-
-def reduce_kernel(
-    gqkv_ref, gout_ref, gup_ref, gdown_ref, gsort_ref, gone_ref, gtwo_ref,
-    qkv_sum, out_sum, up_sum, down_sum, sort_sum, norm_sum,
-    small, small_sum, send, recv, *scratch,
-):
-    tile = norm_rows((gone_ref[...], gtwo_ref[...])).astype(bf16)
-    for i in range(4):
-        for j in range(2):
-            for k in range(2):
-                for m in range(2):
-                    small[i, j, k, m, :16] = gsort_ref[i, j, k, m]
-                    small[i, j, k, m, 16:] = tile
-    meet_neighbours()
-    parts = (gqkv_ref, gout_ref, gup_ref, gdown_ref, small)
-    totals = (qkv_sum, out_sum, up_sum, down_sum, small_sum)
-    plans = [
-        Reduce(part, total, *scratch[7 * b : 7 * b + 7], (send, recv), COPIES * b)
-        for b, (part, total) in enumerate(zip(parts, totals))
-    ]
-    for step in range(4):
-        copies = [plan.copies(step) for plan in plans]
-        for one in copies:
-            start_all(one)
-        for one, plan in zip(copies, plans):
-            wait_all(one)
-            plan.add(step)
-    sort_sum[...] = small_sum[:16, :]
-    quarter, eighth = norm_place()
-    own = norm_sum.shape[1]
-    drop = one_hot((4, 16), lambda r, l: r * 4 + quarter, lambda r, l: l).astype(f32)
-    pick = one_hot((LANES, own), lambda r, l: r, lambda r, l: l + eighth * own).astype(f32)
-
-    def exact(left, right):
-        return lax.dot_general(
-            left, right, (((1,), (0,)), ((), ())),
-            precision=lax.Precision.HIGHEST, preferred_element_type=f32,
-        )
-
-    norm_sum[...] = exact(exact(drop, small_sum[16:, :]), pick)
-
-
-def reduce(gqkv, gout, gup, gdown, gsort, gone, gtwo):
-    devices = 32
-
-    def split(grad):
-        return grad.reshape(SPLIT + (grad.shape[0] // devices, grad.shape[1]))
-
-    parts = tuple(split(grad) for grad in (gqkv, gout, gup, gdown, gsort))
-    shapes = [part.shape[-2:] for part in parts]
-    vmem = pl.BlockSpec(memory_space=pltpu.VMEM)
-    small = (32, LANES)
-    scratch = [pltpu.VMEM(SPLIT + small, bf16), pltpu.VMEM(small, f32)]
-    scratch += [pltpu.SemaphoreType.DMA((5 * COPIES,))] * 2
-    for shape in shapes[:4] + [small]:
-        scratch += reduce_scratch(*shape)
-    qkv, out, up, down, sort, norm = pl.pallas_call(
-        reduce_kernel,
-        out_shape=tuple(
-            jax.ShapeDtypeStruct(shape, f32) for shape in shapes + [(4, gone.shape[1] // devices)]
-        ),
-        in_specs=[vmem] * 7,
-        out_specs=[vmem] * 6,
+        in_specs=[vmem, hbm, hbm, vmem, vmem, vmem, vmem, hbm, hbm, hbm, hbm, hbm] + [vmem] * 4,
+        out_specs=[hbm, hbm] + [vmem] * 5,
         scratch_shapes=scratch,
         compiler_params=pltpu.CompilerParams(
             collective_id=1, has_side_effects=True, vmem_limit_bytes=VMEM_LIMIT
         ),
-        name="reduce",
-    )(*parts, gone, gtwo)
-    return jnp.concatenate([qkv, out], axis=1), up, down, sort, norm
+        name="back",
+    )(*ins, gout, gup, gdown, gnorm_two)
+    return gx, *totals
 
 
 def adamw(master, first, second, grad, rate, decay):
@@ -994,20 +1187,17 @@
     return (*(summed(grad, 0) for grad in (gproj, gup, gdown, gsort)), summed(gnorm, 1))
 
 
-def body(
-    near, layer_input, doc_lengths, out_cotangent, *states,
-):
+def body(near, layer_input, doc_lengths, out_cotangent, *states):
     x = layer_input[0]
     cot = out_cotangent[0]
-    proj, up, down, sort, norms = (gather if near else gather_plain)(*states[::3])
-    normed, qkv, skv, tkv, means, kept = front(doc_lengths, norms, x, proj, sort)
+    proj, up, down, sort, norms, normed, qkv, skv, tkv, means, kept = (
+        front_near if near else front_plain
+    )(doc_lengths, x, *states[::3])
     y, hidden_grad, gq, gkv, gskv, gup, gdown, gout, gnorm_two = middle(
         doc_lengths, norms, x, cot, qkv, skv, proj, up, down
     )
-    gx, gqkv, gsort, gnorm_one = back(
-        norms, gskv, tkv, kept, means, proj, sort, x, normed, hidden_grad, gq, gkv
-    )
-    sums = (reduce if near else reduce_plain)(gqkv, gout, gup, gdown, gsort, gnorm_one, gnorm_two)
+    ins = (norms, gskv, tkv, kept, means, proj, sort, x, normed, hidden_grad, gq, gkv)
+    gx, *sums = (back_near if near else back_plain)(ins, gout, gup, gdown, gnorm_two)
     return (y[None], gx[None], *update(sums, states))
 
 

time: 314 us -> 259 us (0.82)
  Pallas kernels: 309 us -> 250 us
  local copies, waits for them, and re-layouts: 0.6 us -> 7.76 us
  other arithmetic: 3.22 us -> 0 us
    pallas_call x4 -> x2, Pallas kernels: 199 us -> 140 us  [the longest x1 72.3 us: back_near(): pl.pallas_call(back_near_kernel, out_shape=(jax.ShapeDtypeStruct((seq, wi...]
    unnamed x0 -> x1, local copies, waits for them, and re-layouts: none -> 7.76 us
where the time goes in v3:
time: 259 us
  Pallas kernels  250 us (97%)
  local copies, waits for them, and re-layouts  7.76 us (3%)
    pallas_call x1, Pallas kernels, middle(): pl.pallas_call(middle_kernel, grid=(tiles,), out_shape=(jax.ShapeDtypeStr...  107 us
    pallas_call x1, Pallas kernels, back_near(): pl.pallas_call(back_near_kernel, out_shape=(jax.ShapeDtypeStruct((seq, wi...  72.3 us
    pallas_call x1, Pallas kernels, front_near(): pl.pallas_call(front_near_kernel, out_shape=tuple(fulls) + shapes, in_spe...  67.8 us
    unnamed x1, local copies, waits for them, and re-layouts  7.76 us

profile of v3, /device:TPU:0, one launch (start us, length us, event | category | flops | bytes accessed | tf_op | source)
XLA Modules:
  0.0 258.5 jit_solution(1995218905295765864)
XLA Ops:
  0.7 67.8 %front.1 = (bf16[4,2,2,2,16,2048]{5,4,3,2,1,0:T(8,128)(2,1)}, bf16[4,2,2,2,16,2048]{5,4,3,2,1,0:T(8,128)(2,1)}, bf16[4,2,2,2,64,512]{5,4,3,2,1,0:T(8,128)(2,1)},...) custom-call(s32[1,8]{1,0:T(1,128)} %lengths_ref.3, ...), custom_call_target="tpu_custom_call" | custom-call | tf_op jit(solution)/shard_map/front/pallas_call | solution.py:483
  68.5 107.2 %middle.1 = (bf16[4096,512]{1,0:T(8,128)(2,1)}, f32[4096,512]{1,0:T(8,128)}, bf16[4096,512]{1,0:T(8,128)(2,1)}, bf16[4096,1024]{1,0:T(8,128)(2,1)}, bf16[4096,10...) custom-call(s32[1,8]{1,0:T(1,128)} %lengths_ref.3, ...), custom_call_target="tpu_custom_call" | custom-call | tf_op jit(solution)/shard_map/middle/pallas_call | solution.py:681
  175.7 72.3 %back.1 = (f32[4096,512]{1,0:T(8,128)}, bf16[4096,1024]{1,0:T(8,128)(2,1)}, f32[16,2048]{1,0:T(8,128)}, f32[16,2048]{1,0:T(8,128)}, f32[64,512]{1,0:T(8,128)}, /*index=5*/f32[16,128]{1,0:T(8,128)}, f32[4,16]{1,0:T(4,128)}) custom-call(f32[4,512]{1,0:T(4,128)} %get-tuple-element.58.norms_ref.refs_0_, bf16[4096,1024]{1,0:T(8,128)(2,1)} %get-tuple-element.65.refs_1_, ...), custom_call_target="tpu_custom_call" | custom-call | tf_op jit(solution)/shard_map/back/pallas_call | solution.py:1117
  248.0 2.7 %update.1 = (f32[16,2048]{1,0:T(8,128)}, f32[16,2048]{1,0:T(8,128)}, f32[16,2048]{1,0:T(8,128)}, f32[16,2048]{1,0:T(8,128)}, f32[16,2048]{1,0:T(8,128)}, /*index...) custom-call(f32[16,2048]{1,0:T(8,128)} %get-tuple-element.79.refs_0_, ...), custom_call_target="tpu_custom_call" | custom-call | tf_op jit(solution)/shard_map/update/pallas_call | solution.py:1162
  250.8 7.8 %copy.36 = f32[1,4096,512]{2,1,0:T(8,128)} copy(f32[1,4096,512]{2,1,0:T(8,128)} %bitcast.13) | data formatting | bytes 16777216

commit v4 on v3

--- a/solution.py
+++ b/solution.py
@@ -87,34 +87,28 @@
     return (z + 1 - 2 * (z % 2), (z + 2) % 4, 3 - z)
 
 
+def xy_others(x, y):
+    return ((1 - x, y), (x, 1 - y), (1 - x, 1 - y))
+
+
 def neighbours():
     z, x, y, c = coordinates()
-    others = [device_of(one, x, y, c) for one in z_others(z)]
-    return others + [
-        device_of(z, 1 - x, y, c), device_of(z, x, 1 - y, c), device_of(z, x, y, 1 - c)
-    ]
-
-
-def meet_neighbours():
-    barrier = pltpu.get_barrier_semaphore()
-    peers = neighbours()
-    for peer in peers:
-        pl.semaphore_signal(barrier, inc=1, device_id=peer, device_id_type=MESH_ID)
-    pl.semaphore_wait(barrier, len(peers))
-
-
-def halves(shape):
-    if shape[-1] > LANES:
-        middle_column = shape[-1] // 2
-        return (
-            (slice(None), pl.ds(0, middle_column)),
-            (slice(None), pl.ds(middle_column, middle_column)),
+    return (
+        [device_of(one, x, y, c) for one in z_others(z)]
+        + [device_of(z, *one, c) for one in xy_others(x, y)]
+        + [device_of(z, x, y, 1 - c)]
+    )
+
+
+def greet_neighbours():
+    for peer in neighbours():
+        pl.semaphore_signal(
+            pltpu.get_barrier_semaphore(), inc=1, device_id=peer, device_id_type=MESH_ID
         )
-    middle_row = shape[-2] // 2
-    return (
-        (pl.ds(0, middle_row), slice(None)),
-        (pl.ds(middle_row, middle_row), slice(None)),
-    )
+
+
+def await_neighbours():
+    pl.semaphore_wait(pltpu.get_barrier_semaphore(), len(neighbours()))
 
 
 def remote(source, target, sems, index, device):
@@ -125,13 +119,13 @@
     )
 
 
-def gather_stages(full, sems, base):
+def gather_stages(full, sems, base, start=0, size=None):
     z, x, y, c = coordinates()
-    first, second = halves(full.shape)
+    whole = (slice(None), pl.ds(start, size or full.shape[-1]))
     every = slice(None)
 
     def same(index, place, device):
-        part = full.at[place]
+        part = full.at[place + whole]
         return remote(part, part, sems, base + index, device)
 
     def stage_z():
@@ -139,20 +133,50 @@
             same(k, (z, x, y, c), device_of(one, x, y, c)) for k, one in enumerate(z_others(z))
         ]
 
+    def stage_xy():
+        return [
+            same(3 + k, (every, x, y, c), device_of(z, *one, c))
+            for k, one in enumerate(xy_others(x, y))
+        ]
+
+    def stage_core():
+        return [same(6, (every, every, every, c), device_of(z, x, y, 1 - c))]
+
+    return [stage_z, stage_xy, stage_core]
+
+
+def gather_by_halves(full, sems, base, start=0, size=None):
+    z, x, y, c = coordinates()
+    size = size or full.shape[-1]
+    every = slice(None)
+    first = (every, pl.ds(start, size // 2))
+    second = (every, pl.ds(start + size // 2, size // 2))
+    whole = (every, pl.ds(start, size))
+    to_x, to_y = device_of(z, 1 - x, y, c), device_of(z, x, 1 - y, c)
+
+    def same(index, place, device):
+        part = full.at[place]
+        return remote(part, part, sems, base + index, device)
+
+    def stage_z():
+        return [
+            same(k, (z, x, y, c) + whole, device_of(one, x, y, c))
+            for k, one in enumerate(z_others(z))
+        ]
+
     def stage_one():
         return [
-            same(3, (every, x, y, c) + first, device_of(z, 1 - x, y, c)),
-            same(4, (every, x, y, c) + second, device_of(z, x, 1 - y, c)),
+            same(3, (every, x, y, c) + first, to_x), same(4, (every, x, y, c) + second, to_y)
         ]
 
     def stage_two():
         return [
-            same(5, (every, every, y, c) + first, device_of(z, x, 1 - y, c)),
-            same(6, (every, x, every, c) + second, device_of(z, 1 - x, y, c)),
+            same(5, (every, every, y, c) + first, to_y),
+            same(6, (every, x, every, c) + second, to_x),
         ]
 
     def stage_core():
-        return [same(7, (every, every, every, c), device_of(z, x, y, 1 - c))]
+        return [same(7, (every, every, every, c) + whole, device_of(z, x, y, 1 - c))]
 
     return [stage_z, stage_one, stage_two, stage_core]
 
@@ -211,57 +235,79 @@
         return lambda *unused: None
 
 
+GATHERS = 6
+
+
 class GatherSteps:
     def __init__(self, proj, up, down, small, sems):
-        fulls = (proj, up, down, small)
-        self.proj, self.up, self.down, self.small = [
-            gather_stages(full, sems, COPIES * b) for b, full in enumerate(fulls)
+        width = proj.shape[-1] // 4
+        pieces = [(small, 0, None)]
+        pieces += [(proj, width, 2 * width), (proj, 0, width), (proj, 3 * width, width)]
+        pieces += [(up, 0, None), (down, 0, None)]
+        plans = [
+            (gather_stages if b < 3 else gather_by_halves)(piece[0], sems, COPIES * b, *piece[1:])
+            for b, piece in enumerate(pieces)
         ]
-
-    def start(self, plan, step):
-        start_all(plan[step]())
+        self.small, self.pair, self.queries, self.out, self.up, self.down = plans
+
+    def start(self, plan):
+        start_all(plan[0]())
 
     def turn(self, plan, step):
         wait_all(plan[step]())
-        if step < 3:
+        if step + 1 < len(plan):
             start_all(plan[step + 1]())
 
-    def begin(self):
-        self.start(self.small, 0)
-        self.start(self.proj, 0)
-        for step in range(4):
-            self.turn(self.small, step)
-        self.turn(self.proj, 0)
+    def centred(self, quarter):
+        if quarter == 0:
+            await_neighbours()
+            self.start(self.small)
+            self.start(self.pair)
+        else:
+            self.turn(self.small, quarter - 1)
+        if quarter == 1:
+            self.turn(self.pair, 0)
+        if quarter == 2:
+            self.start(self.queries)
+        if quarter == 3:
+            self.start(self.up)
+            self.start(self.out)
 
     def half_normed(self):
-        self.turn(self.proj, 1)
-        self.start(self.up, 0)
-
-    def all_normed(self):
-        self.turn(self.proj, 2)
+        self.turn(self.queries, 0)
+        self.start(self.down)
+        self.turn(self.pair, 1)
 
     def before_project(self):
-        self.turn(self.proj, 3)
-        self.turn(self.up, 0)
-        self.start(self.down, 0)
+        self.turn(self.pair, 2)
 
     def project(self, k):
-        self.when(k, 2, self.up, 1)
-        self.when(k, 5, self.up, 2)
-        self.when(k, 6, self.down, 0)
+        self.when(k, 1, self.queries, 1)
+        self.when(k, 2, self.up, 0)
+        self.when(k, 2, self.out, 0)
+        self.when(k, 3, self.queries, 2)
+        self.when(k, 4, self.down, 0)
+        self.when(k, 6, self.up, 1)
+        self.when(k, 7, self.out, 1)
 
     def sort(self, i):
-        self.when(i, 2, self.down, 1)
+        self.when(i, 1, self.down, 1)
+        self.when(i, 5, self.up, 2)
+        self.when(i, 6, self.out, 2)
 
     def low(self, k):
-        self.when(k, 0, self.up, 3)
-        self.when(k, 2, self.down, 2)
+        self.when(k, 3, self.down, 2)
+        self.when(k, 5, self.up, 3)
+        self.when(k, 6, self.out, 3)
 
     def end(self):
         self.turn(self.down, 3)
 
     def when(self, k, place, plan, step):
-        pl.when(k == place)(functools.partial(self.turn, plan, step))
+        if step < 0:
+            pl.when(k == place)(functools.partial(self.start, plan))
+        else:
+            pl.when(k == place)(functools.partial(self.turn, plan, step))
 
 
 def front_near_kernel(
@@ -269,6 +315,7 @@
     proj, up, down, sort_ref, norms_ref, *rest,
 ):
     rest, (small, send, recv) = rest[:-3], rest[-3:]
+    greet_neighbours()
     mine = coordinates()
     proj[mine] = proj_own[...].astype(bf16)
     up[mine] = up_own[...].astype(bf16)
@@ -280,19 +327,21 @@
     lift = one_hot((16, 4), lambda r, l: r, lambda r, l: l * 4 + quarter)
     tile = dot(lift.astype(f32).astype(bf16), lanes).astype(bf16)
     small[mine] = jnp.concatenate([sort_own[...].astype(bf16), tile], axis=0)
-    meet_neighbours()
     steps = GatherSteps(proj, up, down, small, (send, recv))
-    steps.begin()
-    pieces = small[...].reshape(-1, 32, LANES)
-    sort_ref[...] = pieces[:, :16].reshape(sort_ref.shape)
-    tile = jnp.sum(pieces[:, 16:].astype(f32), axis=0)
-    norms_ref[...] = jnp.concatenate(
-        [
-            jnp.concatenate([tile[4 * i + q : 4 * i + q + 1] for q in range(4)], axis=1)
-            for i in range(4)
-        ],
-        axis=0,
-    )
+
+    def arrived():
+        pieces = small[...].reshape(-1, 32, LANES)
+        sort_ref[...] = pieces[:, :16].reshape(sort_ref.shape)
+        tile = jnp.sum(pieces[:, 16:].astype(f32), axis=0)
+        norms_ref[...] = jnp.concatenate(
+            [
+                jnp.concatenate([tile[4 * i + q : 4 * i + q + 1] for q in range(4)], axis=1)
+                for i in range(4)
+            ],
+            axis=0,
+        )
+
+    steps.arrived = arrived
 
     def columns_of(columns):
         return proj[:, :, :, :, :, columns].reshape(x_ref.shape[1], -1)
@@ -309,7 +358,8 @@
 def front_steps(
     steps, proj_columns, lengths_ref, norms_ref, x_ref, sort_ref,
     normed_hbm, qkv_hbm, skv_hbm, tkv_hbm, means_ref, states_ref,
-    normed_s, stage, matrix, qkv_buf, low_buf, flip_buf, copy_sem, qkv_sem, low_sem, flip_sem,
+    normed_s, stage, matrix, pair_buf, query_buf, low_buf, flip_buf,
+    copy_sem, pair_sem, query_sem, low_sem, flip_sem,
 ):
     seq, width = x_ref.shape
     tiles = seq // TILE
@@ -317,12 +367,24 @@
     per_tile = TILE // BLOCK
     chunks = 2 * width // LANES
     ends = doc_ends(lengths_ref)
+    def centre_step(k, carry):
+        rows = pl.ds(pl.multiple_of(k * TILE, TILE), TILE)
+        xhat, unused = center_scale(x_ref[rows, :].astype(f32))
+        stage[pl.ds(k * (TILE // blocks), TILE // blocks), :, :width] = xhat.reshape(
+            TILE // blocks, blocks, width
+        )
+        return carry
+
+    for quarter in range(4):
+        lax.fori_loop(quarter * tiles // 4, (quarter + 1) * tiles // 4, centre_step, 0)
+        steps.centred(quarter)
+    steps.arrived()
     gain = norms_ref[0:1, :].astype(f32)
     shift = norms_ref[1:2, :].astype(f32)
 
     def norm_step(k, carry):
         rows = pl.ds(pl.multiple_of(k * TILE, TILE), TILE)
-        xhat, unused = center_scale(x_ref[rows, :].astype(f32))
+        xhat = stage[pl.ds(k * (TILE // blocks), TILE // blocks), :, :width].reshape(TILE, width)
         normed = (xhat * gain + shift).astype(bf16)
         normed_s[rows, :] = normed
         sums = jnp.sum(normed.astype(f32).reshape(per_tile, BLOCK, width), axis=1)
@@ -334,7 +396,6 @@
     lax.fori_loop(0, tiles // 2, norm_step, 0)
     steps.half_normed()
     lax.fori_loop(tiles // 2, tiles, norm_step, 0)
-    steps.all_normed()
     normed_copy = pltpu.make_async_copy(normed_s, normed_hbm, copy_sem)
     normed_copy.start()
 
@@ -343,9 +404,13 @@
     first_j = segments_of(lax.broadcasted_iota(jnp.int32, (blocks, blocks), 1) * BLOCK, ends)
     logits = jnp.where(first_i != first_j, logits - mask_penalty, logits)
 
-    def qkv_copy(k, slot):
-        rows = pl.ds(pl.multiple_of(k * TILE, TILE), TILE)
-        return pltpu.make_async_copy(qkv_buf.at[slot], qkv_hbm.at[rows, :], qkv_sem.at[slot])
+    def pair_copy(k, slot):
+        place = (pl.ds(pl.multiple_of(k * TILE, TILE), TILE), pl.ds(width, 2 * width))
+        return pltpu.make_async_copy(pair_buf.at[slot], qkv_hbm.at[place], pair_sem.at[slot])
+
+    def query_copy(k, slot):
+        place = (pl.ds(pl.multiple_of(k * TILE, TILE), TILE), pl.ds(0, width))
+        return pltpu.make_async_copy(query_buf.at[slot], qkv_hbm.at[place], query_sem.at[slot])
 
     def project_step(k, logits):
         rows = pl.ds(pl.multiple_of(k * TILE, TILE), TILE)
@@ -353,7 +418,7 @@
 
         @pl.when(k >= 2)
         def _():
-            qkv_copy(k - 2, slot).wait()
+            pair_copy(k - 2, slot).wait()
 
         steps.project(k)
         logits = logits - log_sum_exp(logits, 1)
@@ -361,14 +426,13 @@
         logits = logits - log_sum_exp(logits, 0)
         states_ref[2 * k + 1] = jnp.exp(logits)
         normed = normed_s[rows, :]
-        qkv_buf[slot, :, :width] = dot(normed, proj_columns(slice(0, width))).astype(bf16)
         product = dot(normed, proj_columns(slice(width, 3 * width))).astype(bf16)
-        qkv_buf[slot, :, width:] = product
+        pair_buf[slot] = product
         spread_tokens(stage, matrix[...], k, product)
-        qkv_copy(k, slot).start()
+        pair_copy(k, slot).start()
         return logits
 
-    assert tiles == SINK_ITERS
+    assert tiles == SINK_ITERS == BLOCK // flip_buf.shape[0]
     steps.before_project()
     matrix[...] = regroup_matrix(False)
     lax.fori_loop(0, tiles, project_step, logits)
@@ -380,6 +444,15 @@
     def sort_step(i, carry):
         group = flip_buf.shape[0]
         steps.sort(i)
+        rows = pl.ds(pl.multiple_of(i * TILE, TILE), TILE)
+        slot = lax.rem(i, 2)
+
+        @pl.when(i >= 2)
+        def _():
+            query_copy(i - 2, slot).wait()
+
+        query_buf[slot] = dot(normed_s[rows, :], proj_columns(slice(0, width))).astype(bf16)
+        query_copy(i, slot).start()
 
         @pl.when(i >= 1)
         def _():
@@ -422,7 +495,8 @@
     for u in range(group):
         flip_copy(BLOCK - group + u, u).wait()
     for k in (tiles - 2, tiles - 1):
-        qkv_copy(k, k % 2).wait()
+        pair_copy(k, k % 2).wait()
+        query_copy(k, k % 2).wait()
         low_copy(k, k % 2).wait()
     normed_copy.wait()
     steps.end()
@@ -444,10 +518,12 @@
             pltpu.VMEM((seq, width), bf16),
             pltpu.VMEM((BLOCK, blocks, 2 * width), f32),
             pltpu.VMEM((GROUP, GROUP), bf16),
-            pltpu.VMEM((2, TILE, 3 * width), bf16),
+            pltpu.VMEM((2, TILE, 2 * width), bf16),
+            pltpu.VMEM((2, TILE, width), bf16),
             pltpu.VMEM((2, TILE, 2 * width), bf16),
             pltpu.VMEM((4, 2 * width, blocks), bf16),
             pltpu.SemaphoreType.DMA,
+            pltpu.SemaphoreType.DMA((2,)),
             pltpu.SemaphoreType.DMA((2,)),
             pltpu.SemaphoreType.DMA((2,)),
             pltpu.SemaphoreType.DMA((8,)),
@@ -479,7 +555,7 @@
     fulls += [jax.ShapeDtypeStruct((32 * sort.shape[0], LANES), bf16)]
     fulls += [jax.ShapeDtypeStruct((4, width), f32)]
     scratch = scratch + [pltpu.VMEM(SPLIT + (32, LANES), bf16)]
-    scratch += [pltpu.SemaphoreType.DMA((4 * COPIES,))] * 2
+    scratch += [pltpu.SemaphoreType.DMA((GATHERS * COPIES,))] * 2
     results = pl.pallas_call(
         front_near_kernel,
         out_shape=tuple(fulls) + shapes,
@@ -613,8 +689,8 @@
     hidden_grad = cot.astype(f32) + layer_norm_back(
         grad_normed_two, gain_two, xhat_two, inverse_two
     )
-    hidden_grad_ref[...] = hidden_grad
     grad_attn = hidden_grad.astype(bf16)
+    hidden_grad_ref[...] = grad_attn
     gout[...] += dot_tn(context, grad_attn)
     gcontext_s[...] = dot_nt(grad_attn, out_proj_ref[...]).astype(bf16)
 
@@ -683,7 +759,7 @@
         grid=(tiles,),
         out_shape=(
             jax.ShapeDtypeStruct((seq, width), bf16),
-            jax.ShapeDtypeStruct((seq, width), f32),
+            jax.ShapeDtypeStruct((seq, width), bf16),
             jax.ShapeDtypeStruct((seq, width), bf16),
             jax.ShapeDtypeStruct((seq, 2 * width), bf16),
             jax.ShapeDtypeStruct((seq, 2 * width), bf16),
@@ -736,35 +812,29 @@
 
 
 class Reduce:
-    def __init__(self, part, total, columns, got_c, got_a, got_b, got_two, got_z, sems, base):
+    def __init__(self, part, total, columns, got_c, got_xy, got_z, sems, base):
         self.part, self.total, self.columns = part, total, columns
-        self.got_c, self.got_a, self.got_b = got_c, got_a, got_b
-        self.got_two, self.got_z, self.sems, self.base = got_two, got_z, sems, base
-        self.first, self.second = halves(part.shape)
+        self.whole = (slice(None), columns)
+        self.got_c, self.got_xy, self.got_z = got_c, got_xy, got_z
+        self.sems, self.base = sems, base
 
     def copies(self, step):
         z, x, y, c = coordinates()
         every = slice(None)
-        to_x, to_y = device_of(z, 1 - x, y, c), device_of(z, x, 1 - y, c)
 
         def one(source, target, index, device):
             return remote(source, target, self.sems, self.base + index, device)
 
         if step == 0:
-            away = self.part.at[every, every, every, 1 - c]
+            away = self.part.at[(every, every, every, 1 - c) + self.whole]
             return [one(away, self.got_c, 0, device_of(z, x, y, 1 - c))]
         if step == 1:
-            away_a = self.got_c.at[(every, every, 1 - y) + self.first]
-            away_b = self.got_c.at[(every, 1 - x, every) + self.second]
-            return [one(away_a, self.got_a, 1, to_y), one(away_b, self.got_b, 2, to_x)]
-        if step == 2:
-            away_a, away_b = self.got_a.at[every, 1 - x], self.got_b.at[every, 1 - y]
             return [
-                one(away_a, self.got_two.at[(every,) + self.first], 3, to_x),
-                one(away_b, self.got_two.at[(every,) + self.second], 4, to_y),
+                one(self.got_c.at[(every,) + other], self.got_xy.at[k], 1 + k, device_of(z, *other, c))
+                for k, other in enumerate(xy_others(x, y))
             ]
         return [
-            one(self.got_two.at[other], self.got_z.at[k], 5 + k, device_of(other, x, y, c))
+            one(self.got_c.at[other, x, y], self.got_z.at[k], 4 + k, device_of(other, x, y, c))
             for k, other in enumerate(z_others(z))
         ]
 
@@ -774,14 +844,14 @@
     def turn(self, step):
         wait_all(self.copies(step))
         self.add(step)
-        if step < 3:
+        if step < 2:
             self.start(step + 1)
 
     def add(self, step):
         z, x, y, c = coordinates()
-        if step == 3:
+        if step == 2:
             self.total[:, self.columns] = add_low(
-                self.got_two[z], *[self.got_z[k] for k in range(3)]
+                self.got_c[z, x, y], *[self.got_z[k] for k in range(3)]
             )
             return
 
@@ -790,22 +860,11 @@
                 for j in range(2):
                     for k in range(2):
                         self.got_c[i, j, k] = add_low(
-                            self.part[i, j, k, c], self.got_c[i, j, k]
+                            self.part[(i, j, k, c) + self.whole], self.got_c[i, j, k]
                         ).astype(bf16)
-            elif step == 1:
-                for j in range(2):
-                    self.got_a[i, j] = add_low(
-                        self.got_c[(i, j, y) + self.first], self.got_a[i, j]
-                    ).astype(bf16)
-                    self.got_b[i, j] = add_low(
-                        self.got_c[(i, x, j) + self.second], self.got_b[i, j]
-                    ).astype(bf16)
             else:
-                self.got_two[(i,) + self.first] = add_low(
-                    self.got_a[i, x], self.got_two[(i,) + self.first]
-                ).astype(bf16)
-                self.got_two[(i,) + self.second] = add_low(
-                    self.got_b[i, y], self.got_two[(i,) + self.second]
+                self.got_c[i, x, y] = add_low(
+                    self.got_c[i, x, y], *[self.got_xy[k, i] for k in range(3)]
                 ).astype(bf16)
             return carry
 
@@ -813,49 +872,57 @@
 
 
 def reduce_scratch(rows, columns):
-    half = (rows, columns // 2) if columns > LANES else (rows // 2, columns)
-    shapes = (
-        (4, 2, 2, rows, columns), (4, 2) + half, (4, 2) + half, (4, rows, columns),
-        (3, rows, columns),
-    )
+    shapes = ((4, 2, 2, rows, columns), (3, 4, rows, columns), (3, rows, columns))
     return [pltpu.VMEM(shape, bf16) for shape in shapes]
 
 
 class ReduceSteps:
-    def __init__(self, qkv, out, up, down, small):
-        self.qkv, self.out, self.up, self.down, self.small = qkv, out, up, down, small
+    def __init__(self, plans):
+        self.up, self.down, self.out, self.query = plans
 
     def begin(self):
+        pass
+
+    def send(self):
+        await_neighbours()
         self.up.start(0)
         self.down.start(0)
         self.out.start(0)
 
+    def during_query(self, k):
+        pl.when(k == 1)(self.send)
+        self.when(k, 4, self.up, 0)
+        self.when(k, 7, self.down, 0)
+
+    def queried(self):
+        self.query.start(0)
+        self.out.turn(0)
+
+    def load(self, k):
+        self.when(k, 4, self.query, 0)
+
     def loaded(self):
-        self.up.turn(0)
+        pass
 
     def sort(self, i):
-        self.when(i, 5, self.up, 1)
-        self.when(i, 6, self.down, 0)
+        self.when(i, 4, self.up, 1)
 
     def swept(self):
+        self.down.turn(1)
         self.up.turn(2)
 
-    def first(self, k):
-        self.when(k, 1, self.down, 1)
-        self.when(k, 2, self.out, 0)
-        self.when(k, 4, self.down, 2)
-        self.when(k, 6, self.up, 3)
-        self.when(k, 7, self.out, 1)
-
-    def between(self):
-        self.qkv.start(0)
+    def weights(self, k):
+        self.when(k, 1, self.out, 1)
+        self.when(k, 2, self.query, 1)
+        self.when(k, 5, self.down, 2)
+
+    def end(self):
         self.out.turn(2)
 
-    def second(self, k):
-        self.when(k, 1, self.down, 3)
-        self.when(k, 2, self.qkv, 0)
-        self.when(k, 3, self.out, 3)
-        self.when(k, 6, self.qkv, 1)
+    def inputs(self, k, pair):
+        self.when(k, 2, pair, 0)
+        self.when(k, 4, self.query, 2)
+        self.when(k, 7, pair, 1)
 
     def when(self, k, place, plan, step):
         pl.when(k == place)(functools.partial(plan.turn, step))
@@ -870,45 +937,59 @@
     return jnp.concatenate(rows, axis=0)
 
 
-def back_plain_kernel(*refs):
-    back_steps(Quiet(), *refs)
-
-
 def back_near_kernel(*refs):
-    ins, refs = refs[:12], refs[12:]
-    (gout, gup, gdown, gnorm_two), refs = refs[:4], refs[4:]
-    (gx_hbm, gsum_hbm, proj_sum, up_sum, down_sum, sort_sum, norm_sum), refs = refs[:7], refs[7:]
-    work, refs = refs[:9], refs[9:]
-    (gqkv, gsort, gnorm, small, small_sum, send, recv), scratch = refs[:7], refs[7:]
-    width = gsort.shape[0]
-    sems = (send, recv)
+    ins, refs = refs[:8], refs[8:]
+    (gout, gup, gdown, gtwo_ref, norms_ref, proj_ref, x_hbm), refs = refs[:7], refs[7:]
+    gx_hbm, refs = refs[0], refs[1:]
+    (query_sum, pair_sum, out_sum, up_sum, down_sum, sort_sum, norm_sum), refs = refs[:7], refs[7:]
+    work, refs = refs[:8], refs[8:]
+    (gsum, gpair, gsort, gmeans, gquery, gone_ref, small, small_sum), refs = refs[:8], refs[8:]
+    (send, recv), scratch = refs[:2], refs[2:]
+    greet_neighbours()
     every = slice(None)
     places = (
-        (gqkv, proj_sum, pl.ds(0, 3 * width)), (gout, proj_sum, pl.ds(3 * width, width)),
-        (gup, up_sum, every), (gdown, down_sum, every), (small, small_sum, every),
+        (gup, up_sum, every), (gdown, down_sum, every), (gout, out_sum, every),
+        (gquery, query_sum, every), (gpair, pair_sum, every), (small, small_sum, every),
     )
-    steps = ReduceSteps(
-        *[
-            Reduce(part, total, columns, *scratch[5 * b : 5 * b + 5], sems, COPIES * b)
-            for b, (part, total, columns) in enumerate(places)
-        ]
-    )
-    meet_neighbours()
-    back_steps(steps, *ins, gx_hbm, gsum_hbm, gqkv, gsort, gnorm, *work)
-    tile = norm_rows((gnorm[...], gnorm_two[...])).astype(bf16)
-    shards = gsort[...].astype(bf16).reshape(SPLIT + (width // 32, LANES))
-    small[:, :, :, :, :16] = shards
+    plans = [
+        Reduce(*place, *scratch[3 * b : 3 * b + 3], (send, recv), COPIES * b)
+        for b, place in enumerate(places)
+    ]
+    pair, small_plan = plans[4:]
+    steps = ReduceSteps(plans[:4])
+    back_steps(steps, *ins, gsum, gpair, gsort, gmeans, gquery, *work)
+    pair.start(0)
+    seq, width = x_hbm.shape
+    gone_ref[...] = jnp.zeros_like(gone_ref)
+
+    def input_step(x_ref, gq_ref, gx_ref):
+        k = pl.program_id(0)
+        steps.inputs(k, pair)
+        part = TILE // BLOCK
+        means = gmeans[pl.ds(pl.multiple_of(k * part, part), part), :]
+        gkv = gsum[pl.ds(pl.multiple_of(k * TILE, TILE), TILE), :]
+        input_tile(norms_ref, x_ref, gq_ref, gkv, means, proj_ref, gx_ref, gone_ref)
+
+    def rows_of(columns):
+        return pl.BlockSpec((TILE, columns), lambda i: (i, 0))
+
+    pltpu.emit_pipeline(
+        input_step,
+        grid=(seq // TILE,),
+        in_specs=[rows_of(width)] * 2,
+        out_specs=[rows_of(width)],
+    )(x_hbm, ins[6], gx_hbm)
+    tile = norm_rows((gone_ref[...], gtwo_ref[...])).astype(bf16)
+    small[:, :, :, :, :16] = gsort[...].astype(bf16).reshape(SPLIT + (width // 32, LANES))
     for i in range(4):
         for j in range(2):
             for k in range(2):
                 for m in range(2):
                     small[i, j, k, m, 16:] = tile
-    steps.small.start(0)
-    steps.small.turn(0)
-    steps.qkv.turn(2)
-    for step in range(1, 4):
-        steps.small.turn(step)
-    steps.qkv.turn(3)
+    small_plan.start(0)
+    for step in range(3):
+        small_plan.turn(step)
+    pair.turn(2)
     sort_sum[...] = small_sum[:16, :]
     quarter, eighth = norm_place()
     own = norm_sum.shape[1]
@@ -924,14 +1005,18 @@
     norm_sum[...] = exact(exact(drop, small_sum[16:, :]), pick)
 
 
+def back_plain_kernel(*refs):
+    back_steps(Quiet(), *refs)
+
+
 def back_steps(
-    steps, norms_ref, gskv_hbm, tkv_hbm, states_ref, means_ref, proj_ref, sort_ref,
-    x_hbm, normed_hbm, hidden_grad_hbm, gq_hbm, gkv_hbm,
-    gx_hbm, gsum_hbm, gproj_ref, gsort_ref, gnorm_ref,
-    stage, matrix, low_buf, flip_buf, gproj, gperm, gmeans, low_sem, flip_sem,
+    steps, gskv_hbm, tkv_hbm, states_ref, means_ref, sort_ref,
+    normed_hbm, gq_hbm, gkv_hbm,
+    gsum, gpair_ref, gsort_ref, gmeans, gquery_ref,
+    stage, matrix, low_buf, flip_buf, gproj, gperm, low_sem, flip_sem,
 ):
     steps.begin()
-    seq, width = x_hbm.shape
+    seq, width = normed_hbm.shape
     tiles = seq // TILE
     blocks = seq // BLOCK
     chunks = 2 * width // LANES
@@ -955,6 +1040,7 @@
         rows = pl.ds(pl.multiple_of(k * TILE, TILE), TILE)
         slot = lax.rem(k, 2)
         low_copy(k, slot).wait()
+        steps.load(k)
         spread_tokens(stage, matrix[...], k, low_buf[slot])
 
         @pl.when(k + 2 < tiles)
@@ -963,6 +1049,20 @@
 
         return carry
 
+    def rows_of(columns):
+        return pl.BlockSpec((TILE, columns), lambda i: (i, 0))
+
+    gproj[...] = jnp.zeros_like(gproj)
+
+    def query_step(normed_ref, gq_ref):
+        steps.during_query(pl.program_id(0))
+        gproj[:, :width] += dot_tn(normed_ref[...], gq_ref[...])
+
+    pltpu.emit_pipeline(query_step, grid=(tiles,), in_specs=[rows_of(width)] * 2)(
+        normed_hbm, gq_hbm
+    )
+    gquery_ref[...] = gproj[:, :width].astype(bf16).reshape(gquery_ref.shape)
+    steps.queried()
     matrix[...] = regroup_matrix(False)
     lax.fori_loop(0, tiles, load_step, 0)
     matrix[...] = regroup_matrix(True)
@@ -1005,51 +1105,21 @@
     gsort_ref[...] = dot_tn(means_ref[...], grad).astype(gsort_ref.dtype)
     gmeans[...] = dot_nt(grad, sort_ref[...]) * (1.0 / BLOCK)
     steps.swept()
-    gproj[...] = jnp.zeros_like(gproj)
-    gnorm_ref[...] = jnp.zeros_like(gnorm_ref)
-    gain = norms_ref[0:1, :].astype(f32)
-
-    def weight_step(normed_ref, gq_ref, gkv_ref, gsum_ref):
+
+    def weight_step(normed_ref, gkv_ref):
         k = pl.program_id(0)
-        steps.first(k)
-        far = collect_tokens(stage, matrix[...], k, TILE)
-        gkv = (gkv_ref[...].astype(f32) + far).astype(bf16)
-        gsum_ref[...] = gkv
-        normed = normed_ref[...]
-        gproj[:, :width] += dot_tn(normed, gq_ref[...])
-        gproj[:, width:] += dot_tn(normed, gkv)
-
-    def input_step(x_ref, hidden_grad_ref, gq_ref, gsum_ref, gx_ref):
-        k = pl.program_id(0)
-        steps.second(k)
-        gq, gkv = gq_ref[...], gsum_ref[...]
-        grad_normed = dot_nt(gq, proj_ref[:, :width]) + dot_nt(gkv, proj_ref[:, width : 3 * width])
-        means = gmeans[pl.ds(pl.multiple_of(k * per_tile, per_tile), per_tile), :]
-        grad_normed = grad_normed + jnp.broadcast_to(
-            means[:, None, :], (per_tile, BLOCK, width)
-        ).reshape(TILE, width)
-        xhat, inverse = center_scale(x_ref[...].astype(f32))
-        gnorm_ref[0:1, :] += jnp.sum(grad_normed * xhat, axis=0, keepdims=True)
-        gnorm_ref[1:2, :] += jnp.sum(grad_normed, axis=0, keepdims=True)
-        gx_ref[...] = hidden_grad_ref[...] + layer_norm_back(grad_normed, gain, xhat, inverse)
-
-    def rows_of(columns):
-        return pl.BlockSpec((TILE, columns), lambda i: (i, 0))
+        steps.weights(k)
+        gkv = (gkv_ref[...].astype(f32) + collect_tokens(stage, matrix[...], k, TILE)).astype(bf16)
+        gsum[pl.ds(pl.multiple_of(k * TILE, TILE), TILE), :] = gkv
+        gproj[:, width:] += dot_tn(normed_ref[...], gkv)
 
     pltpu.emit_pipeline(
         weight_step,
         grid=(tiles,),
-        in_specs=[rows_of(width)] * 2 + [rows_of(2 * width)],
-        out_specs=[rows_of(2 * width)],
-    )(normed_hbm, gq_hbm, gkv_hbm, gsum_hbm)
-    gproj_ref[...] = gproj[...].astype(bf16).reshape(gproj_ref.shape)
-    steps.between()
-    pltpu.emit_pipeline(
-        input_step,
-        grid=(tiles,),
-        in_specs=[rows_of(width)] * 3 + [rows_of(2 * width)],
-        out_specs=[rows_of(width)],
-    )(x_hbm, hidden_grad_hbm, gq_hbm, gsum_hbm, gx_hbm)
+        in_specs=[rows_of(width), rows_of(2 * width)],
+    )(normed_hbm, gkv_hbm)
+    gpair_ref[...] = gproj[:, width:].astype(bf16).reshape(gpair_ref.shape)
+    steps.end()
 
 
 def back_scratch(seq, width):
@@ -1061,75 +1131,141 @@
             pltpu.VMEM((8, 2 * width, blocks), bf16),
             pltpu.VMEM((width, 3 * width), f32),
             pltpu.VMEM((blocks, blocks), f32),
-            pltpu.VMEM((blocks, width), f32),
             pltpu.SemaphoreType.DMA((2,)),
             pltpu.SemaphoreType.DMA((8,)),
     ]
 
 
-def back_plain(ins, gout, gup, gdown, gnorm_two):
-    seq, width = ins[7].shape
-    blocks = seq // BLOCK
+def back_shapes(seq, width):
     hbm = pl.BlockSpec(memory_space=pl.ANY)
     vmem = pl.BlockSpec(memory_space=pltpu.VMEM)
-    gx, unused, gqkv, gsort, gnorm_one = pl.pallas_call(
+    blocks = seq // BLOCK
+    shapes = (
+        jax.ShapeDtypeStruct((seq, 2 * width), bf16),
+        jax.ShapeDtypeStruct((width, 2 * width), bf16),
+        jax.ShapeDtypeStruct((width, blocks), f32),
+        jax.ShapeDtypeStruct((blocks, width), f32),
+    )
+    return shapes, [hbm, hbm, vmem, vmem, vmem, hbm, hbm, hbm], [vmem, vmem, vmem, vmem]
+
+
+def back_plain(seq, width, ins, gout, gup, gdown):
+    shapes, in_specs, out_specs = back_shapes(seq, width)
+    gsum, gpair, gsort, gmeans, gquery = pl.pallas_call(
         back_plain_kernel,
-        out_shape=(
-            jax.ShapeDtypeStruct((seq, width), f32),
-            jax.ShapeDtypeStruct((seq, 2 * width), bf16),
-            jax.ShapeDtypeStruct((width, 3 * width), bf16),
-            jax.ShapeDtypeStruct((width, blocks), f32),
-            jax.ShapeDtypeStruct((2, width), f32),
-        ),
-        in_specs=[vmem, hbm, hbm, vmem, vmem, vmem, vmem, hbm, hbm, hbm, hbm, hbm],
-        out_specs=[hbm, hbm, vmem, vmem, vmem],
+        out_shape=shapes + (jax.ShapeDtypeStruct((width, width), bf16),),
+        in_specs=in_specs,
+        out_specs=out_specs + [pl.BlockSpec(memory_space=pltpu.VMEM)],
         scratch_shapes=back_scratch(seq, width),
         compiler_params=pltpu.CompilerParams(vmem_limit_bytes=VMEM_LIMIT),
         name="back",
     )(*ins)
-    return gx, *reduce_plain(gqkv, gout, gup, gdown, gsort, gnorm_one, gnorm_two)
-
-
-def back_near(ins, gout, gup, gdown, gnorm_two):
-    seq, width = ins[7].shape
-    blocks = seq // BLOCK
+    return gsum, gpair, gsort, gmeans, gquery, gout, gup, gdown
+
+
+def split_shards(grad):
+    return grad.reshape(SPLIT + (grad.shape[0] // 32, grad.shape[1]))
+
+
+def back_near(seq, width, ins, gout, gup, gdown, gtwo, norms, proj, x):
+    shapes, in_specs, unused = back_shapes(seq, width)
     hbm = pl.BlockSpec(memory_space=pl.ANY)
     vmem = pl.BlockSpec(memory_space=pltpu.VMEM)
-
-    def split(grad):
-        return grad.reshape(SPLIT + (grad.shape[0] // 32, grad.shape[1]))
-
-    gout, gup, gdown = split(gout), split(gup), split(gdown)
-    rows = width // 32
-    small = (32, LANES)
-    qkv = (rows, 3 * width)
+    gout, gup, gdown = split_shards(gout), split_shards(gup), split_shards(gdown)
+    blocks = seq // BLOCK
+    query, pair, small = (width // 32, width), (width // 32, 2 * width), (32, LANES)
     scratch = back_scratch(seq, width) + [
-        pltpu.VMEM(SPLIT + qkv, bf16),
+        pltpu.VMEM((seq, 2 * width), bf16),
+        pltpu.VMEM(SPLIT + pair, bf16),
         pltpu.VMEM((width, blocks), f32),
+        pltpu.VMEM((blocks, width), f32),
+        pltpu.VMEM(SPLIT + query, bf16),
         pltpu.VMEM((2, width), f32),
         pltpu.VMEM(SPLIT + small, bf16),
         pltpu.VMEM(small, f32),
     ]
-    scratch += [pltpu.SemaphoreType.DMA((5 * COPIES,))] * 2
-    for shape in (qkv, gout.shape[-2:], gup.shape[-2:], gdown.shape[-2:], small):
+    scratch += [pltpu.SemaphoreType.DMA((6 * COPIES,))] * 2
+    for shape in (gup.shape[-2:], gdown.shape[-2:], gout.shape[-2:], query, pair, small):
         scratch += reduce_scratch(*shape)
-    sums = [(rows, 4 * width), gup.shape[-2:], gdown.shape[-2:], (rows, blocks), (4, rows)]
-    gx, unused, *totals = pl.pallas_call(
+    sums = [query, pair, gout.shape[-2:], gup.shape[-2:], gdown.shape[-2:]]
+    sums += [(width // 32, blocks), (4, width // 32)]
+    gx, *totals = pl.pallas_call(
         back_near_kernel,
-        out_shape=(
-            jax.ShapeDtypeStruct((seq, width), f32),
-            jax.ShapeDtypeStruct((seq, 2 * width), bf16),
-            *[jax.ShapeDtypeStruct(shape, f32) for shape in sums],
-        ),
-        in_specs=[vmem, hbm, hbm, vmem, vmem, vmem, vmem, hbm, hbm, hbm, hbm, hbm] + [vmem] * 4,
-        out_specs=[hbm, hbm] + [vmem] * 5,
+        out_shape=(jax.ShapeDtypeStruct((seq, width), bf16),)
+        + tuple(jax.ShapeDtypeStruct(shape, f32) for shape in sums),
+        in_specs=in_specs + [vmem] * 6 + [hbm],
+        out_specs=[hbm] + [vmem] * 7,
         scratch_shapes=scratch,
         compiler_params=pltpu.CompilerParams(
             collective_id=1, has_side_effects=True, vmem_limit_bytes=VMEM_LIMIT
         ),
         name="back",
-    )(*ins, gout, gup, gdown, gnorm_two)
-    return gx, *totals
+    )(*ins, gout, gup, gdown, gtwo, norms, proj, x)
+    return gx, totals
+
+
+def input_tile(
+    norms_ref, x_ref, gq_ref, gkv, means, proj_ref, gx_ref, gnorm_ref
+):
+    tile, width = x_ref.shape
+    grad_normed = dot_nt(gq_ref[...], proj_ref[:, :width])
+    grad_normed = grad_normed + dot_nt(gkv, proj_ref[:, width : 3 * width])
+    grad_normed = grad_normed + jnp.broadcast_to(
+        means[:, None, :], (tile // BLOCK, BLOCK, width)
+    ).reshape(tile, width)
+    xhat, inverse = center_scale(x_ref[...].astype(f32))
+    gnorm_ref[0:1, :] += jnp.sum(grad_normed * xhat, axis=0, keepdims=True)
+    gnorm_ref[1:2, :] += jnp.sum(grad_normed, axis=0, keepdims=True)
+    gain = norms_ref[0:1, :].astype(f32)
+    gx_ref[...] = layer_norm_back(grad_normed, gain, xhat, inverse).astype(bf16)
+
+
+def inputs_kernel(
+    norms_ref, x_ref, gq_ref, gsum_ref, gmeans_ref, proj_ref, gx_ref, gnorm_ref
+):
+    @pl.when(pl.program_id(0) == 0)
+    def _():
+        gnorm_ref[...] = jnp.zeros_like(gnorm_ref)
+
+    input_tile(
+        norms_ref, x_ref, gq_ref, gsum_ref[...], gmeans_ref[...], proj_ref, gx_ref, gnorm_ref
+    )
+
+
+def inputs_back(norms, x, gq, gsum, gmeans, proj):
+    seq, width = x.shape
+
+    def rows(columns):
+        return pl.BlockSpec((TILE, columns), lambda i: (i, 0))
+
+    def fixed(shape):
+        return pl.BlockSpec(shape, lambda i: (0, 0), pipeline_mode=pl.Buffered(1))
+
+    return pl.pallas_call(
+        inputs_kernel,
+        grid=(seq // TILE,),
+        out_shape=(
+            jax.ShapeDtypeStruct((seq, width), bf16),
+            jax.ShapeDtypeStruct((2, width), f32),
+        ),
+        in_specs=[
+            fixed(norms.shape), rows(width), rows(width), rows(2 * width),
+            pl.BlockSpec((TILE // BLOCK, width), lambda i: (i, 0)), fixed(proj.shape),
+        ],
+        out_specs=[rows(width), fixed((2, width))],
+        compiler_params=pltpu.CompilerParams(vmem_limit_bytes=VMEM_LIMIT),
+        name="inputs",
+    )(norms, x, gq, gsum, gmeans, proj)
+
+
+def last_plain(gpair, gsort, gone, gtwo, gquery, gout, gup, gdown):
+    grads = (gquery, gpair, gout, gup, gdown, gsort, jnp.concatenate([gone, gtwo], axis=0))
+    return tuple(
+        lax.psum_scatter(
+            grad.astype(f32), AXES, scatter_dimension=1 if b == 6 else 0, tiled=True
+        )
+        for b, grad in enumerate(grads)
+    )
 
 
 def adamw(master, first, second, grad, rate, decay):
@@ -1148,25 +1284,39 @@
 
 
 def update_kernel(*refs):
-    sums, states, results = refs[:5], refs[5:20], refs[20:]
+    parts, sums, states, gx_out, results = refs[:2], refs[2:9], refs[9:24], refs[24], refs[25:]
+
+    def add_step(hidden_grad, norm_grad, target):
+        pl.when(pl.program_id(0) == 1)(functools.partial(update_shards, sums, states, results))
+        target[...] = hidden_grad[...].astype(f32) + norm_grad[...].astype(f32)
+
+    rows = pl.BlockSpec((TILE, gx_out.shape[1]), lambda i: (i, 0))
+    pltpu.emit_pipeline(
+        add_step, grid=(gx_out.shape[0] // TILE,), in_specs=[rows] * 2, out_specs=[rows]
+    )(*parts, gx_out)
+
+
+def update_shards(sums, states, results):
+    sums = [jnp.concatenate([ref[...] for ref in sums[:3]], axis=1)] + [ref[...] for ref in sums[3:]]
     for b, (rate, decay) in enumerate(RATES):
         state = [ref[...] for ref in states[3 * b : 3 * b + 3]]
         for ref, value in zip(
-            results[3 * b : 3 * b + 3], adamw(*state, sums[b][...], rate, decay)
+            results[3 * b : 3 * b + 3], adamw(*state, sums[b], rate, decay)
         ):
             ref[...] = value
 
 
-def update(sums, states):
+def update(hidden_grad, gx, sums, states):
     vmem = pl.BlockSpec(memory_space=pltpu.VMEM)
+    hbm = pl.BlockSpec(memory_space=pl.ANY)
     return pl.pallas_call(
         update_kernel,
-        out_shape=tuple(jax.ShapeDtypeStruct(state.shape, f32) for state in states),
-        in_specs=[vmem] * 20,
-        out_specs=[vmem] * 15,
+        out_shape=tuple(jax.ShapeDtypeStruct(array.shape, f32) for array in (gx, *states)),
+        in_specs=[hbm] * 2 + [vmem] * 22,
+        out_specs=[hbm] + [vmem] * 15,
         compiler_params=pltpu.CompilerParams(vmem_limit_bytes=VMEM_LIMIT),
         name="update",
-    )(*sums, *states)
+    )(hidden_grad, gx, *sums, *states)
 
 
 def gather_plain(proj, up, down, sort, norm):
@@ -1174,17 +1324,6 @@
         return lax.all_gather(shard.astype(bf16), AXES, axis=axis, tiled=True)
 
     return (*(gathered(shard, 0) for shard in (proj, up, down, sort)), gathered(norm, 1))
-
-
-def reduce_plain(gqkv, gout, gup, gdown, gsort, gone, gtwo):
-    def summed(grad, axis):
-        return lax.psum_scatter(
-            grad.astype(f32), AXES, scatter_dimension=axis, tiled=True
-        )
-
-    gproj = jnp.concatenate([gqkv, gout], axis=1)
-    gnorm = jnp.concatenate([gone, gtwo], axis=0)
-    return (*(summed(grad, 0) for grad in (gproj, gup, gdown, gsort)), summed(gnorm, 1))
 
 
 def body(near, layer_input, doc_lengths, out_cotangent, *states):
@@ -1196,9 +1335,17 @@
     y, hidden_grad, gq, gkv, gskv, gup, gdown, gout, gnorm_two = middle(
         doc_lengths, norms, x, cot, qkv, skv, proj, up, down
     )
-    ins = (norms, gskv, tkv, kept, means, proj, sort, x, normed, hidden_grad, gq, gkv)
-    gx, *sums = (back_near if near else back_plain)(ins, gout, gup, gdown, gnorm_two)
-    return (y[None], gx[None], *update(sums, states))
+    ins = (gskv, tkv, kept, means, sort, normed, gq, gkv)
+    if near:
+        gx, sums = back_near(
+            *x.shape, ins, gout, gup, gdown, gnorm_two, norms, proj, x
+        )
+    else:
+        gsum, gpair, gsort, gmeans, *done = back_plain(*x.shape, ins, gout, gup, gdown)
+        gx, gnorm_one = inputs_back(norms, x, gq, gsum, gmeans, proj)
+        sums = last_plain(gpair, gsort, gnorm_one, gnorm_two, *done)
+    gx, *updates = update(hidden_grad, gx, sums, states)
+    return (y[None], gx[None], *updates)
 
 
 def solution(mesh):

time: 259 us -> 249 us (0.961)
  local copies, waits for them, and re-layouts: 7.76 us -> 0 us
  Pallas kernels: 250 us -> 247 us
    pallas_call x1, Pallas kernels: 67.8 us -> 56.6 us  [front_near(): pl.pallas_call(front_near_kernel, out_shape=tuple(fulls) + shapes, in_spe...]
    pallas_call x1, Pallas kernels: 2.71 us -> 11.3 us  [update(): pl.pallas_call(update_kernel, out_shape=tuple((jax.ShapeDtypeStruct(array...]
    unnamed x1 -> x0, local copies, waits for them, and re-layouts: 7.76 us -> none
where the time goes in v4:
time: 249 us; the launch traced here: 248 us
  Pallas kernels  247 us (99%)
    pallas_call x1, Pallas kernels, middle(): pl.pallas_call(middle_kernel, grid=(tiles,), out_shape=(jax.ShapeDtypeStr...  107 us
    pallas_call x1, Pallas kernels, back_near(): pl.pallas_call(back_near_kernel, out_shape=(jax.ShapeDtypeStruct((seq, wi...  71.7 us
    pallas_call x1, Pallas kernels, front_near(): pl.pallas_call(front_near_kernel, out_shape=tuple(fulls) + shapes, in_spe...  56.6 us
    pallas_call x1, Pallas kernels, update(): pl.pallas_call(update_kernel, out_shape=tuple((jax.ShapeDtypeStruct(array...  11.3 us

profile of v4, /device:TPU:0, one launch (start us, length us, event | category | flops | bytes accessed | tf_op | source)
XLA Modules:
  0.0 247.8 jit_solution(14982264753263996526)
XLA Ops:
  0.7 56.6 %front.1 = (bf16[4,2,2,2,16,2048]{5,4,3,2,1,0:T(8,128)(2,1)}, bf16[4,2,2,2,16,2048]{5,4,3,2,1,0:T(8,128)(2,1)}, bf16[4,2,2,2,64,512]{5,4,3,2,1,0:T(8,128)(2,1)},...) custom-call(s32[1,8]{1,0:T(1,128)} %lengths_ref.3, ...), custom_call_target="tpu_custom_call" | custom-call | tf_op jit(solution)/shard_map/front/pallas_call | solution.py:559
  57.3 107.4 %middle.1 = (bf16[4096,512]{1,0:T(8,128)(2,1)}, bf16[4096,512]{1,0:T(8,128)(2,1)}, bf16[4096,512]{1,0:T(8,128)(2,1)}, bf16[4096,1024]{1,0:T(8,128)(2,1)}, bf16[4...) custom-call(s32[1,8]{1,0:T(1,128)} %lengths_ref.3, ...), custom_call_target="tpu_custom_call" | custom-call | tf_op jit(solution)/shard_map/middle/pallas_call | solution.py:757
  164.7 71.7 %back.1 = (bf16[4096,512]{1,0:T(8,128)(2,1)}, f32[16,512]{1,0:T(8,128)}, f32[16,1024]{1,0:T(8,128)}, f32[16,512]{1,0:T(8,128)}, f32[16,2048]{1,0:T(8,128)}, /*in...) custom-call(bf16[4096,1024]{1,0:T(8,128)(2,1)} %get-tuple-element.69.refs_0_, ...), custom_call_target="tpu_custom_call" | custom-call | tf_op jit(solution)/shard_map/back/pallas_call | solution.py:1192
  236.3 11.3 %update.1 = (f32[4096,512]{1,0:T(8,128)}, f32[16,2048]{1,0:T(8,128)}, f32[16,2048]{1,0:T(8,128)}, f32[16,2048]{1,0:T(8,128)}, f32[16,2048]{1,0:T(8,128)}, /*inde...) custom-call(bf16[4096,512]{1,0:T(8,128)(2,1)} %get-tuple-element.68., ...), custom_call_target="tpu_custom_call" | custom-call | tf_op jit(solution)/shard_map/update/pallas_call | solution.py:1312

commit v5 on v4

--- a/solution.py
+++ b/solution.py
@@ -291,14 +291,14 @@
         self.when(k, 7, self.out, 1)
 
     def sort(self, i):
-        self.when(i, 1, self.down, 1)
-        self.when(i, 5, self.up, 2)
-        self.when(i, 6, self.out, 2)
+        self.when(i, 2, self.down, 1)
+        self.when(i, 7, self.up, 2)
 
     def low(self, k):
-        self.when(k, 3, self.down, 2)
-        self.when(k, 5, self.up, 3)
-        self.when(k, 6, self.out, 3)
+        self.when(k, 0, self.out, 2)
+        self.when(k, 5, self.down, 2)
+        self.when(k, 6, self.up, 3)
+        self.when(k, 7, self.out, 3)
 
     def end(self):
         self.turn(self.down, 3)
@@ -891,38 +891,39 @@
 
     def during_query(self, k):
         pl.when(k == 1)(self.send)
-        self.when(k, 4, self.up, 0)
-        self.when(k, 7, self.down, 0)
+        self.when(k, 6, self.up, 0)
 
     def queried(self):
         self.query.start(0)
-        self.out.turn(0)
 
     def load(self, k):
-        self.when(k, 4, self.query, 0)
+        self.when(k, 1, self.down, 0)
+        self.when(k, 3, self.out, 0)
+        self.when(k, 6, self.query, 0)
 
     def loaded(self):
         pass
 
     def sort(self, i):
-        self.when(i, 4, self.up, 1)
+        self.when(i, 7, self.up, 1)
 
     def swept(self):
-        self.down.turn(1)
-        self.up.turn(2)
+        pass
 
     def weights(self, k):
-        self.when(k, 1, self.out, 1)
-        self.when(k, 2, self.query, 1)
-        self.when(k, 5, self.down, 2)
+        self.when(k, 2, self.down, 1)
+        self.when(k, 4, self.out, 1)
+        self.when(k, 5, self.query, 1)
+        self.when(k, 6, self.up, 2)
 
     def end(self):
-        self.out.turn(2)
+        pass
 
     def inputs(self, k, pair):
+        self.when(k, 1, self.down, 2)
         self.when(k, 2, pair, 0)
-        self.when(k, 4, self.query, 2)
-        self.when(k, 7, pair, 1)
+        self.when(k, 3, self.out, 2)
+        self.when(k, 5, self.query, 2)
 
     def when(self, k, place, plan, step):
         pl.when(k == place)(functools.partial(plan.turn, step))
@@ -987,8 +988,10 @@
                 for m in range(2):
                     small[i, j, k, m, 16:] = tile
     small_plan.start(0)
-    for step in range(3):
-        small_plan.turn(step)
+    small_plan.turn(0)
+    pair.turn(1)
+    small_plan.turn(1)
+    small_plan.turn(2)
     pair.turn(2)
     sort_sum[...] = small_sum[:16, :]
     quarter, eighth = norm_place()
@@ -1290,9 +1293,9 @@
         pl.when(pl.program_id(0) == 1)(functools.partial(update_shards, sums, states, results))
         target[...] = hidden_grad[...].astype(f32) + norm_grad[...].astype(f32)
 
-    rows = pl.BlockSpec((TILE, gx_out.shape[1]), lambda i: (i, 0))
+    rows = pl.BlockSpec((2 * TILE, gx_out.shape[1]), lambda i: (i, 0))
     pltpu.emit_pipeline(
-        add_step, grid=(gx_out.shape[0] // TILE,), in_specs=[rows] * 2, out_specs=[rows]
+        add_step, grid=(gx_out.shape[0] // (2 * TILE),), in_specs=[rows] * 2, out_specs=[rows]
     )(*parts, gx_out)
 
 

time: 249 us -> 244 us (0.980)
  Pallas kernels: 247 us -> 243 us
where the time goes in v5:
time: 244 us; the launch traced here: 243 us
  Pallas kernels  243 us (100%)
    pallas_call x1, Pallas kernels, middle(): pl.pallas_call(middle_kernel, grid=(tiles,), out_shape=(jax.ShapeDtypeStr...  107 us
    pallas_call x1, Pallas kernels, back_near(): pl.pallas_call(back_near_kernel, out_shape=(jax.ShapeDtypeStruct((seq, wi...  69.2 us
    pallas_call x1, Pallas kernels, front_near(): pl.pallas_call(front_near_kernel, out_shape=tuple(fulls) + shapes, in_spe...  56.2 us
    pallas_call x1, Pallas kernels, update(): pl.pallas_call(update_kernel, out_shape=tuple((jax.ShapeDtypeStruct(array...  9.74 us

profile of v5, /device:TPU:0, one launch (start us, length us, event | category | flops | bytes accessed | tf_op | source)
XLA Modules:
  0.0 243.4 jit_solution(16701581840886714496)
XLA Ops:
  0.7 56.2 %front.1 = (bf16[4,2,2,2,16,2048]{5,4,3,2,1,0:T(8,128)(2,1)}, bf16[4,2,2,2,16,2048]{5,4,3,2,1,0:T(8,128)(2,1)}, bf16[4,2,2,2,64,512]{5,4,3,2,1,0:T(8,128)(2,1)},...) custom-call(s32[1,8]{1,0:T(1,128)} %lengths_ref.3, ...), custom_call_target="tpu_custom_call" | custom-call | tf_op jit(solution)/shard_map/front/pallas_call | solution.py:559
  56.9 107.4 %middle.1 = (bf16[4096,512]{1,0:T(8,128)(2,1)}, bf16[4096,512]{1,0:T(8,128)(2,1)}, bf16[4096,512]{1,0:T(8,128)(2,1)}, bf16[4096,1024]{1,0:T(8,128)(2,1)}, bf16[4...) custom-call(s32[1,8]{1,0:T(1,128)} %lengths_ref.3, ...), custom_call_target="tpu_custom_call" | custom-call | tf_op jit(solution)/shard_map/middle/pallas_call | solution.py:757
  164.3 69.2 %back.1 = (bf16[4096,512]{1,0:T(8,128)(2,1)}, f32[16,512]{1,0:T(8,128)}, f32[16,1024]{1,0:T(8,128)}, f32[16,512]{1,0:T(8,128)}, f32[16,2048]{1,0:T(8,128)}, /*in...) custom-call(bf16[4096,1024]{1,0:T(8,128)(2,1)} %get-tuple-element.69.refs_0_, ...), custom_call_target="tpu_custom_call" | custom-call | tf_op jit(solution)/shard_map/back/pallas_call | solution.py:1195
  233.5 9.7 %update.1 = (f32[4096,512]{1,0:T(8,128)}, f32[16,2048]{1,0:T(8,128)}, f32[16,2048]{1,0:T(8,128)}, f32[16,2048]{1,0:T(8,128)}, f32[16,2048]{1,0:T(8,128)}, /*inde...) custom-call(bf16[4096,512]{1,0:T(8,128)(2,1)} %get-tuple-element.68., ...), custom_call_target="tpu_custom_call" | custom-call | tf_op jit(solution)/shard_map/update/pallas_call | solution.py:1315

commit v6 on v5

--- a/solution.py
+++ b/solution.py
@@ -578,9 +578,10 @@
 
 
 def middle_kernel(
-    lengths_ref, norms_ref, x_ref, cot_ref, qkv_ref, skv_ref, out_proj_ref, up_ref, down_ref,
+    lengths_ref, norms_ref, x_ref, cot_ref, qkv_ref, skv_ref, out_proj_ref, up_hbm, down_hbm,
     y_ref, hidden_grad_ref, gq_ref, gkv_ref, gskv_ref, gup_ref, gdown_ref, gout_ref, gnorm_ref,
     gup, gdown, gout, probs_s, context_s, gcontext_s, gq_s, gkv_s, gskv_s, grads_s,
+    up_ref, down_ref, weight_sem,
 ):
     step = pl.program_id(0)
     tile, width = x_ref.shape
@@ -590,8 +591,14 @@
     scale = HD ** (-0.5)
     ends = doc_ends(lengths_ref)
 
+    weight_copies = [
+        pltpu.make_async_copy(source, target, weight_sem.at[i])
+        for i, (source, target) in enumerate(((up_hbm, up_ref), (down_hbm, down_ref)))
+    ]
+
     @pl.when(step == 0)
     def _():
+        start_all(weight_copies)
         gup[...] = jnp.zeros_like(gup)
         gdown[...] = jnp.zeros_like(gdown)
         gout[...] = jnp.zeros_like(gout)
@@ -655,6 +662,7 @@
 
     lax.fori_loop(0, pairs, attend, 0, unroll=8)
 
+    pl.when(step == 0)(lambda: wait_all(weight_copies))
     inputs = x_ref[...].astype(f32)
     context = context_s[...]
     hidden = inputs + dot(context, out_proj_ref[...])
@@ -776,8 +784,8 @@
             rows(3 * width),
             rows(2 * width),
             fixed((width, width), (0, 3)),
-            fixed(up.shape),
-            fixed(down.shape),
+            pl.BlockSpec(memory_space=pl.ANY),
+            pl.BlockSpec(memory_space=pl.ANY),
         ],
         out_specs=[
             rows(width),
@@ -798,6 +806,9 @@
             pltpu.VMEM((TILE, width), bf16),
             pltpu.VMEM((TILE, width), bf16),pltpu.VMEM((TILE, width), bf16),pltpu.VMEM((TILE, 2*width), bf16),pltpu.VMEM((TILE, 2*width), bf16),
             pltpu.VMEM((TILE // (2 * BLOCK) * (width // LANES), 2 * BLOCK, LANES), bf16),
+            pltpu.VMEM(up.shape, bf16),
+            pltpu.VMEM(down.shape, bf16),
+            pltpu.SemaphoreType.DMA((2,)),
         ],
         compiler_params=pltpu.CompilerParams(vmem_limit_bytes=VMEM_LIMIT),
         name="middle",

time: 244 us -> 245 us (level)
  no operation moved by 1% of the time
where the time goes in v6:
time: 245 us; the launch traced here: 244 us
  Pallas kernels  243 us (99%)
    pallas_call x1, Pallas kernels, middle(): pl.pallas_call(middle_kernel, grid=(tiles,), out_shape=(jax.ShapeDtypeStr...  108 us
    pallas_call x1, Pallas kernels, back_near(): pl.pallas_call(back_near_kernel, out_shape=(jax.ShapeDtypeStruct((seq, wi...  69.2 us
    pallas_call x1, Pallas kernels, front_near(): pl.pallas_call(front_near_kernel, out_shape=tuple(fulls) + shapes, in_spe...  56.2 us
    pallas_call x1, Pallas kernels, update(): pl.pallas_call(update_kernel, out_shape=tuple((jax.ShapeDtypeStruct(array...  9.74 us

profile of v6, /device:TPU:0, one launch (start us, length us, event | category | flops | bytes accessed | tf_op | source)
XLA Modules:
  0.0 243.8 jit_solution(18160375786197564554)
XLA Ops:
  0.7 56.2 %front.1 = (bf16[4,2,2,2,16,2048]{5,4,3,2,1,0:T(8,128)(2,1)}, bf16[4,2,2,2,16,2048]{5,4,3,2,1,0:T(8,128)(2,1)}, bf16[4,2,2,2,64,512]{5,4,3,2,1,0:T(8,128)(2,1)},...) custom-call(s32[1,8]{1,0:T(1,128)} %lengths_ref.3, ...), custom_call_target="tpu_custom_call" | custom-call | tf_op jit(solution)/shard_map/front/pallas_call | solution.py:559
  56.9 107.8 %middle.1 = (bf16[4096,512]{1,0:T(8,128)(2,1)}, bf16[4096,512]{1,0:T(8,128)(2,1)}, bf16[4096,512]{1,0:T(8,128)(2,1)}, bf16[4096,1024]{1,0:T(8,128)(2,1)}, bf16[4...) custom-call(s32[1,8]{1,0:T(1,128)} %lengths_ref.3, ...), custom_call_target="tpu_custom_call" | custom-call | tf_op jit(solution)/shard_map/middle/pallas_call | solution.py:765
  164.7 69.2 %back.1 = (bf16[4096,512]{1,0:T(8,128)(2,1)}, f32[16,512]{1,0:T(8,128)}, f32[16,1024]{1,0:T(8,128)}, f32[16,512]{1,0:T(8,128)}, f32[16,2048]{1,0:T(8,128)}, /*in...) custom-call(bf16[4096,1024]{1,0:T(8,128)(2,1)} %get-tuple-element.69.refs_0_, ...), custom_call_target="tpu_custom_call" | custom-call | tf_op jit(solution)/shard_map/back/pallas_call | solution.py:1206
  233.9 9.7 %update.1 = (f32[4096,512]{1,0:T(8,128)}, f32[16,2048]{1,0:T(8,128)}, f32[16,2048]{1,0:T(8,128)}, f32[16,2048]{1,0:T(8,128)}, f32[16,2048]{1,0:T(8,128)}, /*inde...) custom-call(bf16[4096,512]{1,0:T(8,128)(2,1)} %get-tuple-element.68., ...), custom_call_target="tpu_custom_call" | custom-call | tf_op jit(solution)/shard_map/update/pallas_call | solution.py:1326
